TPU v7x, 256 devices: a whole 4x4x8 slice. The times are simulated.
256 devices in a mesh: grp: 4 (over x_hi, core), gx: 16 (over z, x_lo), gy: 4 (over y).
Axes of the slice: x: 4 (x_hi: 2, x_lo: 2; x = x_hi * 2 + x_lo), y: 4, z: 8, core: 2. Of those that a mesh axis runs over, the one named last changes fastest.
Arguments:
- state: float32 [16, 4096, 512], P(None, ('grp', 'gx'), 'gy'), may hold values from -6 to 6
- winds: float32 [2, 16, 4096, 512], P(None, None, ('grp', 'gx'), 'gy'), may hold values from -0.2 to 0.2
- diffusivity: float32 [2, 16], replicated, may hold values from 0.05 to 0.2
- coupling: float32 [8, 16], replicated, may hold values from -1.5 to 1.5
- heat_coef: float32 [8], replicated, may hold values from 0.2 to 0.6
- remap_blocks: bfloat16 [64, 128, 128], replicated, may hold values from -0.21875 to 0.21875
- source_patch: int32 [16, 4, 64, 6], P('gx', 'gy'), may hold values from 0 to 191
- block_ids: int32 [16, 4, 64, 6], P('gx', 'gy'), may hold values from 0 to 63
- land_sea: int32 [16, 4, 64], P('gx', 'gy'), may hold values 0 or 1
Outputs:
- state_out: float32 [16, 4096, 512], P(None, ('grp', 'gx'), 'gy')
- boundary_field: float32 [4096, 512], P(('grp', 'gx'), 'gy')
- fluxes: float32 [8, 4096, 512], P(None, ('grp', 'gx'), 'gy')
All inputs are finite; a program needn't handle non-finite values. No bound on the sum of `land_sea` on one device may be relied on, other than what follows from the above.
Results may differ from a plain program's by a relative error of at most 0.0013.
Values may be sent and summed in bfloat16 or wider, within the bound.
No kernel may reach another device: no remote copies, remote signals or barrier semaphores. Data moves between devices by JAX's collectives and lax.ppermute only.
A program may use at most 64 MiB of HBM per device.

v0:
```python
import jax
import jax.numpy as jnp
from jax import lax
from jax.sharding import PartitionSpec as P

FIELDS = 8
REMAP_PIECE_SITES = 128
SUBSTEPS = 4


def extended(cells, sides, width):
    for axis, dim in sides:
        count = lax.axis_size(axis)
        ends = count - 1
        head = lax.slice_in_dim(cells, 0, width, axis=dim)
        tail = lax.slice_in_dim(cells, cells.shape[dim] - width, cells.shape[dim], axis=dim)
        cells = jnp.concatenate(
            [
                lax.ppermute(tail, axis, [(i, (i + 1) % count) for i in range(ends)]),
                cells,
                lax.ppermute(head, axis, [((i + 1) % count, i) for i in range(ends)]),
            ],
            axis=dim,
        )
    return cells


def remap_patches(source, indices, block_ids_local, remap_blocks):
    count = indices.shape[0]
    acc = jnp.zeros((count, source.shape[1], source.shape[2]), jnp.float32)
    for entry in range(indices.shape[1]):
        picked = source[indices[:, entry]]
        weights = remap_blocks[block_ids_local[:, entry]]
        term = jnp.einsum("nfp,nqp->nfq", picked, weights, preferred_element_type=jnp.float32)
        acc = acc + term
    return acc


def advance(padded, east_wind, north_wind, rate):
    centre = padded[:, 1:-1, 1:-1]
    north = padded[:, :-2, 1:-1]
    south = padded[:, 2:, 1:-1]
    west = padded[:, 1:-1, :-2]
    east = padded[:, 1:-1, 2:]
    return (
        centre
        - 0.5 * east_wind * (east - west)
        - 0.5 * north_wind * (south - north)
        + rate * (north + south + east + west - 4.0 * centre)
    )


def extend(bundle, extent, group, row_tile, tiles_x):
    near = extended(bundle, ((("grp", "gx"), 2),), extent)
    upper_closed = (row_tile == 0) & (group == 3)
    lower_closed = (row_tile == tiles_x - 1) & (group == 2)
    upper = jnp.where(upper_closed, 0.0, near[:, :, :extent])
    lower = jnp.where(lower_closed, 0.0, near[:, :, -extent:])
    stacked = jnp.concatenate([upper, bundle, lower], axis=2)
    return extended(stacked, (("gy", 3),), extent)


def body(
    state, winds, diffusivity, coupling, heat_coef, remap_blocks, source_patch, block_ids, land_sea
):
    group = lax.axis_index("grp")
    row_tile = lax.axis_index("gx")
    tiles_x = lax.axis_size("gx")
    marine_part = group == 3
    rate = jnp.where(marine_part, diffusivity[1], diffusivity[0])[:, None, None]
    row_count = state.shape[1]
    column_count = state.shape[2]
    total = jnp.zeros((coupling.shape[0], row_count, column_count), jnp.float32)
    field = state
    for step in range(SUBSTEPS):
        padded = extend(field[None], 1, group, row_tile, tiles_x)[0]
        field = advance(padded, winds[0], winds[1], rate)
        total = total + jnp.einsum("fl,lrc->frc", coupling, field, precision=lax.Precision.HIGHEST)
    averaged_exchange = total / float(SUBSTEPS)
    rounded = averaged_exchange.astype(jnp.bfloat16)
    runs_along_line = column_count // REMAP_PIECE_SITES
    patches = (
        rounded.reshape(FIELDS, row_count, runs_along_line, REMAP_PIECE_SITES)
        .transpose(1, 2, 0, 3)
        .reshape(row_count * runs_along_line, FIELDS, REMAP_PIECE_SITES)
    )
    donor_sequence = source_patch[0, 0]
    marine_parts_sequence = block_ids[0, 0]
    water_indicator = land_sea[0, 0]
    gathered = lax.all_gather(patches, "grp", axis=0, tiled=True)
    remapped = remap_patches(gathered, donor_sequence, marine_parts_sequence, remap_blocks)
    water_share = water_indicator.astype(jnp.float32)
    thermal_forcing = jnp.sum(heat_coef[:, None] * remapped, axis=-2)
    uppermost_layer = field[0]
    marine_skin_warmth = uppermost_layer + water_share[:, None] * thermal_forcing
    boundary_field = jnp.where(marine_part, marine_skin_warmth, averaged_exchange[0])
    masked = water_share[:, None, None] * remapped
    marine_boundary_forcing = (
        masked.reshape(row_count, runs_along_line, FIELDS, REMAP_PIECE_SITES)
        .transpose(2, 0, 1, 3)
        .reshape(FIELDS, row_count, column_count)
    )
    fluxes = jnp.where(marine_part, marine_boundary_forcing, averaged_exchange)
    return (field, boundary_field, fluxes)


def solution(mesh):
    return jax.shard_map(
        body,
        mesh=mesh,
        in_specs=(
            P(None, ("grp", "gx"), "gy"),
            P(None, None, ("grp", "gx"), "gy"),
            P(),
            P(),
            P(),
            P(),
            P("gx", "gy", None, None),
            P("gx", "gy", None, None),
            P("gx", "gy", None),
        ),
        out_specs=(
            P(None, ("grp", "gx"), "gy"),
            P(("grp", "gx"), "gy"),
            P(None, ("grp", "gx"), "gy"),
        ),
        check_vma=False,
    )
```

profile of v0, /device:TPU:79, one launch (start us, length us, event | category | flops | bytes accessed | tf_op | source)
XLA Modules:
  0.0 158.1 jit_solution(11080110161822021250)
XLA Ops:
  1.7 3.8 %collective-permute-start = (f32[1,16,1,128]{3,2,1,0:T(1,128)S(1)}, f32[1,16,1,128]{3,2,1,0:T(1,128)S(1)}, u32[]{:S(2)}, u32[]{:S(2)}) collective-permute-start(f32[1,16,1,128]{3,2,1,0:T(1,128)S(1)} %get-tuple-element.23), channel_id=1, source_target_pairs={{0,4},{4,8},{8,12},{12,16},{16,20},{20,24},{24,28},{28,32},{32,36}... | collective-permute-start | bytes 24584 | tf_op jit(solution)/shard_map/ppermute | solution.py:19
  5.5 1.9 %collective-permute-start.1 = (f32[1,16,1,128]{3,2,1,0:T(1,128)S(1)}, f32[1,16,1,128]{3,2,1,0:T(1,128)S(1)}, u32[]{:S(2)}, u32[]{:S(2)}) collective-permute-start(f32[1,16,1,128]{3,2,1,0:T(1,128)S(1)} %get-tuple-element.24), channel_id=1, source_target_pairs={{4,0},{8,4},{12,8},{16,12},{20,16},{24,20},{28,24},{32,28},{36,32}... | collective-permute-start | bytes 24584 | tf_op jit(solution)/shard_map/ppermute | solution.py:21
  10.8 1.1 pad_maximum_fusion
  11.9 1.2 fusion.41
  13.1 1.3 copy.17
  14.4 3.2 %collective-permute-start.2 = (f32[1,16,66,1]{2,1,3,0:T(8,128)S(1)}, f32[1,16,66,1]{2,1,3,0:T(8,128)S(1)}, u32[]{:S(2)}, u32[]{:S(2)}) collective-permute-start(f32[1,16,66,1]{2,1,3,0:T(8,128)S(1)} %copy.17), channel_id=1, source_target_pairs={{0,1},{1,2},{2,3},{4,5},{5,6},{6,7},{8,9},{9,10},{10,11},{12,13},{... | collective-permute-start | bytes 12680 | tf_op jit(solution)/shard_map/ppermute | solution.py:19
  17.6 1.3 copy.18
  18.9 2.2 %collective-permute-start.3 = (f32[1,16,66,1]{2,1,3,0:T(8,128)S(1)}, f32[1,16,66,1]{2,1,3,0:T(8,128)S(1)}, u32[]{:S(2)}, u32[]{:S(2)}) collective-permute-start(f32[1,16,66,1]{2,1,3,0:T(8,128)S(1)} %copy.18), channel_id=1, source_target_pairs={{1,0},{2,1},{3,2},{5,4},{6,5},{7,6},{9,8},{10,9},{11,10},{13,12},{... | collective-permute-start | bytes 12680 | tf_op jit(solution)/shard_map/ppermute | solution.py:21
  21.2 1.1 copy.19
  22.3 1.2 collective-permute-done.3
  24.6 2.0 %maximum_bitcast_fusion = f32[16,66,130]{2,1,0:T(8,128)S(1)} fusion(f32[1,16,66,1]{3,2,1,0:T(8,128)} %copy.20, f32[1,16,1,128]{3,2,1,0:T(1,128)S(1)} %broadcast_select_fusion.3, f32[1,16,64,128]{3,2,1,0:T(8,128)} %bitcast.148, f32[1,16,1,128]{3,2,1,0:T(1,128)S(1)} %broadcast_select_fusion.7, f32[1,16,66,1]{3,2,1,0:T(8,128)} %copy.19), kind=kLoop, calls=%fused_computation.12 | loop fusion | flops 549120 | bytes 1098240 | tf_op jit(solution)/shard_map/squeeze | solution.py:76
  27.3 3.8 %collective-permute-start.4 = (f32[1,16,1,128]{3,2,1,0:T(1,128)S(1)}, f32[1,16,1,128]{3,2,1,0:T(1,128)S(1)}, u32[]{:S(2)}, u32[]{:S(2)}) collective-permute-start(f32[1,16,1,128]{3,2,1,0:T(1,128)S(1)} %get-tuple-element.21), channel_id=1, source_target_pairs={{0,4},{4,8},{8,12},{12,16},{16,20},{20,24},{24,28},{28,32},{32,36}... | collective-permute-start | bytes 24584 | tf_op jit(solution)/shard_map/ppermute | solution.py:19
  31.1 1.9 %collective-permute-start.5 = (f32[1,16,1,128]{3,2,1,0:T(1,128)S(1)}, f32[1,16,1,128]{3,2,1,0:T(1,128)S(1)}, u32[]{:S(2)}, u32[]{:S(2)}) collective-permute-start(f32[1,16,1,128]{3,2,1,0:T(1,128)S(1)} %get-tuple-element.22), channel_id=1, source_target_pairs={{4,0},{8,4},{12,8},{16,12},{20,16},{24,20},{28,24},{32,28},{36,32}... | collective-permute-start | bytes 24584 | tf_op jit(solution)/shard_map/ppermute | solution.py:21
  33.1 4.3 %collective-permute-done.5 = f32[1,16,1,128]{3,2,1,0:T(1,128)S(1)} collective-permute-done((f32[1,16,1,128]{3,2,1,0:T(1,128)S(1)}, f32[1,16,1,128]{3,2,1,0:T(1,128)S(1)}, u32[]{:S(2)}, u32[]{:S(2)}) %collective-permute-start.5) | collective-permute-done | bytes 8224 | tf_op jit(solution)/shard_map/ppermute | solution.py:21
  37.5 1.2 fusion.40
  38.6 1.3 copy.21
  39.9 2.9 %collective-permute-start.6 = (f32[1,16,66,1]{2,1,3,0:T(8,128)S(1)}, f32[1,16,66,1]{2,1,3,0:T(8,128)S(1)}, u32[]{:S(2)}, u32[]{:S(2)}) collective-permute-start(f32[1,16,66,1]{2,1,3,0:T(8,128)S(1)} %copy.21), channel_id=1, source_target_pairs={{0,1},{1,2},{2,3},{4,5},{5,6},{6,7},{8,9},{9,10},{10,11},{12,13},{... | collective-permute-start | bytes 12680 | tf_op jit(solution)/shard_map/ppermute | solution.py:19
  42.9 1.3 copy.22
  44.2 2.4 %collective-permute-start.7 = (f32[1,16,66,1]{2,1,3,0:T(8,128)S(1)}, f32[1,16,66,1]{2,1,3,0:T(8,128)S(1)}, u32[]{:S(2)}, u32[]{:S(2)}) collective-permute-start(f32[1,16,66,1]{2,1,3,0:T(8,128)S(1)} %copy.22), channel_id=1, source_target_pairs={{1,0},{2,1},{3,2},{5,4},{6,5},{7,6},{9,8},{10,9},{11,10},{13,12},{... | collective-permute-start | bytes 12680 | tf_op jit(solution)/shard_map/ppermute | solution.py:21
  46.6 1.1 copy.23
  49.7 2.0 %maximum_bitcast_fusion.1 = f32[16,66,130]{2,1,0:T(8,128)S(1)} fusion(f32[1,16,66,1]{3,2,1,0:T(8,128)} %copy.24, f32[1,16,1,128]{3,2,1,0:T(1,128)S(1)} %broadcast_select_fusion.2, f32[1,16,64,128]{3,2,1,0:T(8,128)} %bitcast.133, f32[1,16,1,128]{3,2,1,0:T(1,128)S(1)} %broadcast_select_fusion.6, f32[1,16,66,1]{3,2,1,0:T(8,128)} %copy.23), kind=kLoop, calls=%fused_computation.13 | loop fusion | flops 549120 | bytes 1098240 | tf_op jit(solution)/shard_map/squeeze | solution.py:76
  53.2 3.8 %collective-permute-start.8 = (f32[1,16,1,128]{3,2,1,0:T(1,128)S(1)}, f32[1,16,1,128]{3,2,1,0:T(1,128)S(1)}, u32[]{:S(2)}, u32[]{:S(2)}) collective-permute-start(f32[1,16,1,128]{3,2,1,0:T(1,128)S(1)} %get-tuple-element.19), channel_id=1, source_target_pairs={{0,4},{4,8},{8,12},{12,16},{16,20},{20,24},{24,28},{28,32},{32,36}... | collective-permute-start | bytes 24584 | tf_op jit(solution)/shard_map/ppermute | solution.py:19
  57.0 2.2 %gather_fusion.1 = bf16[64,128,128]{2,1,0:T(8,128)(2,1)} fusion(bf16[64,128,128]{2,1,0:T(8,128)(2,1)S(1)} %copy-done, s32[1024]{0:T(1024)S(1)} %get-tuple-element.50), kind=kCustom, calls=%fused_computation.1 | custom fusion | bytes 4194560 | tf_op jit(solution)/shard_map/gather | solution.py:33
  59.2 2.1 %gather_fusion.3 = bf16[64,128,128]{2,1,0:T(8,128)(2,1)} fusion(bf16[64,128,128]{2,1,0:T(8,128)(2,1)S(1)} %copy-done, s32[1024]{0:T(1024)S(1)} %get-tuple-element.49), kind=kCustom, calls=%fused_computation.3 | custom fusion | bytes 4194560 | tf_op jit(solution)/shard_map/gather | solution.py:33
  61.4 2.2 %gather_fusion.5 = bf16[64,128,128]{2,1,0:T(8,128)(2,1)} fusion(bf16[64,128,128]{2,1,0:T(8,128)(2,1)S(1)} %copy-done, s32[1024]{0:T(1024)S(1)} %get-tuple-element.48), kind=kCustom, calls=%fused_computation.5 | custom fusion | bytes 4194560 | tf_op jit(solution)/shard_map/gather | solution.py:33
  63.6 2.2 %gather_fusion.7 = bf16[64,128,128]{2,1,0:T(8,128)(2,1)} fusion(bf16[64,128,128]{2,1,0:T(8,128)(2,1)S(1)} %copy-done, s32[1024]{0:T(1024)S(1)} %get-tuple-element.47), kind=kCustom, calls=%fused_computation.7 | custom fusion | bytes 4194560 | tf_op jit(solution)/shard_map/gather | solution.py:33
  65.8 2.1 %gather_fusion.9 = bf16[64,128,128]{2,1,0:T(8,128)(2,1)} fusion(bf16[64,128,128]{2,1,0:T(8,128)(2,1)S(1)} %copy-done, s32[1024]{0:T(1024)S(1)} %get-tuple-element.46), kind=kCustom, calls=%fused_computation.9 | custom fusion | bytes 4194560 | tf_op jit(solution)/shard_map/gather | solution.py:33
  67.9 2.1 %gather_fusion.11 = bf16[64,128,128]{2,1,0:T(8,128)(2,1)} fusion(bf16[64,128,128]{2,1,0:T(8,128)(2,1)S(1)} %copy-done, s32[1024]{0:T(1024)S(1)} %get-tuple-element.45), kind=kCustom, calls=%fused_computation.11 | custom fusion | bytes 4194560 | tf_op jit(solution)/shard_map/gather | solution.py:33
  70.1 1.9 %collective-permute-start.9 = (f32[1,16,1,128]{3,2,1,0:T(1,128)S(1)}, f32[1,16,1,128]{3,2,1,0:T(1,128)S(1)}, u32[]{:S(2)}, u32[]{:S(2)}) collective-permute-start(f32[1,16,1,128]{3,2,1,0:T(1,128)S(1)} %get-tuple-element.20), channel_id=1, source_target_pairs={{4,0},{8,4},{12,8},{16,12},{20,16},{24,20},{28,24},{32,28},{36,32}... | collective-permute-start | bytes 24584 | tf_op jit(solution)/shard_map/ppermute | solution.py:21
  72.0 4.5 %collective-permute-done.9 = f32[1,16,1,128]{3,2,1,0:T(1,128)S(1)} collective-permute-done((f32[1,16,1,128]{3,2,1,0:T(1,128)S(1)}, f32[1,16,1,128]{3,2,1,0:T(1,128)S(1)}, u32[]{:S(2)}, u32[]{:S(2)}) %collective-permute-start.9) | collective-permute-done | bytes 8224 | tf_op jit(solution)/shard_map/ppermute | solution.py:21
  76.6 1.1 pad_maximum_fusion.2
  77.7 1.2 fusion.39
  78.9 1.3 copy.25
  80.2 2.1 %collective-permute-start.10 = (f32[1,16,66,1]{2,1,3,0:T(8,128)S(1)}, f32[1,16,66,1]{2,1,3,0:T(8,128)S(1)}, u32[]{:S(2)}, u32[]{:S(2)}) collective-permute-start(f32[1,16,66,1]{2,1,3,0:T(8,128)S(1)} %copy.25), channel_id=1, source_target_pairs={{0,1},{1,2},{2,3},{4,5},{5,6},{6,7},{8,9},{9,10},{10,11},{12,13},{... | collective-permute-start | bytes 12680 | tf_op jit(solution)/shard_map/ppermute | solution.py:19
  82.2 1.3 copy.26
  83.5 3.2 %collective-permute-start.11 = (f32[1,16,66,1]{2,1,3,0:T(8,128)S(1)}, f32[1,16,66,1]{2,1,3,0:T(8,128)S(1)}, u32[]{:S(2)}, u32[]{:S(2)}) collective-permute-start(f32[1,16,66,1]{2,1,3,0:T(8,128)S(1)} %copy.26), channel_id=1, source_target_pairs={{1,0},{2,1},{3,2},{5,4},{6,5},{7,6},{9,8},{10,9},{11,10},{13,12},{... | collective-permute-start | bytes 12680 | tf_op jit(solution)/shard_map/ppermute | solution.py:21
  86.8 1.7 %fusion.17 = f32[64,128,8]{1,2,0:T(8,128)S(1)} fusion(f32[16,64,128]{2,1,0:T(8,128)} %copy-done.2, f32[8,16]{1,0:T(8,128)S(1)} %copy-done.17), kind=kOutput, calls=%fused_computation.53 | convolution fusion | flops 12582912 | bytes 786944 | tf_op jit(solution)/shard_map/fl,lrc->frc/dot_general | solution.py:78
  88.5 1.1 copy.27
  89.6 1.1 copy.28
  90.8 2.0 %maximum_bitcast_fusion.2 = f32[16,66,130]{2,1,0:T(8,128)S(1)} fusion(f32[1,16,66,1]{3,2,1,0:T(8,128)} %copy.28, f32[1,16,1,128]{3,2,1,0:T(1,128)S(1)} %broadcast_select_fusion.1, f32[1,16,64,128]{3,2,1,0:T(8,128)} %bitcast.136, f32[1,16,1,128]{3,2,1,0:T(1,128)S(1)} %broadcast_select_fusion.5, f32[1,16,66,1]{3,2,1,0:T(8,128)} %copy.27), kind=kLoop, calls=%fused_computation.14 | loop fusion | flops 549120 | bytes 1098240 | tf_op jit(solution)/shard_map/squeeze | solution.py:76
  93.5 3.4 %collective-permute-start.12 = (f32[1,16,1,128]{3,2,1,0:T(1,128)S(1)}, f32[1,16,1,128]{3,2,1,0:T(1,128)S(1)}, u32[]{:S(2)}, u32[]{:S(2)}) collective-permute-start(f32[1,16,1,128]{3,2,1,0:T(1,128)S(1)} %get-tuple-element.17), channel_id=1, source_target_pairs={{0,4},{4,8},{8,12},{12,16},{16,20},{20,24},{24,28},{28,32},{32,36}... | collective-permute-start | bytes 24584 | tf_op jit(solution)/shard_map/ppermute | solution.py:19
  96.9 1.4 convolution_add_fusion.7
  98.3 1.9 %collective-permute-start.13 = (f32[1,16,1,128]{3,2,1,0:T(1,128)S(1)}, f32[1,16,1,128]{3,2,1,0:T(1,128)S(1)}, u32[]{:S(2)}, u32[]{:S(2)}) collective-permute-start(f32[1,16,1,128]{3,2,1,0:T(1,128)S(1)} %get-tuple-element.18), channel_id=1, source_target_pairs={{4,0},{8,4},{12,8},{16,12},{20,16},{24,20},{28,24},{32,28},{36,32}... | collective-permute-start | bytes 24584 | tf_op jit(solution)/shard_map/ppermute | solution.py:21
  100.2 3.3 %collective-permute-done.13 = f32[1,16,1,128]{3,2,1,0:T(1,128)S(1)} collective-permute-done((f32[1,16,1,128]{3,2,1,0:T(1,128)S(1)}, f32[1,16,1,128]{3,2,1,0:T(1,128)S(1)}, u32[]{:S(2)}, u32[]{:S(2)}) %collective-permute-start.13) | collective-permute-done | bytes 8224 | tf_op jit(solution)/shard_map/ppermute | solution.py:21
  103.6 1.2 fusion.38
  104.8 1.3 copy.29
  106.1 2.1 %collective-permute-start.14 = (f32[1,16,66,1]{2,1,3,0:T(8,128)S(1)}, f32[1,16,66,1]{2,1,3,0:T(8,128)S(1)}, u32[]{:S(2)}, u32[]{:S(2)}) collective-permute-start(f32[1,16,66,1]{2,1,3,0:T(8,128)S(1)} %copy.29), channel_id=1, source_target_pairs={{0,1},{1,2},{2,3},{4,5},{5,6},{6,7},{8,9},{9,10},{10,11},{12,13},{... | collective-permute-start | bytes 12680 | tf_op jit(solution)/shard_map/ppermute | solution.py:19
  108.2 1.3 copy.30
  109.5 3.4 %collective-permute-start.15 = (f32[1,16,66,1]{2,1,3,0:T(8,128)S(1)}, f32[1,16,66,1]{2,1,3,0:T(8,128)S(1)}, u32[]{:S(2)}, u32[]{:S(2)}) collective-permute-start(f32[1,16,66,1]{2,1,3,0:T(8,128)S(1)} %copy.30), channel_id=1, source_target_pairs={{1,0},{2,1},{3,2},{5,4},{6,5},{7,6},{9,8},{10,9},{11,10},{13,12},{... | collective-permute-start | bytes 12680 | tf_op jit(solution)/shard_map/ppermute | solution.py:21
  112.9 2.4 %convolution_add_fusion.6 = f32[64,128,8]{1,2,0:T(8,128)} fusion(f32[64,128,8]{1,2,0:T(8,128)S(1)} %copy-done.11, f32[16,64,128]{2,1,0:T(8,128)} %copy-done.5, f32[8,16]{1,0:T(8,128)S(1)} %copy-done.17), kind=kOutput, calls=%fused_computation.24 | convolution fusion | flops 12648448 | bytes 1049088 | tf_op jit(solution)/shard_map/fl,lrc->frc/dot_general | solution.py:78
  115.4 1.1 copy.31
  116.5 1.1 copy.32
  117.6 2.0 %maximum_bitcast_fusion.3 = f32[16,66,130]{2,1,0:T(8,128)S(1)} fusion(f32[1,16,66,1]{3,2,1,0:T(8,128)} %copy.32, f32[1,16,1,128]{3,2,1,0:T(1,128)S(1)} %broadcast_select_fusion, f32[1,16,64,128]{3,2,1,0:T(8,128)} %bitcast.139, f32[1,16,1,128]{3,2,1,0:T(1,128)S(1)} %broadcast_select_fusion.4, f32[1,16,66,1]{3,2,1,0:T(8,128)} %copy.31), kind=kLoop, calls=%fused_computation.15 | loop fusion | flops 549120 | bytes 1098240 | tf_op jit(solution)/shard_map/squeeze | solution.py:76
  122.0 17.3 %all-gather = bf16[256,1,8,128]{3,2,1,0:T(8,128)(2,1)S(1)} all-gather(bf16[64,1,8,128]{3,2,1,0:T(8,128)(2,1)S(1)} %convert_bitcast_fusion), channel_id=2, replica_groups=mesh['grp'=4,'gx'=16,'gy'=4] {'grp'}, dimensions={0}, use_global_device_ids=true | all-gather | bytes 655360 | tf_op jit(solution)/shard_map/all_gather | solution.py:90
  139.9 1.3 gather_fusion.2
  141.2 1.3 gather_fusion.4
  142.5 1.3 gather_fusion.6
  145.0 2.9 %fusion.46 = f32[64,8,128]{2,1,0:T(8,128)S(1)} fusion(bf16[64,8,128]{2,1,0:T(8,128)(2,1)S(1)} %gather_fusion, bf16[64,128,128]{2,1,0:T(8,128)(2,1)} %gather_fusion.1), kind=kOutput, calls=%fused_computation.124 | convolution fusion | flops 16777216 | bytes 2490368 | tf_op jit(solution)/shard_map/nfp,nqp->nfq/dot_general | solution.py:34
  148.0 2.9 %convolution_add_fusion.4 = f32[64,8,128]{2,1,0:T(8,128)S(1)} fusion(f32[64,8,128]{2,1,0:T(8,128)S(1)} %fusion.46, bf16[64,8,128]{2,1,0:T(8,128)(2,1)S(1)} %copy-done.15, bf16[64,128,128]{2,1,0:T(8,128)(2,1)} %gather_fusion.3), kind=kOutput, calls=%fused_computation.20 | convolution fusion | flops 16842752 | bytes 2752512 | tf_op jit(solution)/shard_map/nfp,nqp->nfq/dot_general | solution.py:34
  150.9 1.2 convolution_add_fusion.3
  152.1 1.2 convolution_add_fusion.2
  153.3 1.2 convolution_add_fusion.1
  154.6 1.2 multiply_reduce_fusion
  156.7 1.5 fusion.20
  (90 shorter events, 15.7 us)
Async XLA Ops:
  0.6 56.4 %copy-start = (bf16[64,128,128]{2,1,0:T(8,128)(2,1)S(1)}, bf16[64,128,128]{2,1,0:T(8,128)(2,1)}, u32[]{:S(2)}) copy-start(bf16[64,128,128]{2,1,0:T(8,128)(2,1)} %param.14) | copy-start | bytes 6291460
  1.7 8.6 %collective-permute-start = (f32[1,16,1,128]{3,2,1,0:T(1,128)S(1)}, f32[1,16,1,128]{3,2,1,0:T(1,128)S(1)}, u32[]{:S(2)}, u32[]{:S(2)}) collective-permute-start(f32[1,16,1,128]{3,2,1,0:T(1,128)S(1)} %get-tuple-element.23), channel_id=1, source_target_pairs={{0,4},{4,8},{8,12},{12,16},{16,20},{20,24},{24,28},{28,32},{32,36}... | collective-permute-start | bytes 24584 | tf_op jit(solution)/shard_map/ppermute | solution.py:19
  5.5 5.3 %collective-permute-start.1 = (f32[1,16,1,128]{3,2,1,0:T(1,128)S(1)}, f32[1,16,1,128]{3,2,1,0:T(1,128)S(1)}, u32[]{:S(2)}, u32[]{:S(2)}) collective-permute-start(f32[1,16,1,128]{3,2,1,0:T(1,128)S(1)} %get-tuple-element.24), channel_id=1, source_target_pairs={{4,0},{8,4},{12,8},{16,12},{20,16},{24,20},{28,24},{32,28},{36,32}... | collective-permute-start | bytes 24584 | tf_op jit(solution)/shard_map/ppermute | solution.py:21
  14.4 6.8 %collective-permute-start.2 = (f32[1,16,66,1]{2,1,3,0:T(8,128)S(1)}, f32[1,16,66,1]{2,1,3,0:T(8,128)S(1)}, u32[]{:S(2)}, u32[]{:S(2)}) collective-permute-start(f32[1,16,66,1]{2,1,3,0:T(8,128)S(1)} %copy.17), channel_id=1, source_target_pairs={{0,1},{1,2},{2,3},{4,5},{5,6},{6,7},{8,9},{9,10},{10,11},{12,13},{... | collective-permute-start | bytes 12680 | tf_op jit(solution)/shard_map/ppermute | solution.py:19
  18.9 7.6 %copy-start.1 = (f32[2,16,64,128]{3,2,1,0:T(8,128)S(1)}, f32[2,16,64,128]{3,2,1,0:T(8,128)}, u32[]{:S(2)}) copy-start(f32[2,16,64,128]{3,2,1,0:T(8,128)} %param.10) | copy-start | bytes 3145732
  18.9 4.5 %collective-permute-start.3 = (f32[1,16,66,1]{2,1,3,0:T(8,128)S(1)}, f32[1,16,66,1]{2,1,3,0:T(8,128)S(1)}, u32[]{:S(2)}, u32[]{:S(2)}) collective-permute-start(f32[1,16,66,1]{2,1,3,0:T(8,128)S(1)} %copy.18), channel_id=1, source_target_pairs={{1,0},{2,1},{3,2},{5,4},{6,5},{7,6},{9,8},{10,9},{11,10},{13,12},{... | collective-permute-start | bytes 12680 | tf_op jit(solution)/shard_map/ppermute | solution.py:21
  27.2 10.2 %copy-start.2 = (f32[16,64,128]{2,1,0:T(8,128)}, f32[16,64,128]{2,1,0:T(8,128)S(1)}, u32[]{:S(2)}) copy-start(f32[16,64,128]{2,1,0:T(8,128)S(1)} %fusion.3) | copy-start | bytes 1572868
  27.3 5.8 %collective-permute-start.4 = (f32[1,16,1,128]{3,2,1,0:T(1,128)S(1)}, f32[1,16,1,128]{3,2,1,0:T(1,128)S(1)}, u32[]{:S(2)}, u32[]{:S(2)}) collective-permute-start(f32[1,16,1,128]{3,2,1,0:T(1,128)S(1)} %get-tuple-element.21), channel_id=1, source_target_pairs={{0,4},{4,8},{8,12},{12,16},{16,20},{20,24},{24,28},{28,32},{32,36}... | collective-permute-start | bytes 24584 | tf_op jit(solution)/shard_map/ppermute | solution.py:19
  31.1 6.3 %collective-permute-start.5 = (f32[1,16,1,128]{3,2,1,0:T(1,128)S(1)}, f32[1,16,1,128]{3,2,1,0:T(1,128)S(1)}, u32[]{:S(2)}, u32[]{:S(2)}) collective-permute-start(f32[1,16,1,128]{3,2,1,0:T(1,128)S(1)} %get-tuple-element.22), channel_id=1, source_target_pairs={{4,0},{8,4},{12,8},{16,12},{20,16},{24,20},{28,24},{32,28},{36,32}... | collective-permute-start | bytes 24584 | tf_op jit(solution)/shard_map/ppermute | solution.py:21
  39.9 6.6 %collective-permute-start.6 = (f32[1,16,66,1]{2,1,3,0:T(8,128)S(1)}, f32[1,16,66,1]{2,1,3,0:T(8,128)S(1)}, u32[]{:S(2)}, u32[]{:S(2)}) collective-permute-start(f32[1,16,66,1]{2,1,3,0:T(8,128)S(1)} %copy.21), channel_id=1, source_target_pairs={{0,1},{1,2},{2,3},{4,5},{5,6},{6,7},{8,9},{9,10},{10,11},{12,13},{... | collective-permute-start | bytes 12680 | tf_op jit(solution)/shard_map/ppermute | solution.py:19
  44.2 4.4 %collective-permute-start.7 = (f32[1,16,66,1]{2,1,3,0:T(8,128)S(1)}, f32[1,16,66,1]{2,1,3,0:T(8,128)S(1)}, u32[]{:S(2)}, u32[]{:S(2)}) collective-permute-start(f32[1,16,66,1]{2,1,3,0:T(8,128)S(1)} %copy.22), channel_id=1, source_target_pairs={{1,0},{2,1},{3,2},{5,4},{6,5},{7,6},{9,8},{10,9},{11,10},{13,12},{... | collective-permute-start | bytes 12680 | tf_op jit(solution)/shard_map/ppermute | solution.py:21
  52.4 0.8 copy-start.3
  53.2 18.8 %collective-permute-start.8 = (f32[1,16,1,128]{3,2,1,0:T(1,128)S(1)}, f32[1,16,1,128]{3,2,1,0:T(1,128)S(1)}, u32[]{:S(2)}, u32[]{:S(2)}) collective-permute-start(f32[1,16,1,128]{3,2,1,0:T(1,128)S(1)} %get-tuple-element.19), channel_id=1, source_target_pairs={{0,4},{4,8},{8,12},{12,16},{16,20},{20,24},{24,28},{28,32},{32,36}... | collective-permute-start | bytes 24584 | tf_op jit(solution)/shard_map/ppermute | solution.py:19
  70.1 6.5 %collective-permute-start.9 = (f32[1,16,1,128]{3,2,1,0:T(1,128)S(1)}, f32[1,16,1,128]{3,2,1,0:T(1,128)S(1)}, u32[]{:S(2)}, u32[]{:S(2)}) collective-permute-start(f32[1,16,1,128]{3,2,1,0:T(1,128)S(1)} %get-tuple-element.20), channel_id=1, source_target_pairs={{4,0},{8,4},{12,8},{16,12},{20,16},{24,20},{28,24},{32,28},{36,32}... | collective-permute-start | bytes 24584 | tf_op jit(solution)/shard_map/ppermute | solution.py:21
  76.6 10.2 %copy-start.17 = (f32[8,16]{1,0:T(8,128)S(1)}, f32[8,16]{1,0:T(8,128)}, u32[]{:S(2)}) copy-start(f32[8,16]{1,0:T(8,128)} %param.12) | copy-start | bytes 1540
  80.2 8.4 %collective-permute-start.10 = (f32[1,16,66,1]{2,1,3,0:T(8,128)S(1)}, f32[1,16,66,1]{2,1,3,0:T(8,128)S(1)}, u32[]{:S(2)}, u32[]{:S(2)}) collective-permute-start(f32[1,16,66,1]{2,1,3,0:T(8,128)S(1)} %copy.25), channel_id=1, source_target_pairs={{0,1},{1,2},{2,3},{4,5},{5,6},{6,7},{8,9},{9,10},{10,11},{12,13},{... | collective-permute-start | bytes 12680 | tf_op jit(solution)/shard_map/ppermute | solution.py:19
  83.5 6.1 %collective-permute-start.11 = (f32[1,16,66,1]{2,1,3,0:T(8,128)S(1)}, f32[1,16,66,1]{2,1,3,0:T(8,128)S(1)}, u32[]{:S(2)}, u32[]{:S(2)}) collective-permute-start(f32[1,16,66,1]{2,1,3,0:T(8,128)S(1)} %copy.26), channel_id=1, source_target_pairs={{1,0},{2,1},{3,2},{5,4},{6,5},{7,6},{9,8},{10,9},{11,10},{13,12},{... | collective-permute-start | bytes 12680 | tf_op jit(solution)/shard_map/ppermute | solution.py:21
  92.8 4.1 %copy-start.4 = (f32[16,64,128]{2,1,0:T(8,128)S(1)}, f32[16,64,128]{2,1,0:T(8,128)}, u32[]{:S(2)}) copy-start(f32[16,64,128]{2,1,0:T(8,128)} %copy-done.3) | copy-start | bytes 1572868
  93.4 11.4 %copy-start.5 = (f32[16,64,128]{2,1,0:T(8,128)}, f32[16,64,128]{2,1,0:T(8,128)S(1)}, u32[]{:S(2)}) copy-start(f32[16,64,128]{2,1,0:T(8,128)S(1)} %fusion.7) | copy-start | bytes 1572868
  93.5 6.7 %collective-permute-start.12 = (f32[1,16,1,128]{3,2,1,0:T(1,128)S(1)}, f32[1,16,1,128]{3,2,1,0:T(1,128)S(1)}, u32[]{:S(2)}, u32[]{:S(2)}) collective-permute-start(f32[1,16,1,128]{3,2,1,0:T(1,128)S(1)} %get-tuple-element.17), channel_id=1, source_target_pairs={{0,4},{4,8},{8,12},{12,16},{16,20},{20,24},{24,28},{28,32},{32,36}... | collective-permute-start | bytes 24584 | tf_op jit(solution)/shard_map/ppermute | solution.py:19
  98.3 5.3 %collective-permute-start.13 = (f32[1,16,1,128]{3,2,1,0:T(1,128)S(1)}, f32[1,16,1,128]{3,2,1,0:T(1,128)S(1)}, u32[]{:S(2)}, u32[]{:S(2)}) collective-permute-start(f32[1,16,1,128]{3,2,1,0:T(1,128)S(1)} %get-tuple-element.18), channel_id=1, source_target_pairs={{4,0},{8,4},{12,8},{16,12},{20,16},{24,20},{28,24},{32,28},{36,32}... | collective-permute-start | bytes 24584 | tf_op jit(solution)/shard_map/ppermute | solution.py:21
  103.6 9.4 %copy-start.11 = (f32[64,128,8]{1,2,0:T(8,128)S(1)}, f32[64,128,8]{1,2,0:T(8,128)}, u32[]{:S(2)}) copy-start(f32[64,128,8]{1,2,0:T(8,128)} %convolution_add_fusion.7) | copy-start | bytes 786436
  106.1 9.2 %collective-permute-start.14 = (f32[1,16,66,1]{2,1,3,0:T(8,128)S(1)}, f32[1,16,66,1]{2,1,3,0:T(8,128)S(1)}, u32[]{:S(2)}, u32[]{:S(2)}) collective-permute-start(f32[1,16,66,1]{2,1,3,0:T(8,128)S(1)} %copy.29), channel_id=1, source_target_pairs={{0,1},{1,2},{2,3},{4,5},{5,6},{6,7},{8,9},{9,10},{10,11},{12,13},{... | collective-permute-start | bytes 12680 | tf_op jit(solution)/shard_map/ppermute | solution.py:19
  109.5 7.0 %collective-permute-start.15 = (f32[1,16,66,1]{2,1,3,0:T(8,128)S(1)}, f32[1,16,66,1]{2,1,3,0:T(8,128)S(1)}, u32[]{:S(2)}, u32[]{:S(2)}) collective-permute-start(f32[1,16,66,1]{2,1,3,0:T(8,128)S(1)} %copy.30), channel_id=1, source_target_pairs={{1,0},{2,1},{3,2},{5,4},{6,5},{7,6},{9,8},{10,9},{11,10},{13,12},{... | collective-permute-start | bytes 12680 | tf_op jit(solution)/shard_map/ppermute | solution.py:21
  119.6 1.0 copy-start.12
  120.6 0.8 copy-start.10
  145.0 2.9 %copy-start.15 = (bf16[64,8,128]{2,1,0:T(8,128)(2,1)S(1)}, bf16[64,8,128]{2,1,0:T(8,128)(2,1)}, u32[]{:S(2)}) copy-start(bf16[64,8,128]{2,1,0:T(8,128)(2,1)} %gather_fusion.2) | copy-start | bytes 393220
  145.0 5.9 %copy-start.9 = (bf16[64,128,128]{2,1,0:T(8,128)(2,1)S(1)}, bf16[64,128,128]{2,1,0:T(8,128)(2,1)}, u32[]{:S(2)}) copy-start(bf16[64,128,128]{2,1,0:T(8,128)(2,1)} %gather_fusion.5) | copy-start | bytes 6291460
  145.0 5.9 %copy-start.14 = (bf16[64,8,128]{2,1,0:T(8,128)(2,1)S(1)}, bf16[64,8,128]{2,1,0:T(8,128)(2,1)}, u32[]{:S(2)}) copy-start(bf16[64,8,128]{2,1,0:T(8,128)(2,1)} %gather_fusion.4) | copy-start | bytes 393220
  148.0 4.2 %copy-start.8 = (bf16[64,128,128]{2,1,0:T(8,128)(2,1)S(1)}, bf16[64,128,128]{2,1,0:T(8,128)(2,1)}, u32[]{:S(2)}) copy-start(bf16[64,128,128]{2,1,0:T(8,128)(2,1)} %gather_fusion.7) | copy-start | bytes 6291460
  148.0 4.2 %copy-start.13 = (bf16[64,8,128]{2,1,0:T(8,128)(2,1)S(1)}, bf16[64,8,128]{2,1,0:T(8,128)(2,1)}, u32[]{:S(2)}) copy-start(bf16[64,8,128]{2,1,0:T(8,128)(2,1)} %gather_fusion.6) | copy-start | bytes 393220
  150.9 2.4 %copy-start.7 = (bf16[64,128,128]{2,1,0:T(8,128)(2,1)S(1)}, bf16[64,128,128]{2,1,0:T(8,128)(2,1)}, u32[]{:S(2)}) copy-start(bf16[64,128,128]{2,1,0:T(8,128)(2,1)} %gather_fusion.9) | copy-start | bytes 6291460
  152.1 2.4 %copy-start.6 = (bf16[64,128,128]{2,1,0:T(8,128)(2,1)S(1)}, bf16[64,128,128]{2,1,0:T(8,128)(2,1)}, u32[]{:S(2)}) copy-start(bf16[64,128,128]{2,1,0:T(8,128)(2,1)} %gather_fusion.11) | copy-start | bytes 6291460
  152.1 2.4 %copy-start.18 = (f32[8]{0:T(128)S(1)}, f32[8]{0:T(128)}, u32[]{:S(2)}) copy-start(f32[8]{0:T(128)} %param.13) | copy-start | bytes 100
  154.5 2.1 %copy-start.16 = (f32[1,64,128]{2,0,1:T(1,128)S(1)}, f32[1,64,128]{2,0,1:T(1,128)}, u32[]{:S(2)}) copy-start(f32[1,64,128]{2,0,1:T(1,128)} %slice.283) | copy-start | bytes 98308
where the time goes:
time: 160 us; the launch traced here: 158 us
  local copies, waits for them, and re-layouts  47.8 us (30%)
  starting transfers between devices  44 us (28%)
  blocking collectives  17.3 us (11%)
  matrix products  16.9 us (11%)
  other arithmetic  16.1 us (10%)
  waiting for transfers between devices  14.8 us (9%)
    ppermute x8, starting transfers between devices, extended(): lax.ppermute(tail, axis, [(i, (i + 1) % count) for i in range(ends)])  25 us
    ppermute x8, starting transfers between devices, extended(): lax.ppermute(head, axis, [((i + 1) % count, i) for i in range(ends)])  18.9 us
    all_gather x1, blocking collectives, body(): gathered = lax.all_gather(patches, 'grp', axis=0, tiled=True)  17.3 us
    ppermute x8, waiting for transfers between devices, extended(): lax.ppermute(head, axis, [((i + 1) % count, i) for i in range(ends)])  14.7 us
    gather x6, local copies, waits for them, and re-layouts, remap_patches(): weights = remap_blocks[block_ids_local[:, entry]]  13 us
    slice x12, local copies, waits for them, and re-layouts, extended(): lax.slice_in_dim(cells, cells.shape[dim] - width, cells.shape[dim], axis=...  11 us
    dot_general x6, matrix products, remap_patches(): jnp.einsum('nfp,nqp->nfq', picked, weights, preferred_element_type=jnp.fl...  10.6 us
    squeeze x4, other arithmetic, body(): padded = extend(field[None], 1, group, row_tile, tiles_x)[0]  7.96 us
  transfers between devices with their start and end apart: 16, of which 6 were waited for; matrix products, arithmetic and copies ran while one was open for 20% of the time, Pallas kernels for 0%

commit v1 on v0

v1 whole, which is shorter than its diff:
```python
import jax
import jax.numpy as jnp
from jax import lax
from jax.experimental import pallas as pl
from jax.experimental.pallas import tpu as pltpu
from jax.sharding import PartitionSpec as P

FIELDS = 8
LEVELS = 16
SUBSTEPS = 4
ROWS = 64
COLS = 128
TILES = ROWS // 8
BASE = 16
DEEP = ROWS + 32
F32 = jnp.float32
BF16 = jnp.bfloat16

VMEM = pl.BlockSpec(memory_space=pltpu.VMEM)
SMEM = pl.BlockSpec(memory_space=pltpu.SMEM)
ANY = pl.BlockSpec(memory_space=pl.ANY)


def sub_ids():
    return lax.broadcasted_iota(jnp.int32, (8, COLS), 0)


def lane_ids():
    return lax.broadcasted_iota(jnp.int32, (8, COLS), 1)


def edge_rows_kernel(st_top, st_low, wi_top, wi_low, to_up, to_down, sheet_up, sheet_down):
    upper = sub_ids() < 4
    for l in range(LEVELS):
        top, low = st_top[l], st_low[l]
        top_hi, low_hi = top.astype(BF16).astype(F32), low.astype(BF16).astype(F32)
        sheet_up[8 * l : 8 * l + 8] = jnp.where(upper, top_hi, pltpu.roll(top - top_hi, 4, 0))
        sheet_down[8 * l : 8 * l + 8] = jnp.where(upper, pltpu.roll(low_hi, 4, 0), low - low_hi)
        k = LEVELS + l
        sheet_up[8 * k : 8 * k + 8] = jnp.where(upper, wi_top[0, l], pltpu.roll(wi_top[1, l], 4, 0))
        sheet_down[8 * k : 8 * k + 8] = jnp.where(upper, pltpu.roll(wi_low[0, l], 4, 0), wi_low[1, l])
    to_up[...] = sheet_up[...].astype(BF16)
    to_down[...] = sheet_down[...].astype(BF16)


def packed(strip, tile, l):
    turned = pltpu.roll(tile, 8 * l + 4, 1)
    return jnp.where((lane_ids() >> 3) == l, turned, strip)


def own_strips_kernel(state, winds, strips):
    def row_tile(t, carry):
        r = pl.multiple_of(t * 8, 8)
        sources = (state, winds.at[0], winds.at[1])
        for c in range(3):
            strip = jnp.zeros((8, COLS), F32)
            for l in range(LEVELS):
                strip = packed(strip, sources[c][l, pl.ds(r, 8), :], l)
            strips[c, pl.ds(r, 8), :] = strip
        return carry

    lax.fori_loop(0, TILES, row_tile, 0)


def edge_columns_kernel(flags, from_below, from_above, own, halo, strip0, to_right, to_left,
                        below, above, full, right_sheet, left_sheet):
    below[...] = from_below[...].astype(F32)
    above[...] = from_above[...].astype(F32)
    upper = sub_ids() < 4
    ok = jnp.where(upper, flags[1], flags[0]) != 0
    full[:, 0:ROWS, :] = own[...]
    parts = [jnp.zeros((8, COLS), F32)] * 3
    for l in range(LEVELS):
        b, a = below[8 * l : 8 * l + 8], above[8 * l : 8 * l + 8]
        s = jnp.where(upper, b + pltpu.roll(b, 4, 0), a + pltpu.roll(a, 4, 0))
        k = LEVELS + l
        b, a = below[8 * k : 8 * k + 8], above[8 * k : 8 * k + 8]
        u = jnp.where(upper, b, pltpu.roll(a, 4, 0))
        v = jnp.where(upper, pltpu.roll(b, 4, 0), a)
        for c, x in enumerate((s, u, v)):
            x = jnp.where(ok, x, 0.0)
            halo[c, 8 * l : 8 * l + 8] = x
            parts[c] = packed(parts[c], x, l)
    for c in range(3):
        full[c, ROWS : ROWS + 8] = parts[c]
    strip0[...] = full[0]
    first = (lane_ids() & 7) < 4
    n = ROWS + 8
    for t in range(TILES + 1):
        r = 8 * t
        s, u, v = full[0, r : r + 8], full[1, r : r + 8], full[2, r : r + 8]
        hi = s.astype(BF16).astype(F32)
        lo = s - hi
        right_sheet[r : r + 8] = jnp.where(first, hi, pltpu.roll(lo, 4, 1))
        left_sheet[r : r + 8] = jnp.where(first, pltpu.roll(lo, COLS - 4, 1), hi)
        right_sheet[n + r : n + r + 8] = jnp.where(first, u, pltpu.roll(v, 4, 1))
        left_sheet[n + r : n + r + 8] = jnp.where(first, pltpu.roll(v, COLS - 4, 1), u)
    to_right[...] = right_sheet[...].astype(BF16)
    to_left[...] = left_sheet[...].astype(BF16)


def stencil(s, n, so, w, e, u, v, d):
    drift = u * (e - w) + v * (so - n)
    return s + d * ((n + so) + (w + e) - 4.0 * s) - 0.5 * drift


def substeps_kernel(flags, diffusivity, coupling, state, winds, halo, strip0, from_left, from_right,
                    state_out, fluxes, boundary, rounded,
                    cells, strips, inner, wind_strips, rate_strip, rate_halo_ok, total, left, right):
    lane = lane_ids()
    sub = sub_ids()
    upper = sub < 4
    place = lane & 7
    first = place < 4
    last_lane, first_lane = lane == COLS - 1, lane == 0
    inner_left, inner_right = place == 3, place == 4
    ocean = flags[4]
    is_ocean = ocean == 1

    left[...] = from_left[...].astype(F32)
    right[...] = from_right[...].astype(F32)
    side_ok = jnp.where(first, flags[2], flags[3]) != 0
    row_ok = jnp.where(upper, flags[1], flags[0]) != 0
    n = ROWS + 8
    rate = jnp.zeros((8, COLS), F32)
    for l in range(LEVELS):
        rate = jnp.where((lane >> 3) == l, diffusivity[ocean, l], rate)
    rate = jnp.where(side_ok, rate, 0.0)
    rate_strip[0:8] = rate
    rate_strip[8:16] = jnp.where(row_ok, rate, 0.0)
    rate_halo_ok[...] = jnp.where(row_ok, 1.0, 0.0)

    def put_strip(buf, t, x):
        if t < TILES:
            strips[buf, BASE + 8 * t : BASE + 8 * t + 8] = x
        else:
            strips[buf, BASE - 8 : BASE] = x
            strips[buf, BASE + ROWS : BASE + ROWS + 8] = x

    for t in range(TILES + 1):
        r = 8 * t
        a, b = left[r : r + 8], right[r : r + 8]
        s = jnp.where(first, a + pltpu.roll(a, COLS - 4, 1), b + pltpu.roll(b, 4, 1))
        put_strip(0, t, jnp.where(side_ok, s, 0.0))
        a, b = left[n + r : n + r + 8], right[n + r : n + r + 8]
        u = jnp.where(first, a, b)
        v = jnp.where(first, pltpu.roll(a, COLS - 4, 1), pltpu.roll(b, 4, 1))
        wind_strips[0, r : r + 8] = jnp.where(side_ok, u, 0.0)
        wind_strips[1, r : r + 8] = jnp.where(side_ok, v, 0.0)
        inner[0, r : r + 8] = strip0[r : r + 8]

    def copy_level(l, carry):
        h = pl.multiple_of(8 * l, 8)
        cells[0, l, BASE : BASE + ROWS] = state[l]
        x = halo[0, pl.ds(h, 8), :]
        cells[0, l, BASE - 8 : BASE] = x
        cells[0, l, BASE + ROWS : BASE + ROWS + 8] = x
        return carry

    lax.fori_loop(0, LEVELS, copy_level, 0)

    def rows_of(load, t):
        if t < TILES:
            r = BASE + 8 * t
            return load(r), load(r - 1), load(r + 1)
        low, up = BASE + ROWS, BASE - 8
        north = jnp.where(upper, load(low - 1), load(up - 1))
        south = jnp.where(upper, load(low + 1), load(up + 1))
        return load(low), north, south

    for step in range(SUBSTEPS):
        now, later = step % 2, (step + 1) % 2
        last = step == SUBSTEPS - 1
        count = TILES if last else TILES + 1
        if not last:
            for t in range(count):
                s, no, so = rows_of(lambda r: strips[now, r : r + 8], t)
                edge = inner[now, 8 * t : 8 * t + 8]
                w = pltpu.roll(jnp.where(inner_left, edge, s), 1, 1)
                e = pltpu.roll(jnp.where(inner_right, edge, s), COLS - 1, 1)
                u, v = wind_strips[0, 8 * t : 8 * t + 8], wind_strips[1, 8 * t : 8 * t + 8]
                d = rate_strip[0:8] if t < TILES else rate_strip[8:16]
                put_strip(later, t, stencil(s, no, so, w, e, u, v, d))

        def level(l, carry):
            h = pl.multiple_of(8 * l, 8)
            d_level = diffusivity[ocean, l]
            mine = (lane >> 3) == l
            for t in range(count):
                s, no, so = rows_of(lambda r: cells[now, l, r : r + 8, :], t)
                r = BASE + 8 * t
                side = pltpu.roll(strips[now, r : r + 8], COLS - 4 - 8 * l, 1)
                w = pltpu.roll(jnp.where(last_lane, side, s), 1, 1)
                e = pltpu.roll(jnp.where(first_lane, side, s), COLS - 1, 1)
                if t < TILES:
                    u, v = winds[0, l, 8 * t : 8 * t + 8, :], winds[1, l, 8 * t : 8 * t + 8, :]
                    d = d_level
                else:
                    u, v = halo[1, pl.ds(h, 8), :], halo[2, pl.ds(h, 8), :]
                    d = d_level * rate_halo_ok[...]
                x = stencil(s, no, so, w, e, u, v, d)
                if not last:
                    if t < TILES:
                        cells[later, l, r : r + 8, :] = x
                    else:
                        cells[later, l, BASE - 8 : BASE, :] = x
                        cells[later, l, BASE + ROWS : BASE + ROWS + 8, :] = x
                    turned = pltpu.roll(x, 8 * l + 4, 1)
                    old = inner[later, 8 * t : 8 * t + 8]
                    inner[later, 8 * t : 8 * t + 8] = jnp.where(mine, turned, old)
                else:
                    state_out[l, 8 * t : 8 * t + 8, :] = x
                if t < TILES:
                    if step == 0:
                        total[l, 8 * t : 8 * t + 8, :] = x
                    else:
                        total[l, 8 * t : 8 * t + 8, :] = total[l, 8 * t : 8 * t + 8, :] + x
            return carry

        if step == 0:
            inner[later] = jnp.zeros((n, COLS), F32)
        lax.fori_loop(0, LEVELS, level, 0)

    def flux(t, carry):
        r = pl.multiple_of(16 * t, 16)
        sums = [None] * FIELDS
        for l in range(LEVELS):
            x = total[l, pl.ds(r, 16), :]
            for f in range(FIELDS):
                term = coupling[f, l] * x
                sums[f] = term if l == 0 else sums[f] + term
        for f in range(FIELDS):
            mean = sums[f] * (1.0 / SUBSTEPS)
            fluxes[f, pl.ds(r, 16), :] = mean
            rounded[pl.ds(pl.multiple_of(f * ROWS + r, 16), 16), :] = mean.astype(BF16)
            if f == 0:
                boundary[pl.ds(r, 16), :] = jnp.where(is_ocean, state_out[0, pl.ds(r, 16), :], mean)
        return carry

    lax.fori_loop(0, ROWS // 16, flux, 0)


def remap_kernel(flags, source, blocks, sea, heat, gathered, weights, flux_in, boundary_in,
                 flux_out, boundary_out, patches, remapped, surface, sems):
    @pl.when(flags[4] == 1)
    def _():
        fetch = pltpu.make_async_copy(boundary_in, surface, sems.at[0])
        fetch.start()
        patches[...] = gathered[...].astype(F32)

        def patch(o, carry):
            total = jnp.zeros((FIELDS, COLS), F32)
            for entry in range(6):
                where = source[o, entry]
                start = (where >> 6) * (FIELDS * ROWS) + (where & 63)
                picked = patches[pl.ds(start, FIELDS, stride=ROWS), :].astype(BF16)
                block = weights[blocks[o, entry]]
                total = total + lax.dot_general(
                    picked, block, (((1,), (1,)), ((), ())), preferred_element_type=F32
                )
            remapped[pl.ds(o, FIELDS, stride=ROWS), :] = total * sea[0, o].astype(F32)
            return carry

        lax.fori_loop(0, ROWS, patch, 0, unroll=4)
        send = pltpu.make_async_copy(remapped, flux_out, sems.at[1])
        send.start()
        warmth = jnp.zeros((ROWS, COLS), F32)
        for f in range(FIELDS):
            warmth = warmth + heat[f] * remapped[f * ROWS : (f + 1) * ROWS, :]
        fetch.wait()
        surface[...] = surface[...] + warmth
        put = pltpu.make_async_copy(surface, boundary_out, sems.at[2])
        put.start()
        send.wait()
        put.wait()


def body(
    state, winds, diffusivity, coupling, heat_coef, remap_blocks, source_patch, block_ids, land_sea
):
    group = lax.axis_index("grp")
    row_tile = lax.axis_index("gx")
    column_tile = lax.axis_index("gy")
    tiles_x = lax.axis_size("gx")
    tiles_y = lax.axis_size("gy")
    groups = lax.axis_size("grp")
    ocean = group == groups - 1
    line = group * tiles_x + row_tile
    top = (line == 0) | (ocean & (row_tile == 0))
    bottom = (row_tile == tiles_x - 1) & (group >= groups - 2)
    flags = jnp.stack(
        [~top, ~bottom, column_tile > 0, column_tile < tiles_y - 1, ocean]
    ).astype(jnp.int32)

    def ring(x, axis, shift):
        count = lax.axis_size(axis)
        return lax.ppermute(x, axis, [(i, (i + shift) % count) for i in range(count)])

    sheet = jax.ShapeDtypeStruct((2 * LEVELS * 8, COLS), BF16)
    first_rows = pl.BlockSpec((LEVELS, 8, COLS), lambda i: (0, 0, 0))
    last_rows = pl.BlockSpec((LEVELS, 8, COLS), lambda i: (0, TILES - 1, 0))
    first_winds = pl.BlockSpec((2, LEVELS, 8, COLS), lambda i: (0, 0, 0, 0))
    last_winds = pl.BlockSpec((2, LEVELS, 8, COLS), lambda i: (0, 0, TILES - 1, 0))
    whole = pl.BlockSpec(sheet.shape, lambda i: (0, 0))
    to_up, to_down = pl.pallas_call(
        edge_rows_kernel,
        grid=(1,),
        in_specs=[first_rows, last_rows, first_winds, last_winds],
        out_specs=[whole, whole],
        out_shape=[sheet, sheet],
        scratch_shapes=[pltpu.VMEM(sheet.shape, F32)] * 2,
        name="edge_rows",
    )(state, state, winds, winds)
    from_below = ring(to_up, ("grp", "gx"), -1)
    from_above = ring(to_down, ("grp", "gx"), 1)
    own = pl.pallas_call(
        own_strips_kernel,
        in_specs=[VMEM, VMEM],
        out_specs=VMEM,
        out_shape=jax.ShapeDtypeStruct((3, ROWS, COLS), F32),
        name="own_strips",
    )(state, winds)
    n = ROWS + 8
    columns = jax.ShapeDtypeStruct((2 * n, COLS), BF16)
    halo, strip0, to_right, to_left = pl.pallas_call(
        edge_columns_kernel,
        in_specs=[SMEM, VMEM, VMEM, VMEM],
        out_specs=[VMEM] * 4,
        out_shape=[
            jax.ShapeDtypeStruct((3, LEVELS * 8, COLS), F32),
            jax.ShapeDtypeStruct((n, COLS), F32),
            columns,
            columns,
        ],
        scratch_shapes=[
            pltpu.VMEM(sheet.shape, F32),
            pltpu.VMEM(sheet.shape, F32),
            pltpu.VMEM((3, n, COLS), F32),
            pltpu.VMEM((2 * n, COLS), F32),
            pltpu.VMEM((2 * n, COLS), F32),
        ],
        name="edge_columns",
    )(flags, from_below, from_above, own)
    from_left = ring(to_right, "gy", 1)
    from_right = ring(to_left, "gy", -1)
    state_out, fluxes, boundary, rounded = pl.pallas_call(
        substeps_kernel,
        in_specs=[SMEM] * 3 + [VMEM] * 6,
        out_specs=[VMEM] * 4,
        out_shape=[
            jax.ShapeDtypeStruct(state.shape, F32),
            jax.ShapeDtypeStruct((FIELDS, ROWS, COLS), F32),
            jax.ShapeDtypeStruct((ROWS, COLS), F32),
            jax.ShapeDtypeStruct((FIELDS * ROWS, COLS), BF16),
        ],
        scratch_shapes=[
            pltpu.VMEM((2, LEVELS, DEEP, COLS), F32),
            pltpu.VMEM((2, DEEP, COLS), F32),
            pltpu.VMEM((2, n, COLS), F32),
            pltpu.VMEM((2, n, COLS), F32),
            pltpu.VMEM((16, COLS), F32),
            pltpu.VMEM((8, COLS), F32),
            pltpu.VMEM((LEVELS, ROWS, COLS), F32),
            pltpu.VMEM((2 * n, COLS), F32),
            pltpu.VMEM((2 * n, COLS), F32),
        ],
        compiler_params=pltpu.CompilerParams(vmem_limit_bytes=16 * 2**20),
        name="substeps",
    )(flags, diffusivity, coupling, state, winds, halo, strip0, from_left, from_right)
    gathered = lax.all_gather(rounded, "grp", axis=0, tiled=True)
    fluxes, boundary = pl.pallas_call(
        remap_kernel,
        in_specs=[SMEM] * 5 + [VMEM] * 2 + [ANY] * 2,
        out_specs=[ANY] * 2,
        out_shape=[
            jax.ShapeDtypeStruct((FIELDS * ROWS, COLS), F32),
            jax.ShapeDtypeStruct((ROWS, COLS), F32),
        ],
        input_output_aliases={7: 0, 8: 1},
        scratch_shapes=[
            pltpu.VMEM(gathered.shape, F32),
            pltpu.VMEM((FIELDS * ROWS, COLS), F32),
            pltpu.VMEM((ROWS, COLS), F32),
            pltpu.SemaphoreType.DMA((3,)),
        ],
        compiler_params=pltpu.CompilerParams(vmem_limit_bytes=16 * 2**20),
        name="remap",
    )(
        flags,
        source_patch[0, 0],
        block_ids[0, 0],
        land_sea[0],
        heat_coef,
        gathered,
        remap_blocks,
        fluxes.reshape(FIELDS * ROWS, COLS),
        boundary,
    )
    return state_out, boundary, fluxes.reshape(FIELDS, ROWS, COLS)


def solution(mesh):
    return jax.shard_map(
        body,
        mesh=mesh,
        in_specs=(
            P(None, ("grp", "gx"), "gy"),
            P(None, None, ("grp", "gx"), "gy"),
            P(),
            P(),
            P(),
            P(),
            P("gx", "gy", None, None),
            P("gx", "gy", None, None),
            P("gx", "gy", None),
        ),
        out_specs=(
            P(None, ("grp", "gx"), "gy"),
            P(("grp", "gx"), "gy"),
            P(None, ("grp", "gx"), "gy"),
        ),
        check_vma=False,
    )
```

time: 160 us -> 61.9 us (0.39)
  the two profiles are of different devices: /device:TPU:79 before, /device:TPU:5 now
where the time goes in v1:
time: 61.9 us; the launch traced here: 61.6 us
  Pallas kernels  33.4 us (54%)
  blocking collectives  9.95 us (16%)
  starting transfers between devices  9.54 us (15%)
  waiting for transfers between devices  4.17 us (7%)
  local copies, waits for them, and re-layouts  3.31 us (5%)
  between operations  0.72 us (1%)
    pallas_call x1, Pallas kernels, body(): pl.pallas_call(substeps_kernel, in_specs=[SMEM] * 3 + [VMEM] * 6, out_spe...  15.9 us
    pallas_call x1, Pallas kernels, body(): pl.pallas_call(remap_kernel, in_specs=[SMEM] * 5 + [VMEM] * 2 + [ANY] * 2...  10.9 us
    all_gather x1, blocking collectives, body(): gathered = lax.all_gather(rounded, 'grp', axis=0, tiled=True)  9.95 us
    ppermute x4, starting transfers between devices, ring(): lax.ppermute(x, axis, [(i, (i + shift) % count) for i in range(count)])  9.54 us
    ppermute x4, waiting for transfers between devices, ring(): lax.ppermute(x, axis, [(i, (i + shift) % count) for i in range(count)])  4.17 us
    unnamed x30, local copies, waits for them, and re-layouts  3.2 us
    pallas_call x1, Pallas kernels, body(): pl.pallas_call(own_strips_kernel, in_specs=[VMEM, VMEM], out_specs=VMEM,...  3 us
    pallas_call x1, Pallas kernels, body(): pl.pallas_call(edge_rows_kernel, grid=(1,), in_specs=[first_rows, last_ro...  1.81 us
  transfers between devices with their start and end apart: 4, of which 2 were waited for; matrix products, arithmetic and copies ran while one was open for 1% of the time, Pallas kernels for 5%

profile of v1, /device:TPU:5, one launch (start us, length us, event | category | flops | bytes accessed | tf_op | source)
XLA Modules:
  0.0 61.6 jit_solution(14766888632168669581)
XLA Ops:
  0.6 0.0 copy-start
  0.6 0.0 copy-start.1
  0.7 0.0 copy-start.12
  0.7 0.0 copy-start.13
  0.7 0.0 copy-start.6
  0.7 0.0 copy-start.7
  0.7 1.8 %edge_rows.1 = (bf16[256,128]{1,0:T(8,128)(2,1)}, bf16[256,128]{1,0:T(8,128)(2,1)}) custom-call(f32[16,64,128]{2,1,0:T(8,128)} %state.3, f32[16,64,128]{2,1,0:T(8,128)} %state.3, f32[2,16,64,128]{3,2,1,0:T(8,128)} %winds.3, f32[2,16,64,128]{3,2,1,0:T(8,128)} %winds.3), custom_call_target="tpu_custom_call" | custom-call | tf_op jit(solution)/shard_map/edge_rows/pallas_call | solution.py:305
  2.5 6.8 %collective-permute-start = (bf16[256,128]{1,0:T(8,128)(2,1)}, bf16[256,128]{1,0:T(8,128)(2,1)S(1)}, u32[]{:S(2)}, u32[]{:S(2)}) collective-permute-start(bf16[256,128]{1,0:T(8,128)(2,1)} %get-tuple-element.15), channel_id=1, source_target_pairs={{0,252},{4,0},{8,4},{12,8},{16,12},{20,16},{24,20},{28,24},{32,28}... | collective-permute-start | bytes 196616 | tf_op jit(solution)/shard_map/ppermute | solution.py:297
  9.3 0.0 collective-permute-start.1
  9.3 0.0 copy-start.8
  9.3 0.0 copy-start.9
  9.3 3.0 %own_strips.1.own = f32[3,64,128]{2,1,0:T(8,128)} custom-call(f32[16,64,128]{2,1,0:T(8,128)} %state.3, f32[2,16,64,128]{3,2,1,0:T(8,128)} %winds.3), custom_call_target="tpu_custom_call" | custom-call | tf_op jit(solution)/shard_map/own_strips/pallas_call | solution.py:316
  12.3 0.1 stack.23
  12.4 0.5 convert_element_type.3.flags
  12.9 0.0 collective-permute-done.from_below
  12.9 0.0 copy-start.10
  12.9 2.8 %collective-permute-done.1.from_above = bf16[256,128]{1,0:T(8,128)(2,1)S(1)} collective-permute-done((bf16[256,128]{1,0:T(8,128)(2,1)}, bf16[256,128]{1,0:T(8,128)(2,1)S(1)}, u32[]{:S(2)}, u32[]{:S(2)}) %collective-permute-start.1) | collective-permute-done | bytes 65568 | tf_op jit(solution)/shard_map/ppermute | solution.py:297
  15.7 0.0 copy-done.10
  15.7 0.0 copy-start.11
  15.7 0.6 %copy-done.11 = bf16[256,128]{1,0:T(8,128)(2,1)} copy-done((bf16[256,128]{1,0:T(8,128)(2,1)}, bf16[256,128]{1,0:T(8,128)(2,1)S(1)}, u32[]{:S(2)}) %copy-start.11) | copy-done | bytes 65560
  16.4 1.8 %edge_columns.1 = (f32[3,128,128]{2,1,0:T(8,128)}, f32[72,128]{1,0:T(8,128)}, bf16[144,128]{1,0:T(8,128)(2,1)}, bf16[144,128]{1,0:T(8,128)(2,1)}) custom-call(s32[5]{0:T(128)} %convert_element_type.3.flags, bf16[256,128]{1,0:T(8,128)(2,1)} %copy-done.10, bf16[256,128]{1,0:T(8,128)(2,1)} %copy-done.11, f32[3,64,128]{2,1,0:T(8,128)} %own_strips.1.own), custom_call_target="tpu_custom_call" | custom-call | tf_op jit(solution)/shard_map/edge_columns/pallas_call | solution.py:325
  18.1 1.3 %collective-permute-start.2 = (bf16[144,128]{1,0:T(8,128)(2,1)}, bf16[144,128]{1,0:T(8,128)(2,1)S(1)}, u32[]{:S(2)}, u32[]{:S(2)}) collective-permute-start(bf16[144,128]{1,0:T(8,128)(2,1)} %get-tuple-element.19), channel_id=1, source_target_pairs={{0,1},{1,2},{2,3},{3,0},{4,5},{5,6},{6,7},{7,4},{8,9},{9,10},{10,1... | collective-permute-start | bytes 110600 | tf_op jit(solution)/shard_map/ppermute | solution.py:297
  19.4 1.5 %collective-permute-start.3 = (bf16[144,128]{1,0:T(8,128)(2,1)}, bf16[144,128]{1,0:T(8,128)(2,1)S(1)}, u32[]{:S(2)}, u32[]{:S(2)}) collective-permute-start(bf16[144,128]{1,0:T(8,128)(2,1)} %get-tuple-element.20), channel_id=1, source_target_pairs={{0,3},{1,0},{2,1},{3,2},{4,7},{5,4},{6,5},{7,6},{8,11},{9,8},{10,9... | collective-permute-start | bytes 110600 | tf_op jit(solution)/shard_map/ppermute | solution.py:297
  20.9 0.0 copy-done.12
  20.9 0.1 copy.14
  21.0 0.0 copy-done.13
  21.0 0.1 copy.15
  21.1 0.0 copy-start.2
  21.1 1.3 %collective-permute-done.2.from_left = bf16[144,128]{1,0:T(8,128)(2,1)S(1)} collective-permute-done((bf16[144,128]{1,0:T(8,128)(2,1)}, bf16[144,128]{1,0:T(8,128)(2,1)S(1)}, u32[]{:S(2)}, u32[]{:S(2)}) %collective-permute-start.2) | collective-permute-done | bytes 36896 | tf_op jit(solution)/shard_map/ppermute | solution.py:297
  22.4 0.0 collective-permute-done.3.from_right
  22.5 0.0 copy-done
  22.5 0.0 copy-done.1
  22.5 0.0 copy-done.6
  22.5 0.0 copy-done.7
  22.5 0.0 copy-start.3
  22.5 0.9 %copy-done.3 = f32[3,128,128]{2,1,0:T(8,128)S(1)} copy-done((f32[3,128,128]{2,1,0:T(8,128)S(1)}, f32[3,128,128]{2,1,0:T(8,128)}, u32[]{:S(2)}) %copy-start.3) | copy-done | bytes 196632
  23.4 0.0 copy-start.4
  23.4 0.8 %copy-done.4 = f32[72,128]{1,0:T(8,128)S(1)} copy-done((f32[72,128]{1,0:T(8,128)S(1)}, f32[72,128]{1,0:T(8,128)}, u32[]{:S(2)}) %copy-start.4) | copy-done | bytes 36888
  24.2 0.0 copy-start.5
  24.2 0.7 %copy-done.5 = s32[5]{0:T(128)S(1)} copy-done((s32[5]{0:T(128)S(1)}, s32[5]{0:T(128)}, u32[]{:S(2)}) %copy-start.5) | copy-done | bytes 44
  24.8 15.9 %substeps.1 = (f32[16,64,128]{2,1,0:T(8,128)}, f32[8,64,128]{2,1,0:T(8,128)}, f32[64,128]{1,0:T(8,128)}, bf16[512,128]{1,0:T(8,128)(2,1)S(1)}) custom-call(s32[5]{0:T(128)S(1)} %copy-done.5, f32[2,16]{1,0:T(2,128)S(1)} %copy-done.7, f32[8,16]{1,0:T(8,128)S(1)} %copy-done.6, f32[16,64,128]{2,1,0:T(8,128)S(1)} %copy-done.1, f32[2,16,64,128]{3,2,1,0:T(8,128)S(1)} %copy-done, ...), custom_call_target="tpu_custom_call" | custom-call | tf_op jit(solution)/shard_map/substeps/pallas_call | solution.py:346
  40.7 10.0 %all_gather.3.gathered = bf16[2048,128]{1,0:T(8,128)(2,1)S(1)} all-gather(bf16[512,128]{1,0:T(8,128)(2,1)S(1)} %get-tuple-element.22), channel_id=1, replica_groups=mesh['grp'=4,'gx'=16,'gy'=4] {'grp'}, dimensions={0}, use_global_device_ids=true | all-gather | bytes 655360 | tf_op jit(solution)/shard_map/all_gather | solution.py:370
  50.7 0.0 copy-done.8
  50.7 0.0 copy-done.9
  50.7 0.0 copy-done.2
  50.7 10.9 %remap.1 = (f32[512,128]{1,0:T(8,128)}, f32[64,128]{1,0:T(8,128)}) custom-call(s32[5]{0:T(128)S(1)} %copy-done.5, s32[64,6]{1,0:T(8,128)S(1)} %bitcast.10, s32[64,6]{1,0:T(8,128)S(1)} %bitcast.11, s32[1,64]{1,0:T(1,128)S(1)} %bitcast.12, f32[8]{0:T(128)S(1)} %copy-done.9, ...), custom_call_target="tpu_custom_call", output_to_operand_aliasing={{0}: (7, {}), {1}: (8, {})} | custom-call | tf_op jit(solution)/shard_map/remap/pallas_call | solution.py:371
Async XLA Ops:
  0.6 21.8 %copy-start = (f32[2,16,64,128]{3,2,1,0:T(8,128)S(1)}, f32[2,16,64,128]{3,2,1,0:T(8,128)}, u32[]{:S(2)}) copy-start(f32[2,16,64,128]{3,2,1,0:T(8,128)} %winds.3) | copy-start | bytes 3145732
  0.6 21.8 %copy-start.1 = (f32[16,64,128]{2,1,0:T(8,128)S(1)}, f32[16,64,128]{2,1,0:T(8,128)}, u32[]{:S(2)}) copy-start(f32[16,64,128]{2,1,0:T(8,128)} %state.3) | copy-start | bytes 1572868
  0.7 20.2 %copy-start.12 = (s32[1,1,64,6]{2,1,3,0:T(1,128)S(1)}, s32[1,1,64,6]{2,1,3,0:T(1,128)}, u32[]{:S(2)}) copy-start(s32[1,1,64,6]{2,1,3,0:T(1,128)} %param.15) | copy-start | bytes 4612
  0.7 20.3 %copy-start.13 = (s32[1,1,64,6]{2,1,3,0:T(1,128)S(1)}, s32[1,1,64,6]{2,1,3,0:T(1,128)}, u32[]{:S(2)}) copy-start(s32[1,1,64,6]{2,1,3,0:T(1,128)} %param.16) | copy-start | bytes 4612
  0.7 21.8 %copy-start.6 = (f32[8,16]{1,0:T(8,128)S(1)}, f32[8,16]{1,0:T(8,128)}, u32[]{:S(2)}) copy-start(f32[8,16]{1,0:T(8,128)} %coupling.1) | copy-start | bytes 1540
  0.7 21.8 %copy-start.7 = (f32[2,16]{1,0:T(2,128)S(1)}, f32[2,16]{1,0:T(2,128)}, u32[]{:S(2)}) copy-start(f32[2,16]{1,0:T(2,128)} %diffusivity.1) | copy-start | bytes 388
  2.5 10.4 %collective-permute-start = (bf16[256,128]{1,0:T(8,128)(2,1)}, bf16[256,128]{1,0:T(8,128)(2,1)S(1)}, u32[]{:S(2)}, u32[]{:S(2)}) collective-permute-start(bf16[256,128]{1,0:T(8,128)(2,1)} %get-tuple-element.15), channel_id=1, source_target_pairs={{0,252},{4,0},{8,4},{12,8},{16,12},{20,16},{24,20},{28,24},{32,28}... | collective-permute-start | bytes 196616 | tf_op jit(solution)/shard_map/ppermute | solution.py:297
  9.3 6.5 %collective-permute-start.1 = (bf16[256,128]{1,0:T(8,128)(2,1)}, bf16[256,128]{1,0:T(8,128)(2,1)S(1)}, u32[]{:S(2)}, u32[]{:S(2)}) collective-permute-start(bf16[256,128]{1,0:T(8,128)(2,1)} %get-tuple-element.16), channel_id=1, source_target_pairs={{0,4},{4,8},{8,12},{12,16},{16,20},{20,24},{24,28},{28,32},{32,36}... | collective-permute-start | bytes 196616 | tf_op jit(solution)/shard_map/ppermute | solution.py:297
  9.3 41.4 %copy-start.8 = (s32[1,1,64]{2,1,0:T(1,128)S(1)}, s32[1,1,64]{2,1,0:T(1,128)}, u32[]{:S(2)}) copy-start(s32[1,1,64]{2,1,0:T(1,128)} %param.17) | copy-start | bytes 772
  9.3 41.4 %copy-start.9 = (f32[8]{0:T(128)S(1)}, f32[8]{0:T(128)}, u32[]{:S(2)}) copy-start(f32[8]{0:T(128)} %heat.1) | copy-start | bytes 100
  12.9 2.8 %copy-start.10 = (bf16[256,128]{1,0:T(8,128)(2,1)}, bf16[256,128]{1,0:T(8,128)(2,1)S(1)}, u32[]{:S(2)}) copy-start(bf16[256,128]{1,0:T(8,128)(2,1)S(1)} %collective-permute-done.from_below) | copy-start | bytes 196612
  15.7 0.6 %copy-start.11 = (bf16[256,128]{1,0:T(8,128)(2,1)}, bf16[256,128]{1,0:T(8,128)(2,1)S(1)}, u32[]{:S(2)}) copy-start(bf16[256,128]{1,0:T(8,128)(2,1)S(1)} %collective-permute-done.1.from_above) | copy-start | bytes 196612
  18.1 4.3 %collective-permute-start.2 = (bf16[144,128]{1,0:T(8,128)(2,1)}, bf16[144,128]{1,0:T(8,128)(2,1)S(1)}, u32[]{:S(2)}, u32[]{:S(2)}) collective-permute-start(bf16[144,128]{1,0:T(8,128)(2,1)} %get-tuple-element.19), channel_id=1, source_target_pairs={{0,1},{1,2},{2,3},{3,0},{4,5},{5,6},{6,7},{7,4},{8,9},{9,10},{10,1... | collective-permute-start | bytes 110600 | tf_op jit(solution)/shard_map/ppermute | solution.py:297
  19.4 3.0 %collective-permute-start.3 = (bf16[144,128]{1,0:T(8,128)(2,1)}, bf16[144,128]{1,0:T(8,128)(2,1)S(1)}, u32[]{:S(2)}, u32[]{:S(2)}) collective-permute-start(bf16[144,128]{1,0:T(8,128)(2,1)} %get-tuple-element.20), channel_id=1, source_target_pairs={{0,3},{1,0},{2,1},{3,2},{4,7},{5,4},{6,5},{7,6},{8,11},{9,8},{10,9... | collective-permute-start | bytes 110600 | tf_op jit(solution)/shard_map/ppermute | solution.py:297
  21.1 29.6 %copy-start.2 = (bf16[64,128,128]{2,1,0:T(8,128)(2,1)S(1)}, bf16[64,128,128]{2,1,0:T(8,128)(2,1)}, u32[]{:S(2)}) copy-start(bf16[64,128,128]{2,1,0:T(8,128)(2,1)} %weights.1) | copy-start | bytes 6291460
  22.5 0.9 %copy-start.3 = (f32[3,128,128]{2,1,0:T(8,128)S(1)}, f32[3,128,128]{2,1,0:T(8,128)}, u32[]{:S(2)}) copy-start(f32[3,128,128]{2,1,0:T(8,128)} %get-tuple-element.17.halo) | copy-start | bytes 589828
  23.4 0.8 %copy-start.4 = (f32[72,128]{1,0:T(8,128)S(1)}, f32[72,128]{1,0:T(8,128)}, u32[]{:S(2)}) copy-start(f32[72,128]{1,0:T(8,128)} %get-tuple-element.18.strip0) | copy-start | bytes 110596
  24.2 0.7 %copy-start.5 = (s32[5]{0:T(128)S(1)}, s32[5]{0:T(128)}, u32[]{:S(2)}) copy-start(s32[5]{0:T(128)} %convert_element_type.3.flags) | copy-start | bytes 64

commit v2 on v0

v2 whole, which is shorter than its diff:
```python
import jax
import jax.numpy as jnp
from jax import lax
from jax.experimental import pallas as pl
from jax.experimental.pallas import tpu as pltpu
from jax.sharding import PartitionSpec as P

FIELDS = 8
LEVELS = 16
SUBSTEPS = 4
INTERSECTIONS = 6
ROWS = 64
COLS = 128
TILES = ROWS // 8
BASE = 16
DEEP = ROWS + 32
UNROLL = 4
BLOCK = 8
FLUX_ROWS = 32
FLUX_ON = True
STEPS = 4
CHUNK = 16
F32 = jnp.float32
BF16 = jnp.bfloat16

VMEM = pl.BlockSpec(memory_space=pltpu.VMEM)
SMEM = pl.BlockSpec(memory_space=pltpu.SMEM)
ANY = pl.BlockSpec(memory_space=pl.ANY)
HBM = pl.BlockSpec(memory_space=pltpu.HBM)


def sub_ids():
    return lax.broadcasted_iota(jnp.int32, (8, COLS), 0)


def lane_ids():
    return lax.broadcasted_iota(jnp.int32, (8, COLS), 1)


def edge_rows_kernel(state, winds, to_up, to_down, st_top, st_low, wi_top, wi_low,
                     sheet_up, sheet_down, sems):
    first, last = slice(0, 8), slice(ROWS - 8, ROWS)
    fetches = [
        pltpu.make_async_copy(source, target, sems.at[i])
        for i, (source, target) in enumerate((
            (winds.at[:, :, first], wi_top),
            (winds.at[:, :, last], wi_low),
            (state.at[:, first], st_top),
            (state.at[:, last], st_low),
        ))
    ]
    for fetch in fetches:
        fetch.start()
    for fetch in fetches:
        fetch.wait()
    upper = sub_ids() < 4
    for l in range(LEVELS):
        top, low = st_top[l], st_low[l]
        top_hi, low_hi = top.astype(BF16).astype(F32), low.astype(BF16).astype(F32)
        sheet_up[8 * l : 8 * l + 8] = jnp.where(upper, top_hi, pltpu.roll(top - top_hi, 4, 0))
        sheet_down[8 * l : 8 * l + 8] = jnp.where(upper, pltpu.roll(low_hi, 4, 0), low - low_hi)
        k = LEVELS + l
        sheet_up[8 * k : 8 * k + 8] = jnp.where(upper, wi_top[0, l], pltpu.roll(wi_top[1, l], 4, 0))
        sheet_down[8 * k : 8 * k + 8] = jnp.where(upper, pltpu.roll(wi_low[0, l], 4, 0), wi_low[1, l])
    to_up[...] = sheet_up[...].astype(BF16)
    to_down[...] = sheet_down[...].astype(BF16)


def packed(strip, tile, l):
    turned = pltpu.roll(tile, 8 * l + 4, 1)
    return jnp.where((lane_ids() >> 3) == l, turned, strip)


def own_strips_kernel(state, winds, strips):
    def row_tile(t, carry):
        r = pl.multiple_of(t * 8, 8)
        sources = (state, winds.at[0], winds.at[1])
        for c in range(3):
            strip = jnp.zeros((8, COLS), F32)
            for l in range(LEVELS):
                strip = packed(strip, sources[c][l, pl.ds(r, 8), :], l)
            strips[c, pl.ds(r, 8), :] = strip
        return carry

    lax.fori_loop(0, TILES, row_tile, 0)


def edge_columns_kernel(masks, from_below, from_above, own, halo, strip0, to_right, to_left,
                        below, above, full, right_sheet, left_sheet):
    below[...] = from_below[...].astype(F32)
    above[...] = from_above[...].astype(F32)
    upper = sub_ids() < 4
    ok = masks[0]
    full[:, 0:ROWS, :] = own[...]
    parts = [jnp.zeros((8, COLS), F32)] * 3
    for l in range(LEVELS):
        b, a = below[8 * l : 8 * l + 8], above[8 * l : 8 * l + 8]
        s = jnp.where(upper, b + pltpu.roll(b, 4, 0), a + pltpu.roll(a, 4, 0))
        k = LEVELS + l
        b, a = below[8 * k : 8 * k + 8], above[8 * k : 8 * k + 8]
        u = jnp.where(upper, b, pltpu.roll(a, 4, 0))
        v = jnp.where(upper, pltpu.roll(b, 4, 0), a)
        for c, x in enumerate((s, u, v)):
            x = x * ok
            halo[c, 8 * l : 8 * l + 8] = x
            parts[c] = packed(parts[c], x, l)
    for c in range(3):
        full[c, ROWS : ROWS + 8] = parts[c]
    strip0[...] = full[0]
    first = (lane_ids() & 7) < 4
    n = ROWS + 8
    for t in range(TILES + 1):
        r = 8 * t
        s, u, v = full[0, r : r + 8], full[1, r : r + 8], full[2, r : r + 8]
        hi = s.astype(BF16).astype(F32)
        lo = s - hi
        right_sheet[r : r + 8] = jnp.where(first, hi, pltpu.roll(lo, 4, 1))
        left_sheet[r : r + 8] = jnp.where(first, pltpu.roll(lo, COLS - 4, 1), hi)
        right_sheet[n + r : n + r + 8] = jnp.where(first, u, pltpu.roll(v, 4, 1))
        left_sheet[n + r : n + r + 8] = jnp.where(first, pltpu.roll(v, COLS - 4, 1), u)
    to_right[...] = right_sheet[...].astype(BF16)
    to_left[...] = left_sheet[...].astype(BF16)


def stencil(s, n, so, w, e, u, v, d, c):
    drift = u * (e - w) + v * (so - n)
    return c * s + d * ((n + so) + (w + e)) - 0.5 * drift


def substeps_kernel(scalars, masks, state, winds, halo, strip0, from_left, from_right,
                    state_out, fluxes, boundary, rounded,
                    cells0, cells1, cells2, cells3, strips0, strips1, strips2, strips3,
                    inner0, inner1, inner2, inner3, wind_strips, left, right):
    cells = (cells0, cells1, cells2, cells3)
    strips = (strips0, strips1, strips2, strips3)
    inner = (inner0, inner1, inner2, inner3)
    upper = sub_ids() < 4
    is_ocean = scalars[0] != 0.0
    n = ROWS + 8
    own = slice(BASE, BASE + ROWS)
    high, low = slice(BASE - 8, BASE), slice(BASE + ROWS, BASE + ROWS + 8)

    def lanes(rows):
        return lax.broadcasted_iota(jnp.int32, (rows, COLS), 1)

    row_one, side_one, rate = masks[0], masks[1], masks[2]
    rate_low = rate * row_one
    left[...] = from_left[...].astype(F32)
    right[...] = from_right[...].astype(F32)
    first = (lane_ids() & 7) < 4
    for t in range(TILES + 1):
        r = slice(8 * t, 8 * t + 8)
        a, b = left[r], right[r]
        x = jnp.where(first, a + pltpu.roll(a, COLS - 4, 1), b + pltpu.roll(b, 4, 1)) * side_one
        if t < TILES:
            strips0[BASE + 8 * t : BASE + 8 * t + 8] = x
        else:
            strips0[high] = x
            strips0[low] = x
        a, b = left[n + 8 * t : n + 8 * t + 8], right[n + 8 * t : n + 8 * t + 8]
        wind_strips[0, r] = jnp.where(first, a, b) * side_one
        wind_strips[1, r] = jnp.where(first, pltpu.roll(a, COLS - 4, 1), pltpu.roll(b, 4, 1)) * side_one
        inner0[r] = strip0[r]

    def copy_level(l, carry):
        h = pl.multiple_of(8 * l, 8)
        cells0[l, own] = state[l]
        x = halo[0, pl.ds(h, 8), :]
        cells0[l, high] = x
        cells0[l, low] = x
        return carry

    lax.fori_loop(0, LEVELS, copy_level, 0, unroll=2)

    def halo_rows(load):
        d, u = BASE + ROWS, BASE - 8
        return (
            load(d),
            jnp.where(upper, load(d - 1), load(u - 1)),
            jnp.where(upper, load(d + 1), load(u + 1)),
        )

    def beside(s, west_lane, west, east_lane, east):
        return (
            pltpu.roll(jnp.where(west_lane, west, s), 1, 1),
            pltpu.roll(jnp.where(east_lane, east, s), COLS - 1, 1),
        )

    lane = lanes(BLOCK)
    lane8 = lane_ids()
    place = lane8 & 7

    for step in range(STEPS):
        last = step == SUBSTEPS - 1
        src, strip, edge = cells[step], strips[step], inner[step]
        if not last:
            dst, strip_next, edge_next = cells[step + 1], strips[step + 1], inner[step + 1]
            for t in range(TILES + 1):
                r = BASE + 8 * t
                if t < TILES:
                    s, no, so = strip[r : r + 8], strip[r - 1 : r + 7], strip[r + 1 : r + 9]
                else:
                    s, no, so = halo_rows(lambda r: strip[r : r + 8])
                k = slice(8 * t, 8 * t + 8)
                w, e = beside(s, place == 3, edge[k], place == 4, edge[k])
                d = rate if t < TILES else rate_low
                x = stencil(s, no, so, w, e, wind_strips[0, k], wind_strips[1, k], d, 1.0 - 4.0 * d)
                if t < TILES:
                    strip_next[r : r + 8] = x
                else:
                    strip_next[high] = x
                    strip_next[low] = x

        def level(l, carry):
            h = pl.multiple_of(8 * l, 8)
            d = scalars[1 + l]
            c = 1.0 - 4.0 * d
            turn = COLS - 4 - 8 * l
            mine = (lane >> 3) == l
            for t in range(ROWS // BLOCK):
                k = slice(BLOCK * t, BLOCK * (t + 1))
                r = BASE + BLOCK * t
                s = src[l, r : r + BLOCK, :]
                side = pltpu.roll(strip[r : r + BLOCK], turn, 1)
                w, e = beside(s, lane == COLS - 1, side, lane == 0, side)
                x = stencil(s, src[l, r - 1 : r + BLOCK - 1, :], src[l, r + 1 : r + BLOCK + 1, :],
                            w, e, winds[0, l, k, :], winds[1, l, k, :], d, c)
                if last:
                    state_out[l, k, :] = x
                else:
                    dst[l, r : r + BLOCK, :] = x
                    edge_next[k] = jnp.where(mine, pltpu.roll(x, 8 * l + 4, 1), edge_next[k])
            if last:
                return carry
            s, no, so = halo_rows(lambda r: src[l, r : r + 8, :])
            side = pltpu.roll(strip[low], turn, 1)
            w, e = beside(s, lane8 == COLS - 1, side, lane8 == 0, side)
            d = d * row_one
            y = stencil(s, no, so, w, e, halo[1, pl.ds(h, 8), :], halo[2, pl.ds(h, 8), :], d, 1.0 - 4.0 * d)
            edge_next[ROWS:n] = jnp.where(mine[0:8], pltpu.roll(y, 8 * l + 4, 1), edge_next[ROWS:n])
            dst[l, high, :] = y
            dst[l, low, :] = y
            return carry

        lax.fori_loop(0, LEVELS, level, 0, unroll=UNROLL)

    def flux(t, carry):
        r = pl.multiple_of(FLUX_ROWS * t, FLUX_ROWS)
        at = pl.ds(BASE + r, FLUX_ROWS)
        out = pl.ds(r, FLUX_ROWS)
        sums = [None] * FIELDS
        for l in range(LEVELS):
            x = (cells1[l, at, :] + cells2[l, at, :]) + (cells3[l, at, :] + state_out[l, out, :])
            for f in range(FIELDS):
                term = scalars[1 + LEVELS + f * LEVELS + l] * x
                sums[f] = term if l == 0 else sums[f] + term
        for f in range(FIELDS):
            mean = sums[f] * (1.0 / SUBSTEPS)
            fluxes[f, out, :] = mean
            rounded[pl.ds(pl.multiple_of(f * ROWS + r, FLUX_ROWS), FLUX_ROWS), :] = mean.astype(BF16)
            if f == 0:
                boundary[out, :] = jnp.where(is_ocean, state_out[0, out, :], mean)
        return carry

    if FLUX_ON:
        lax.fori_loop(0, ROWS // FLUX_ROWS, flux, 0)


def remap_kernel(table, heat, gathered, weights, flux_in, boundary_in,
                 flux_out, boundary_out, patches, remapped, surface, fetch_sem, flux_sems, surface_sems):
    @pl.when(table[0] == 1)
    def _():
        fetch = pltpu.make_async_copy(boundary_in, surface, fetch_sem.at[0])
        fetch.start()
        size = FIELDS * ROWS
        patches[...] = gathered[0 : 3 * size].astype(F32)
        fetch.wait()

        def sends(i):
            at = pl.ds(pl.multiple_of(i * CHUNK, CHUNK), CHUNK)
            return (
                pltpu.make_async_copy(remapped.at[:, at], flux_out.at[:, at], flux_sems.at[i]),
                pltpu.make_async_copy(surface.at[at], boundary_out.at[at], surface_sems.at[i]),
            )

        def chunk(i, carry):
            at = pl.ds(pl.multiple_of(i * CHUNK, CHUNK), CHUNK)
            for j in range(CHUNK):
                o = i * CHUNK + j
                picked, chosen = [], []
                for entry in range(INTERSECTIONS):
                    at_entry = 1 + ROWS + 2 * ROWS * entry + o
                    start = table[at_entry]
                    picked.append(patches[pl.ds(start, FIELDS, stride=ROWS), :].astype(BF16))
                    chosen.append(weights[table[at_entry + ROWS]])
                total = lax.dot_general(
                    jnp.concatenate(picked, 1),
                    jnp.concatenate(chosen, 1),
                    (((1,), (1,)), ((), ())),
                    preferred_element_type=F32,
                )
                remapped[:, o, :] = total * table[1 + o].astype(F32)
            warmth = surface[at, :]
            for f in range(FIELDS):
                warmth = warmth + heat[f : f + 1] * remapped[f, at, :]
            surface[at, :] = warmth
            for send in sends(i):
                send.start()
            return carry

        lax.fori_loop(0, ROWS // CHUNK, chunk, 0)
        for i in range(ROWS // CHUNK):
            for send in sends(i):
                send.wait()


LIMIT = pltpu.CompilerParams(vmem_limit_bytes=16 * 2**20)
N = ROWS + 8
SHEET = jax.ShapeDtypeStruct((2 * LEVELS * 8, COLS), BF16)
COLUMNS = jax.ShapeDtypeStruct((2 * N, COLS), BF16)


def f32(*shape):
    return jax.ShapeDtypeStruct(shape, F32)


def edge_rows(state, winds):
    return pl.pallas_call(
        edge_rows_kernel,
        in_specs=[HBM, HBM],
        out_specs=[VMEM, VMEM],
        out_shape=[SHEET, SHEET],
        scratch_shapes=[
            *[pltpu.VMEM((LEVELS, 8, COLS), F32)] * 2,
            *[pltpu.VMEM((2, LEVELS, 8, COLS), F32)] * 2,
            *[pltpu.VMEM(SHEET.shape, F32)] * 2,
            pltpu.SemaphoreType.DMA((4,)),
        ],
        compiler_params=LIMIT,
        name="edge_rows",
    )(state, winds)


def own_strips(state, winds):
    return pl.pallas_call(
        own_strips_kernel,
        in_specs=[VMEM, VMEM],
        out_specs=VMEM,
        out_shape=f32(3, ROWS, COLS),
        compiler_params=LIMIT,
        name="own_strips",
    )(state, winds)


def edge_columns(masks, from_below, from_above, own):
    return pl.pallas_call(
        edge_columns_kernel,
        in_specs=[VMEM] * 4,
        out_specs=[VMEM] * 4,
        out_shape=[f32(3, LEVELS * 8, COLS), f32(N, COLS), COLUMNS, COLUMNS],
        scratch_shapes=[
            pltpu.VMEM(SHEET.shape, F32),
            pltpu.VMEM(SHEET.shape, F32),
            pltpu.VMEM((3, N, COLS), F32),
            pltpu.VMEM((2 * N, COLS), F32),
            pltpu.VMEM((2 * N, COLS), F32),
        ],
        compiler_params=LIMIT,
        name="edge_columns",
    )(masks, from_below, from_above, own)


def substeps(scalars, masks, state, winds, halo, strip0, from_left, from_right):
    return pl.pallas_call(
        substeps_kernel,
        in_specs=[SMEM] + [VMEM] * 7,
        out_specs=[VMEM] * 4,
        out_shape=[
            f32(LEVELS, ROWS, COLS),
            f32(FIELDS, ROWS, COLS),
            f32(ROWS, COLS),
            jax.ShapeDtypeStruct((FIELDS * ROWS, COLS), BF16),
        ],
        scratch_shapes=[
            *[pltpu.VMEM((LEVELS, DEEP, COLS), F32)] * 4,
            *[pltpu.VMEM((DEEP, COLS), F32)] * 4,
            *[pltpu.VMEM((N, COLS), F32)] * 4,
            pltpu.VMEM((2, N, COLS), F32),
            pltpu.VMEM((2 * N, COLS), F32),
            pltpu.VMEM((2 * N, COLS), F32),
        ],
        compiler_params=LIMIT,
        name="substeps",
    )(scalars, masks, state, winds, halo, strip0, from_left, from_right)


def remap(table, heat, gathered, weights, fluxes, boundary):
    return pl.pallas_call(
        remap_kernel,
        in_specs=[SMEM] + [VMEM] * 3 + [ANY] * 2,
        out_specs=[ANY] * 2,
        out_shape=[f32(FIELDS, ROWS, COLS), f32(ROWS, COLS)],
        input_output_aliases={4: 0, 5: 1},
        scratch_shapes=[
            pltpu.VMEM((3 * FIELDS * ROWS, COLS), F32),
            pltpu.VMEM((FIELDS, ROWS, COLS), F32),
            pltpu.VMEM((ROWS, COLS), F32),
            pltpu.SemaphoreType.DMA((1,)),
            pltpu.SemaphoreType.DMA((ROWS // CHUNK,)),
            pltpu.SemaphoreType.DMA((ROWS // CHUNK,)),
        ],
        compiler_params=LIMIT,
        name="remap",
    )(table, heat, gathered, weights, fluxes, boundary)


def body(
    state, winds, diffusivity, coupling, heat_coef, remap_blocks, source_patch, block_ids, land_sea
):
    group = lax.axis_index("grp")
    row_tile = lax.axis_index("gx")
    column_tile = lax.axis_index("gy")
    tiles_x = lax.axis_size("gx")
    tiles_y = lax.axis_size("gy")
    groups = lax.axis_size("grp")
    ocean = group == groups - 1
    line = group * tiles_x + row_tile
    top = (line == 0) | (ocean & (row_tile == 0))
    bottom = (row_tile == tiles_x - 1) & (group >= groups - 2)
    row = lax.broadcasted_iota(jnp.int32, (8, COLS), 0)
    lane = lax.broadcasted_iota(jnp.int32, (8, COLS), 1)
    row_one = jnp.where(row < 4, ~bottom, ~top).astype(F32)
    side_one = jnp.where((lane & 7) < 4, column_tile > 0, column_tile < tiles_y - 1).astype(F32)
    own_rate = jnp.where(ocean, diffusivity[1], diffusivity[0])
    rate = jnp.broadcast_to(own_rate[:, None], (LEVELS, 8)).reshape(1, COLS) * side_one
    masks = jnp.stack([row_one, side_one, rate])
    scalars = jnp.concatenate([ocean.astype(F32)[None], own_rate, coupling.reshape(-1)])
    source = source_patch[0, 0].T
    starts = (source // ROWS) * (FIELDS * ROWS) + source % ROWS
    table = jnp.concatenate([
        ocean.astype(jnp.int32)[None],
        land_sea.reshape(-1),
        jnp.concatenate([starts, block_ids[0, 0].T], 1).reshape(-1),
    ])
    heat = jnp.broadcast_to(heat_coef[:, None], (FIELDS, COLS))

    def ring(x, axis, shift):
        count = lax.axis_size(axis)
        return lax.ppermute(x, axis, [(i, (i + shift) % count) for i in range(count)])

    to_up, to_down = edge_rows(state, winds)
    from_below = ring(to_up, ("grp", "gx"), -1)
    from_above = ring(to_down, ("grp", "gx"), 1)
    own = own_strips(state, winds)
    halo, strip0, to_right, to_left = edge_columns(masks, from_below, from_above, own)
    from_left = ring(to_right, "gy", 1)
    from_right = ring(to_left, "gy", -1)
    state_out, fluxes, boundary, rounded = substeps(
        scalars, masks, state, winds, halo, strip0, from_left, from_right
    )
    gathered = lax.all_gather(rounded, "grp", axis=0, tiled=True)
    fluxes, boundary = remap(table, heat, gathered, remap_blocks, fluxes, boundary)
    return state_out, boundary, fluxes


def solution(mesh):
    return jax.shard_map(
        body,
        mesh=mesh,
        in_specs=(
            P(None, ("grp", "gx"), "gy"),
            P(None, None, ("grp", "gx"), "gy"),
            P(),
            P(),
            P(),
            P(),
            P("gx", "gy", None, None),
            P("gx", "gy", None, None),
            P("gx", "gy", None),
        ),
        out_specs=(
            P(None, ("grp", "gx"), "gy"),
            P(("grp", "gx"), "gy"),
            P(None, ("grp", "gx"), "gy"),
        ),
        check_vma=False,
    )
```

time: 160 us -> 43.4 us (0.27)
  the two profiles are of different devices: /device:TPU:79 before, /device:TPU:5 now
where the time goes in v2:
time: 43.4 us; the launch traced here: 43.1 us
  Pallas kernels  13.8 us (32%)
  blocking collectives  9.95 us (23%)
  starting transfers between devices  9.71 us (22%)
  waiting for transfers between devices  4.81 us (11%)
  local copies, waits for them, and re-layouts  3.72 us (9%)
  between operations  0.8 us (2%)
    all_gather x1, blocking collectives, body(): gathered = lax.all_gather(rounded, 'grp', axis=0, tiled=True)  9.95 us
    ppermute x4, starting transfers between devices, ring(): lax.ppermute(x, axis, [(i, (i + shift) % count) for i in range(count)])  9.71 us
    pallas_call x1, Pallas kernels, substeps(): pl.pallas_call(substeps_kernel, in_specs=[SMEM] + [VMEM] * 7, out_specs=[...  6.52 us
    pallas_call x1, Pallas kernels, remap(): pl.pallas_call(remap_kernel, in_specs=[SMEM] + [VMEM] * 3 + [ANY] * 2, ou...  6.04 us
    ppermute x4, waiting for transfers between devices, ring(): lax.ppermute(x, axis, [(i, (i + shift) % count) for i in range(count)])  4.81 us
    unnamed x25, local copies, waits for them, and re-layouts  3.34 us
    pallas_call x1, Pallas kernels, own_strips(): pl.pallas_call(own_strips_kernel, in_specs=[VMEM, VMEM], out_specs=VMEM,...  0.95 us
  transfers between devices with their start and end apart: 4, of which 2 were waited for; matrix products, arithmetic and copies ran while one was open for 1% of the time, Pallas kernels for 2%

profile of v2, /device:TPU:5, one launch (start us, length us, event | category | flops | bytes accessed | tf_op | source)
XLA Modules:
  0.0 43.1 jit_solution(788148626138436026)
XLA Ops:
  0.6 0.0 copy-start
  0.6 1.2 %copy-done = f32[2,16,64,128]{3,2,1,0:T(8,128)S(1)} copy-done((f32[2,16,64,128]{3,2,1,0:T(8,128)S(1)}, f32[2,16,64,128]{3,2,1,0:T(8,128)}, u32[]{:S(2)}) %copy-start) | copy-done | bytes 1048600
  1.9 0.0 copy-start.2
  1.9 1.0 %copy-done.2 = f32[16,64,128]{2,1,0:T(8,128)S(1)} copy-done((f32[16,64,128]{2,1,0:T(8,128)S(1)}, f32[16,64,128]{2,1,0:T(8,128)}, u32[]{:S(2)}) %copy-start.2) | copy-done | bytes 524312
  2.9 0.0 copy-start.1
  2.9 0.0 copy-start.9
  2.9 0.0 copy-start.6
  2.9 0.0 copy-start.7
  2.9 0.0 copy-start.8
  2.9 0.0 copy-start.10
  2.9 0.0 copy-start.4
  2.9 0.1 edge_rows.1
  3.1 6.9 %collective-permute-start = (bf16[256,128]{1,0:T(8,128)(2,1)S(1)}, bf16[256,128]{1,0:T(8,128)(2,1)S(1)}, u32[]{:S(2)}, u32[]{:S(2)}) collective-permute-start(bf16[256,128]{1,0:T(8,128)(2,1)S(1)} %get-tuple-element.15), channel_id=1, source_target_pairs={{0,252},{4,0},{8,4},{12,8},{16,12},{20,16},{24,20},{28,24},{32,28}... | collective-permute-start | bytes 196616 | tf_op jit(solution)/shard_map/ppermute | solution.py:449
  9.9 0.0 collective-permute-start.1
  9.9 0.0 copy-done.1
  9.9 0.0 copy-start.3
  9.9 1.0 %copy-done.3 = f32[16,64,128]{2,1,0:T(8,128)S(1)} copy-done((f32[16,64,128]{2,1,0:T(8,128)S(1)}, f32[16,64,128]{2,1,0:T(8,128)}, u32[]{:S(2)}) %copy-start.3) | copy-done | bytes 524312
  11.0 0.0 copy-start.11
  11.0 0.9 %own_strips.1.own = f32[3,64,128]{2,1,0:T(8,128)S(1)} custom-call(f32[16,64,128]{2,1,0:T(8,128)S(1)} %copy-done.3, f32[2,16,64,128]{3,2,1,0:T(8,128)S(1)} %copy-done.1), custom_call_target="tpu_custom_call" | custom-call | tf_op jit(solution)/shard_map/own_strips/pallas_call | solution.py:345
  12.0 0.0 copy-done.9
  12.0 0.0 copy-done.6
  12.0 0.1 reshape.85
  12.1 0.0 copy-done.7
  12.1 0.0 copy-done.8
  12.1 0.1 broadcast_in_dim.42
  12.2 0.1 mul.20
  12.3 0.0 copy-start.5
  12.3 0.1 add_bitcast_fusion
  12.4 0.1 iota.15
  12.5 0.0 copy-done.10
  12.5 0.1 pad_add_fusion.table
  12.6 0.0 collective-permute-done.from_below
  12.6 3.6 %collective-permute-done.1.from_above = bf16[256,128]{1,0:T(8,128)(2,1)S(1)} collective-permute-done((bf16[256,128]{1,0:T(8,128)(2,1)S(1)}, bf16[256,128]{1,0:T(8,128)(2,1)S(1)}, u32[]{:S(2)}, u32[]{:S(2)}) %collective-permute-start.1) | collective-permute-done | bytes 65568 | tf_op jit(solution)/shard_map/ppermute | solution.py:449
  16.2 0.2 edge_columns.1
  16.4 1.3 %collective-permute-start.2 = (bf16[144,128]{1,0:T(8,128)(2,1)S(1)}, bf16[144,128]{1,0:T(8,128)(2,1)S(1)}, u32[]{:S(2)}, u32[]{:S(2)}) collective-permute-start(bf16[144,128]{1,0:T(8,128)(2,1)S(1)} %get-tuple-element.19), channel_id=1, source_target_pairs={{0,1},{1,2},{2,3},{3,0},{4,5},{5,6},{6,7},{7,4},{8,9},{9,10},{10,1... | collective-permute-start | bytes 110600 | tf_op jit(solution)/shard_map/ppermute | solution.py:449
  17.7 1.5 %collective-permute-start.3 = (bf16[144,128]{1,0:T(8,128)(2,1)S(1)}, bf16[144,128]{1,0:T(8,128)(2,1)S(1)}, u32[]{:S(2)}, u32[]{:S(2)}) collective-permute-start(bf16[144,128]{1,0:T(8,128)(2,1)S(1)} %get-tuple-element.20), channel_id=1, source_target_pairs={{0,3},{1,0},{2,1},{3,2},{4,7},{5,4},{6,5},{7,6},{8,11},{9,8},{10,9... | collective-permute-start | bytes 110600 | tf_op jit(solution)/shard_map/ppermute | solution.py:449
  19.2 0.1 pad_maximum_fusion.1.scalars
  19.3 1.2 %collective-permute-done.2.from_left = bf16[144,128]{1,0:T(8,128)(2,1)S(1)} collective-permute-done((bf16[144,128]{1,0:T(8,128)(2,1)S(1)}, bf16[144,128]{1,0:T(8,128)(2,1)S(1)}, u32[]{:S(2)}, u32[]{:S(2)}) %collective-permute-start.2) | collective-permute-done | bytes 36896 | tf_op jit(solution)/shard_map/ppermute | solution.py:449
  20.5 0.0 collective-permute-done.3.from_right
  20.5 0.0 copy-done.4
  20.5 6.5 %substeps.1 = (f32[16,64,128]{2,1,0:T(8,128)}, f32[8,64,128]{2,1,0:T(8,128)}, f32[64,128]{1,0:T(8,128)}, bf16[512,128]{1,0:T(8,128)(2,1)S(1)}) custom-call(f32[145]{0:T(256)S(1)} %pad_maximum_fusion.1.scalars, f32[3,8,128]{2,1,0:T(8,128)S(1)} %pad_maximum_fusion.masks, f32[16,64,128]{2,1,0:T(8,128)S(1)} %copy-done.4, f32[2,16,64,128]{3,2,1,0:T(8,128)S(1)} %copy-done.1, ...), custom_call_target="tpu_custom_call" | custom-call | tf_op jit(solution)/shard_map/substeps/pallas_call | solution.py:374
  27.0 10.0 %all_gather.3.gathered = bf16[2048,128]{1,0:T(8,128)(2,1)S(1)} all-gather(bf16[512,128]{1,0:T(8,128)(2,1)S(1)} %get-tuple-element.22), channel_id=1, replica_groups=mesh['grp'=4,'gx'=16,'gy'=4] {'grp'}, dimensions={0}, use_global_device_ids=true | all-gather | bytes 655360 | tf_op jit(solution)/shard_map/all_gather | solution.py:461
  37.0 0.0 copy-done.11
  37.0 0.1 broadcast_in_dim.44.heat
  37.0 0.0 copy-done.5
  37.0 6.0 %remap.1 = (f32[8,64,128]{2,1,0:T(8,128)}, f32[64,128]{1,0:T(8,128)}) custom-call(s32[833]{0:T(1024)S(1)} %pad_add_fusion.table, f32[8,128]{1,0:T(8,128)S(1)} %broadcast_in_dim.44.heat, bf16[2048,128]{1,0:T(8,128)(2,1)S(1)} %all_gather.3.gathered, bf16[64,128,128]{2,1,0:T(8,128)(2,1)S(1)} %copy-done.5, ...), custom_call_target="tpu_custom_call", output_to_operand_aliasing={{0}: (4, {}), {1}: (5, {})} | custom-call | tf_op jit(solution)/shard_map/remap/pallas_call | solution.py:398
  (8 shorter events, 0.0 us)
Async XLA Ops:
  0.6 1.2 %copy-start = (f32[2,16,64,128]{3,2,1,0:T(8,128)S(1)}, f32[2,16,64,128]{3,2,1,0:T(8,128)}, u32[]{:S(2)}) copy-start(f32[2,16,64,128]{3,2,1,0:T(8,128)} %winds.5) | copy-start | bytes 3145732
  1.9 1.0 %copy-start.2 = (f32[16,64,128]{2,1,0:T(8,128)S(1)}, f32[16,64,128]{2,1,0:T(8,128)}, u32[]{:S(2)}) copy-start(f32[16,64,128]{2,1,0:T(8,128)} %state.5) | copy-start | bytes 1572868
  2.9 7.0 %copy-start.1 = (f32[2,16,64,128]{3,2,1,0:T(8,128)S(1)}, f32[2,16,64,128]{3,2,1,0:T(8,128)}, u32[]{:S(2)}) copy-start(f32[2,16,64,128]{3,2,1,0:T(8,128)} %winds.5) | copy-start | bytes 3145732
  2.9 9.1 %copy-start.9 = (f32[2,16]{1,0:T(2,128)S(1)}, f32[2,16]{1,0:T(2,128)}, u32[]{:S(2)}) copy-start(f32[2,16]{1,0:T(2,128)} %param.11) | copy-start | bytes 388
  2.9 9.1 %copy-start.6 = (f32[8,16]{1,0:T(8,128)S(1)}, f32[8,16]{1,0:T(8,128)}, u32[]{:S(2)}) copy-start(f32[8,16]{1,0:T(8,128)} %param.12) | copy-start | bytes 1540
  2.9 9.2 %copy-start.7 = (s32[1,1,64,6]{2,1,3,0:T(1,128)S(1)}, s32[1,1,64,6]{2,1,3,0:T(1,128)}, u32[]{:S(2)}) copy-start(s32[1,1,64,6]{2,1,3,0:T(1,128)} %param.15) | copy-start | bytes 4612
  2.9 9.2 %copy-start.8 = (s32[1,1,64,6]{2,1,3,0:T(1,128)S(1)}, s32[1,1,64,6]{2,1,3,0:T(1,128)}, u32[]{:S(2)}) copy-start(s32[1,1,64,6]{2,1,3,0:T(1,128)} %param.16) | copy-start | bytes 4612
  2.9 9.6 %copy-start.10 = (s32[1,1,64]{2,1,0:T(1,128)S(1)}, s32[1,1,64]{2,1,0:T(1,128)}, u32[]{:S(2)}) copy-start(s32[1,1,64]{2,1,0:T(1,128)} %param.17) | copy-start | bytes 772
  2.9 17.6 %copy-start.4 = (f32[16,64,128]{2,1,0:T(8,128)S(1)}, f32[16,64,128]{2,1,0:T(8,128)}, u32[]{:S(2)}) copy-start(f32[16,64,128]{2,1,0:T(8,128)} %state.5) | copy-start | bytes 1572868
  3.1 9.5 %collective-permute-start = (bf16[256,128]{1,0:T(8,128)(2,1)S(1)}, bf16[256,128]{1,0:T(8,128)(2,1)S(1)}, u32[]{:S(2)}, u32[]{:S(2)}) collective-permute-start(bf16[256,128]{1,0:T(8,128)(2,1)S(1)} %get-tuple-element.15), channel_id=1, source_target_pairs={{0,252},{4,0},{8,4},{12,8},{16,12},{20,16},{24,20},{28,24},{32,28}... | collective-permute-start | bytes 196616 | tf_op jit(solution)/shard_map/ppermute | solution.py:449
  9.9 6.2 %collective-permute-start.1 = (bf16[256,128]{1,0:T(8,128)(2,1)S(1)}, bf16[256,128]{1,0:T(8,128)(2,1)S(1)}, u32[]{:S(2)}, u32[]{:S(2)}) collective-permute-start(bf16[256,128]{1,0:T(8,128)(2,1)S(1)} %get-tuple-element.16), channel_id=1, source_target_pairs={{0,4},{4,8},{8,12},{12,16},{16,20},{20,24},{24,28},{28,32},{32,36}... | collective-permute-start | bytes 196616 | tf_op jit(solution)/shard_map/ppermute | solution.py:449
  9.9 1.0 %copy-start.3 = (f32[16,64,128]{2,1,0:T(8,128)S(1)}, f32[16,64,128]{2,1,0:T(8,128)}, u32[]{:S(2)}) copy-start(f32[16,64,128]{2,1,0:T(8,128)} %state.5) | copy-start | bytes 1572868
  11.0 26.0 %copy-start.11 = (f32[8]{0:T(128)S(1)}, f32[8]{0:T(128)}, u32[]{:S(2)}) copy-start(f32[8]{0:T(128)} %param.13) | copy-start | bytes 100
  12.3 24.8 %copy-start.5 = (bf16[64,128,128]{2,1,0:T(8,128)(2,1)S(1)}, bf16[64,128,128]{2,1,0:T(8,128)(2,1)}, u32[]{:S(2)}) copy-start(bf16[64,128,128]{2,1,0:T(8,128)(2,1)} %weights.1) | copy-start | bytes 6291460
  16.4 4.1 %collective-permute-start.2 = (bf16[144,128]{1,0:T(8,128)(2,1)S(1)}, bf16[144,128]{1,0:T(8,128)(2,1)S(1)}, u32[]{:S(2)}, u32[]{:S(2)}) collective-permute-start(bf16[144,128]{1,0:T(8,128)(2,1)S(1)} %get-tuple-element.19), channel_id=1, source_target_pairs={{0,1},{1,2},{2,3},{3,0},{4,5},{5,6},{6,7},{7,4},{8,9},{9,10},{10,1... | collective-permute-start | bytes 110600 | tf_op jit(solution)/shard_map/ppermute | solution.py:449
  17.7 2.8 %collective-permute-start.3 = (bf16[144,128]{1,0:T(8,128)(2,1)S(1)}, bf16[144,128]{1,0:T(8,128)(2,1)S(1)}, u32[]{:S(2)}, u32[]{:S(2)}) collective-permute-start(bf16[144,128]{1,0:T(8,128)(2,1)S(1)} %get-tuple-element.20), channel_id=1, source_target_pairs={{0,3},{1,0},{2,1},{3,2},{4,7},{5,4},{6,5},{7,6},{8,11},{9,8},{10,9... | collective-permute-start | bytes 110600 | tf_op jit(solution)/shard_map/ppermute | solution.py:449

commit v3 on v2

--- a/solution.py
+++ b/solution.py
@@ -17,9 +17,8 @@
 UNROLL = 4
 BLOCK = 8
 FLUX_ROWS = 32
-FLUX_ON = True
 STEPS = 4
-CHUNK = 16
+CHUNK = 32
 F32 = jnp.float32
 BF16 = jnp.bfloat16
 
@@ -106,7 +105,7 @@
             parts[c] = packed(parts[c], x, l)
     for c in range(3):
         full[c, ROWS : ROWS + 8] = parts[c]
-    strip0[...] = full[0]
+    strip0[...] = full[...]
     first = (lane_ids() & 7) < 4
     n = ROWS + 8
     for t in range(TILES + 1):
@@ -127,40 +126,69 @@
     return c * s + d * ((n + so) + (w + e)) - 0.5 * drift
 
 
-def substeps_kernel(scalars, masks, state, winds, halo, strip0, from_left, from_right,
-                    state_out, fluxes, boundary, rounded,
-                    cells0, cells1, cells2, cells3, strips0, strips1, strips2, strips3,
-                    inner0, inner1, inner2, inner3, wind_strips, left, right):
+def substeps_kernel(rates, weights, masks, state, winds, halo, strip0, from_left, from_right,
+                    state_out, fluxes, rounded, top,
+                    cells0, cells1, cells2, cells3, ready,
+                    lefts, rights, sides, left_winds, right_winds, left, right, sems):
     cells = (cells0, cells1, cells2, cells3)
-    strips = (strips0, strips1, strips2, strips3)
-    inner = (inner0, inner1, inner2, inner3)
     upper = sub_ids() < 4
-    is_ocean = scalars[0] != 0.0
     n = ROWS + 8
     own = slice(BASE, BASE + ROWS)
     high, low = slice(BASE - 8, BASE), slice(BASE + ROWS, BASE + ROWS + 8)
-
-    def lanes(rows):
-        return lax.broadcasted_iota(jnp.int32, (rows, COLS), 1)
-
+    lane = lane_ids()
+    place = lane & 7
+    first = place < 4
     row_one, side_one, rate = masks[0], masks[1], masks[2]
-    rate_low = rate * row_one
+
+    def halo_rows(load):
+        d, u = BASE + ROWS, BASE - 8
+        return (
+            load(d),
+            jnp.where(upper, load(d - 1), load(u - 1)),
+            jnp.where(upper, load(d + 1), load(u + 1)),
+        )
+
+    def put(buf, t, x):
+        if t < TILES:
+            buf[BASE + 8 * t : BASE + 8 * t + 8] = x
+        else:
+            buf[high] = x
+            buf[low] = x
+
     left[...] = from_left[...].astype(F32)
     right[...] = from_right[...].astype(F32)
-    first = (lane_ids() & 7) < 4
     for t in range(TILES + 1):
-        r = slice(8 * t, 8 * t + 8)
+        r, q = slice(8 * t, 8 * t + 8), slice(n + 8 * t, n + 8 * t + 8)
         a, b = left[r], right[r]
-        x = jnp.where(first, a + pltpu.roll(a, COLS - 4, 1), b + pltpu.roll(b, 4, 1)) * side_one
-        if t < TILES:
-            strips0[BASE + 8 * t : BASE + 8 * t + 8] = x
-        else:
-            strips0[high] = x
-            strips0[low] = x
-        a, b = left[n + 8 * t : n + 8 * t + 8], right[n + 8 * t : n + 8 * t + 8]
-        wind_strips[0, r] = jnp.where(first, a, b) * side_one
-        wind_strips[1, r] = jnp.where(first, pltpu.roll(a, COLS - 4, 1), pltpu.roll(b, 4, 1)) * side_one
-        inner0[r] = strip0[r]
+        a = (a + pltpu.roll(a, COLS - 4, 1)) * side_one
+        b = (b + pltpu.roll(b, 4, 1)) * side_one
+        put(lefts[0], t, jnp.where(first, a, strip0[0, r]))
+        put(rights[0], t, jnp.where(first, strip0[0, r], b))
+        put(sides[0], t, jnp.where(first, a, b))
+        a, b = left[q], right[q]
+        left_winds[0, r] = jnp.where(first, a * side_one, strip0[1, r])
+        right_winds[0, r] = jnp.where(first, strip0[1, r], b * side_one)
+        a, b = pltpu.roll(a, COLS - 4, 1), pltpu.roll(b, 4, 1)
+        left_winds[1, r] = jnp.where(first, a * side_one, strip0[2, r])
+        right_winds[1, r] = jnp.where(first, strip0[2, r], b * side_one)
+    left_rate = jnp.where(first, rate * side_one, rate)
+    right_rate = jnp.where(first, rate, rate * side_one)
+    for step in range(SUBSTEPS - 1):
+        for t in range(TILES + 1):
+            r, k = BASE + 8 * t, slice(8 * t, 8 * t + 8)
+            new = []
+            for strip, wind, d in ((lefts[step], left_winds, left_rate), (rights[step], right_winds, right_rate)):
+                if t < TILES:
+                    s, no, so = strip[r : r + 8], strip[r - 1 : r + 7], strip[r + 1 : r + 9]
+                else:
+                    s, no, so = halo_rows(lambda r: strip[r : r + 8])
+                    d = d * row_one
+                w, e = pltpu.roll(s, 1, 1), pltpu.roll(s, COLS - 1, 1)
+                new.append(stencil(s, no, so, w, e, wind[0, k], wind[1, k], d, 1.0 - 4.0 * d))
+            if step < SUBSTEPS - 2:
+                put(lefts[step + 1], t, new[0])
+                put(rights[step + 1], t, new[1])
+            put(sides[step + 1], t, jnp.where(first, new[0], new[1]))
 
     def copy_level(l, carry):
         h = pl.multiple_of(8 * l, 8)
@@ -172,77 +200,51 @@
 
     lax.fori_loop(0, LEVELS, copy_level, 0, unroll=2)
 
-    def halo_rows(load):
-        d, u = BASE + ROWS, BASE - 8
+    def beside(s, side, last, first):
         return (
-            load(d),
-            jnp.where(upper, load(d - 1), load(u - 1)),
-            jnp.where(upper, load(d + 1), load(u + 1)),
+            pltpu.roll(jnp.where(last, side, s), 1, 1),
+            pltpu.roll(jnp.where(first, side, s), COLS - 1, 1),
         )
 
-    def beside(s, west_lane, west, east_lane, east):
-        return (
-            pltpu.roll(jnp.where(west_lane, west, s), 1, 1),
-            pltpu.roll(jnp.where(east_lane, east, s), COLS - 1, 1),
-        )
-
-    lane = lanes(BLOCK)
-    lane8 = lane_ids()
-    place = lane8 & 7
-
-    for step in range(STEPS):
+    wide = lax.broadcasted_iota(jnp.int32, (BLOCK, COLS), 1)
+    last_wide, first_wide = wide == COLS - 1, wide == 0
+    last_lane, first_lane = lane == COLS - 1, lane == 0
+
+    for step in range(SUBSTEPS):
         last = step == SUBSTEPS - 1
-        src, strip, edge = cells[step], strips[step], inner[step]
-        if not last:
-            dst, strip_next, edge_next = cells[step + 1], strips[step + 1], inner[step + 1]
-            for t in range(TILES + 1):
-                r = BASE + 8 * t
-                if t < TILES:
-                    s, no, so = strip[r : r + 8], strip[r - 1 : r + 7], strip[r + 1 : r + 9]
-                else:
-                    s, no, so = halo_rows(lambda r: strip[r : r + 8])
-                k = slice(8 * t, 8 * t + 8)
-                w, e = beside(s, place == 3, edge[k], place == 4, edge[k])
-                d = rate if t < TILES else rate_low
-                x = stencil(s, no, so, w, e, wind_strips[0, k], wind_strips[1, k], d, 1.0 - 4.0 * d)
-                if t < TILES:
-                    strip_next[r : r + 8] = x
-                else:
-                    strip_next[high] = x
-                    strip_next[low] = x
+        src, strip = cells[step], sides[step]
 
         def level(l, carry):
             h = pl.multiple_of(8 * l, 8)
-            d = scalars[1 + l]
+            d = rates[pl.ds(l, 1), :]
             c = 1.0 - 4.0 * d
             turn = COLS - 4 - 8 * l
-            mine = (lane >> 3) == l
             for t in range(ROWS // BLOCK):
                 k = slice(BLOCK * t, BLOCK * (t + 1))
                 r = BASE + BLOCK * t
                 s = src[l, r : r + BLOCK, :]
-                side = pltpu.roll(strip[r : r + BLOCK], turn, 1)
-                w, e = beside(s, lane == COLS - 1, side, lane == 0, side)
+                w, e = beside(s, pltpu.roll(strip[r : r + BLOCK], turn, 1), last_wide, first_wide)
                 x = stencil(s, src[l, r - 1 : r + BLOCK - 1, :], src[l, r + 1 : r + BLOCK + 1, :],
                             w, e, winds[0, l, k, :], winds[1, l, k, :], d, c)
                 if last:
-                    state_out[l, k, :] = x
+                    ready[l, k, :] = x
                 else:
-                    dst[l, r : r + BLOCK, :] = x
-                    edge_next[k] = jnp.where(mine, pltpu.roll(x, 8 * l + 4, 1), edge_next[k])
+                    cells[step + 1][l, r : r + BLOCK, :] = x
             if last:
                 return carry
             s, no, so = halo_rows(lambda r: src[l, r : r + 8, :])
-            side = pltpu.roll(strip[low], turn, 1)
-            w, e = beside(s, lane8 == COLS - 1, side, lane8 == 0, side)
+            w, e = beside(s, pltpu.roll(strip[low], turn, 1), last_lane, first_lane)
             d = d * row_one
             y = stencil(s, no, so, w, e, halo[1, pl.ds(h, 8), :], halo[2, pl.ds(h, 8), :], d, 1.0 - 4.0 * d)
-            edge_next[ROWS:n] = jnp.where(mine[0:8], pltpu.roll(y, 8 * l + 4, 1), edge_next[ROWS:n])
-            dst[l, high, :] = y
-            dst[l, low, :] = y
+            cells[step + 1][l, high, :] = y
+            cells[step + 1][l, low, :] = y
             return carry
 
-        lax.fori_loop(0, LEVELS, level, 0, unroll=UNROLL)
+        if step < STEPS:
+            lax.fori_loop(0, LEVELS, level, 0, unroll=UNROLL)
+
+    send = pltpu.make_async_copy(ready, state_out, sems.at[0])
+    send.start()
 
     def flux(t, carry):
         r = pl.multiple_of(FLUX_ROWS * t, FLUX_ROWS)
@@ -250,32 +252,41 @@
         out = pl.ds(r, FLUX_ROWS)
         sums = [None] * FIELDS
         for l in range(LEVELS):
-            x = (cells1[l, at, :] + cells2[l, at, :]) + (cells3[l, at, :] + state_out[l, out, :])
+            x = (cells1[l, at, :] + cells2[l, at, :]) + (cells3[l, at, :] + ready[l, out, :])
             for f in range(FIELDS):
-                term = scalars[1 + LEVELS + f * LEVELS + l] * x
+                k = f * LEVELS + l
+                term = weights[k : k + 1, :] * x
                 sums[f] = term if l == 0 else sums[f] + term
         for f in range(FIELDS):
             mean = sums[f] * (1.0 / SUBSTEPS)
             fluxes[f, out, :] = mean
             rounded[pl.ds(pl.multiple_of(f * ROWS + r, FLUX_ROWS), FLUX_ROWS), :] = mean.astype(BF16)
-            if f == 0:
-                boundary[out, :] = jnp.where(is_ocean, state_out[0, out, :], mean)
         return carry
 
-    if FLUX_ON:
-        lax.fori_loop(0, ROWS // FLUX_ROWS, flux, 0)
-
-
-def remap_kernel(table, heat, gathered, weights, flux_in, boundary_in,
-                 flux_out, boundary_out, patches, remapped, surface, fetch_sem, flux_sems, surface_sems):
-    @pl.when(table[0] == 1)
+    lax.fori_loop(0, ROWS // FLUX_ROWS, flux, 0)
+    top[...] = ready[0]
+    send.wait()
+
+
+def turn_blocks_kernel(blocks, turned):
+    def turn(i, carry):
+        turned[i] = blocks[i].T
+        return carry
+
+    lax.fori_loop(0, blocks.shape[0], turn, 0, unroll=8)
+
+
+def remap_kernel(words, heat, gathered, weights, fluxes, top, flux_out, boundary_out,
+                 table, patches, remapped, surface, table_sem, out_sems, flux_sems, surface_sems):
+    size = FIELDS * ROWS
+    fetch = pltpu.make_async_copy(words, table, table_sem.at[0])
+    fetch.start()
+    patches[...] = gathered[0 : 3 * size].astype(F32)
+    fetch.wait()
+    is_ocean = table[table.shape[0] - 1] == 1
+
+    @pl.when(is_ocean)
     def _():
-        fetch = pltpu.make_async_copy(boundary_in, surface, fetch_sem.at[0])
-        fetch.start()
-        size = FIELDS * ROWS
-        patches[...] = gathered[0 : 3 * size].astype(F32)
-        fetch.wait()
-
         def sends(i):
             at = pl.ds(pl.multiple_of(i * CHUNK, CHUNK), CHUNK)
             return (
@@ -289,18 +300,15 @@
                 o = i * CHUNK + j
                 picked, chosen = [], []
                 for entry in range(INTERSECTIONS):
-                    at_entry = 1 + ROWS + 2 * ROWS * entry + o
+                    at_entry = ROWS + 2 * ROWS * entry + o
                     start = table[at_entry]
                     picked.append(patches[pl.ds(start, FIELDS, stride=ROWS), :].astype(BF16))
                     chosen.append(weights[table[at_entry + ROWS]])
-                total = lax.dot_general(
-                    jnp.concatenate(picked, 1),
-                    jnp.concatenate(chosen, 1),
-                    (((1,), (1,)), ((), ())),
-                    preferred_element_type=F32,
+                total = jnp.dot(
+                    jnp.concatenate(picked, 1), jnp.concatenate(chosen, 0), preferred_element_type=F32
                 )
-                remapped[:, o, :] = total * table[1 + o].astype(F32)
-            warmth = surface[at, :]
+                remapped[:, o, :] = total * table[o].astype(F32)
+            warmth = top[at, :]
             for f in range(FIELDS):
                 warmth = warmth + heat[f : f + 1] * remapped[f, at, :]
             surface[at, :] = warmth
@@ -313,7 +321,19 @@
             for send in sends(i):
                 send.wait()
 
-
+    @pl.when(jnp.logical_not(is_ocean))
+    def _():
+        copies = (
+            pltpu.make_async_copy(fluxes, flux_out, out_sems.at[0]),
+            pltpu.make_async_copy(fluxes.at[0], boundary_out, out_sems.at[1]),
+        )
+        for copy in copies:
+            copy.start()
+        for copy in copies:
+            copy.wait()
+
+
+WIDE = pltpu.CompilerParams(vmem_limit_bytes=63 * 2**20 + 2**19)
 LIMIT = pltpu.CompilerParams(vmem_limit_bytes=16 * 2**20)
 N = ROWS + 8
 SHEET = jax.ShapeDtypeStruct((2 * LEVELS * 8, COLS), BF16)
@@ -336,7 +356,7 @@
             *[pltpu.VMEM(SHEET.shape, F32)] * 2,
             pltpu.SemaphoreType.DMA((4,)),
         ],
-        compiler_params=LIMIT,
+        compiler_params=WIDE,
         name="edge_rows",
     )(state, winds)
 
@@ -357,7 +377,7 @@
         edge_columns_kernel,
         in_specs=[VMEM] * 4,
         out_specs=[VMEM] * 4,
-        out_shape=[f32(3, LEVELS * 8, COLS), f32(N, COLS), COLUMNS, COLUMNS],
+        out_shape=[f32(3, LEVELS * 8, COLS), f32(3, N, COLS), COLUMNS, COLUMNS],
         scratch_shapes=[
             pltpu.VMEM(SHEET.shape, F32),
             pltpu.VMEM(SHEET.shape, F32),
@@ -370,48 +390,63 @@
     )(masks, from_below, from_above, own)
 
 
-def substeps(scalars, masks, state, winds, halo, strip0, from_left, from_right):
+def substeps(rates, weights, masks, state, winds, halo, strip0, from_left, from_right):
     return pl.pallas_call(
         substeps_kernel,
-        in_specs=[SMEM] + [VMEM] * 7,
-        out_specs=[VMEM] * 4,
+        in_specs=[VMEM] * 9,
+        out_specs=[ANY] + [VMEM] * 3,
         out_shape=[
             f32(LEVELS, ROWS, COLS),
             f32(FIELDS, ROWS, COLS),
+            jax.ShapeDtypeStruct((FIELDS * ROWS, COLS), BF16),
             f32(ROWS, COLS),
-            jax.ShapeDtypeStruct((FIELDS * ROWS, COLS), BF16),
         ],
         scratch_shapes=[
             *[pltpu.VMEM((LEVELS, DEEP, COLS), F32)] * 4,
-            *[pltpu.VMEM((DEEP, COLS), F32)] * 4,
-            *[pltpu.VMEM((N, COLS), F32)] * 4,
-            pltpu.VMEM((2, N, COLS), F32),
-            pltpu.VMEM((2 * N, COLS), F32),
-            pltpu.VMEM((2 * N, COLS), F32),
+            pltpu.VMEM((LEVELS, ROWS, COLS), F32),
+            [pltpu.VMEM((DEEP, COLS), F32)] * 3,
+            [pltpu.VMEM((DEEP, COLS), F32)] * 3,
+            [pltpu.VMEM((DEEP, COLS), F32)] * 4,
+            *[pltpu.VMEM((2, N, COLS), F32)] * 2,
+            *[pltpu.VMEM((2 * N, COLS), F32)] * 2,
+            pltpu.SemaphoreType.DMA((1,)),
         ],
         compiler_params=LIMIT,
         name="substeps",
-    )(scalars, masks, state, winds, halo, strip0, from_left, from_right)
-
-
-def remap(table, heat, gathered, weights, fluxes, boundary):
+    )(rates, weights, masks, state, winds, halo, strip0, from_left, from_right)
+
+
+def turn_blocks(blocks):
+    return pl.pallas_call(
+        turn_blocks_kernel,
+        in_specs=[VMEM],
+        out_specs=VMEM,
+        out_shape=jax.ShapeDtypeStruct(blocks.shape, BF16),
+        compiler_params=LIMIT,
+        name="turn_blocks",
+    )(blocks)
+
+
+def remap(table, heat, gathered, weights, fluxes, top):
+    chunks = ROWS // CHUNK
     return pl.pallas_call(
         remap_kernel,
-        in_specs=[SMEM] + [VMEM] * 3 + [ANY] * 2,
+        in_specs=[ANY] + [VMEM] * 5,
         out_specs=[ANY] * 2,
         out_shape=[f32(FIELDS, ROWS, COLS), f32(ROWS, COLS)],
-        input_output_aliases={4: 0, 5: 1},
         scratch_shapes=[
+            pltpu.SMEM(table.shape, jnp.int32),
             pltpu.VMEM((3 * FIELDS * ROWS, COLS), F32),
             pltpu.VMEM((FIELDS, ROWS, COLS), F32),
             pltpu.VMEM((ROWS, COLS), F32),
             pltpu.SemaphoreType.DMA((1,)),
-            pltpu.SemaphoreType.DMA((ROWS // CHUNK,)),
-            pltpu.SemaphoreType.DMA((ROWS // CHUNK,)),
+            pltpu.SemaphoreType.DMA((2,)),
+            pltpu.SemaphoreType.DMA((chunks,)),
+            pltpu.SemaphoreType.DMA((chunks,)),
         ],
         compiler_params=LIMIT,
         name="remap",
-    )(table, heat, gathered, weights, fluxes, boundary)
+    )(table, heat, gathered, weights, fluxes, top)
 
 
 def body(
@@ -432,15 +467,16 @@
     row_one = jnp.where(row < 4, ~bottom, ~top).astype(F32)
     side_one = jnp.where((lane & 7) < 4, column_tile > 0, column_tile < tiles_y - 1).astype(F32)
     own_rate = jnp.where(ocean, diffusivity[1], diffusivity[0])
-    rate = jnp.broadcast_to(own_rate[:, None], (LEVELS, 8)).reshape(1, COLS) * side_one
+    rate = jnp.broadcast_to(own_rate[:, None], (LEVELS, 8)).reshape(1, COLS) * jnp.ones((8, 1), F32)
     masks = jnp.stack([row_one, side_one, rate])
-    scalars = jnp.concatenate([ocean.astype(F32)[None], own_rate, coupling.reshape(-1)])
+    rates = jnp.broadcast_to(own_rate[:, None], (LEVELS, COLS))
+    weights = jnp.broadcast_to(coupling.reshape(-1, 1), (FIELDS * LEVELS, COLS))
     source = source_patch[0, 0].T
     starts = (source // ROWS) * (FIELDS * ROWS) + source % ROWS
     table = jnp.concatenate([
-        ocean.astype(jnp.int32)[None],
         land_sea.reshape(-1),
         jnp.concatenate([starts, block_ids[0, 0].T], 1).reshape(-1),
+        ocean.astype(jnp.int32)[None],
     ])
     heat = jnp.broadcast_to(heat_coef[:, None], (FIELDS, COLS))
 
@@ -455,11 +491,14 @@
     halo, strip0, to_right, to_left = edge_columns(masks, from_below, from_above, own)
     from_left = ring(to_right, "gy", 1)
     from_right = ring(to_left, "gy", -1)
-    state_out, fluxes, boundary, rounded = substeps(
-        scalars, masks, state, winds, halo, strip0, from_left, from_right
+    turned = turn_blocks(remap_blocks)
+    state_out, fluxes, rounded, top_level = substeps(
+        rates, weights, masks, state, winds, halo, strip0, from_left, from_right
     )
     gathered = lax.all_gather(rounded, "grp", axis=0, tiled=True)
-    fluxes, boundary = remap(table, heat, gathered, remap_blocks, fluxes, boundary)
+    fluxes, boundary = remap(
+        table, heat, gathered, turned, fluxes, top_level
+    )
     return state_out, boundary, fluxes
 
 

time: 43.4 us -> 39.9 us (0.919)
  waiting for transfers between devices: 4.81 us -> 2.77 us
  Pallas kernels: 13.8 us -> 12.6 us
  blocking collectives: 9.95 us -> 8.95 us
  local copies, waits for them, and re-layouts: 3.72 us -> 4.61 us
    pallas_call x2 -> x3, Pallas kernels: 12.6 us -> 9.7 us  [the longest x1 4.68 us: substeps(): pl.pallas_call(substeps_kernel, in_specs=[VMEM] * 9, out_specs=[ANY] + [V...]
    ppermute x4, waiting for transfers between devices: 4.81 us -> 2.77 us  [ring(): lax.ppermute(x, axis, [(i, (i + shift) % count) for i in range(count)])]
    pallas_call x1, Pallas kernels: 0.14 us -> 1.74 us  [edge_rows(): pl.pallas_call(edge_rows_kernel, in_specs=[HBM, HBM], out_specs=[VMEM, VM...]
    all_gather x1, blocking collectives: 9.95 us -> 8.95 us  [body(): gathered = lax.all_gather(rounded, 'grp', axis=0, tiled=True)]
    unnamed x25 -> x23, local copies, waits for them, and re-layouts: 3.34 us -> 4.09 us
  transfers between devices with their start and end apart: 4 -> 4, of which waited for: 2 -> 1; matrix products, arithmetic and copies ran while one was open for 1% -> 1% of each run, Pallas kernels for 2% -> 5%
where the time goes in v3:
time: 39.9 us; the launch traced here: 39.7 us
  Pallas kernels  12.6 us (32%)
  starting transfers between devices  9.73 us (24%)
  blocking collectives  8.95 us (22%)
  local copies, waits for them, and re-layouts  4.61 us (12%)
  waiting for transfers between devices  2.77 us (7%)
  between operations  0.84 us (2%)
    ppermute x4, starting transfers between devices, ring(): lax.ppermute(x, axis, [(i, (i + shift) % count) for i in range(count)])  9.73 us
    all_gather x1, blocking collectives, body(): gathered = lax.all_gather(rounded, 'grp', axis=0, tiled=True)  8.95 us
    pallas_call x1, Pallas kernels, substeps(): pl.pallas_call(substeps_kernel, in_specs=[VMEM] * 9, out_specs=[ANY] + [V...  4.68 us
    unnamed x23, local copies, waits for them, and re-layouts  4.09 us
    pallas_call x1, Pallas kernels, remap(): pl.pallas_call(remap_kernel, in_specs=[ANY] + [VMEM] * 5, out_specs=[ANY]...  4.05 us
    ppermute x4, waiting for transfers between devices, ring(): lax.ppermute(x, axis, [(i, (i + shift) % count) for i in range(count)])  2.77 us
    pallas_call x1, Pallas kernels, edge_rows(): pl.pallas_call(edge_rows_kernel, in_specs=[HBM, HBM], out_specs=[VMEM, VM...  1.74 us
    pallas_call x1, Pallas kernels, turn_blocks(): pl.pallas_call(turn_blocks_kernel, in_specs=[VMEM], out_specs=VMEM, out_s...  0.97 us
  transfers between devices with their start and end apart: 4, of which 1 were waited for; matrix products, arithmetic and copies ran while one was open for 1% of the time, Pallas kernels for 5%

profile of v3, /device:TPU:5, one launch (start us, length us, event | category | flops | bytes accessed | tf_op | source)
XLA Modules:
  0.0 39.7 jit_solution(13295249691963730978)
XLA Ops:
  0.6 0.0 copy-start.8
  0.6 0.0 copy-start.6
  0.7 0.0 copy-start.7
  0.7 0.0 copy-start.9
  0.7 0.0 copy-start.5
  0.7 1.7 %edge_rows.1 = (bf16[256,128]{1,0:T(8,128)(2,1)}, bf16[256,128]{1,0:T(8,128)(2,1)}) custom-call(f32[16,64,128]{2,1,0:T(8,128)} %state.5, f32[2,16,64,128]{3,2,1,0:T(8,128)} %winds.5), custom_call_target="tpu_custom_call" | custom-call | tf_op jit(solution)/shard_map/edge_rows/pallas_call | solution.py:348
  2.4 6.9 %collective-permute-start = (bf16[256,128]{1,0:T(8,128)(2,1)}, bf16[256,128]{1,0:T(8,128)(2,1)S(1)}, u32[]{:S(2)}, u32[]{:S(2)}) collective-permute-start(bf16[256,128]{1,0:T(8,128)(2,1)} %get-tuple-element.15), channel_id=1, source_target_pairs={{0,252},{4,0},{8,4},{12,8},{16,12},{20,16},{24,20},{28,24},{32,28}... | collective-permute-start | bytes 196616 | tf_op jit(solution)/shard_map/ppermute | solution.py:485
  9.3 0.0 collective-permute-start.1
  9.3 0.0 copy-start
  9.3 1.2 %copy-done = f32[2,16,64,128]{3,2,1,0:T(8,128)S(1)} copy-done((f32[2,16,64,128]{3,2,1,0:T(8,128)S(1)}, f32[2,16,64,128]{3,2,1,0:T(8,128)}, u32[]{:S(2)}) %copy-start) | copy-done | bytes 1048600
  10.5 0.0 copy-start.2
  10.5 1.0 %copy-done.2 = f32[16,64,128]{2,1,0:T(8,128)S(1)} copy-done((f32[16,64,128]{2,1,0:T(8,128)S(1)}, f32[16,64,128]{2,1,0:T(8,128)}, u32[]{:S(2)}) %copy-start.2) | copy-done | bytes 524312
  11.5 0.9 %own_strips.1.own = f32[3,64,128]{2,1,0:T(8,128)S(1)} custom-call(f32[16,64,128]{2,1,0:T(8,128)S(1)} %copy-done.2, f32[2,16,64,128]{3,2,1,0:T(8,128)S(1)} %copy-done), custom_call_target="tpu_custom_call" | custom-call | tf_op jit(solution)/shard_map/own_strips/pallas_call | solution.py:365
  12.5 0.0 copy-done.8
  12.6 0.0 copy-done.6
  12.6 0.0 copy-done.7
  12.6 0.1 broadcast_in_dim.52
  12.7 0.1 mul.15
  12.8 0.1 iota.13
  12.9 0.1 add_bitcast_fusion
  13.0 0.0 collective-permute-done.from_below
  13.0 2.8 %collective-permute-done.1.from_above = bf16[256,128]{1,0:T(8,128)(2,1)S(1)} collective-permute-done((bf16[256,128]{1,0:T(8,128)(2,1)}, bf16[256,128]{1,0:T(8,128)(2,1)S(1)}, u32[]{:S(2)}, u32[]{:S(2)}) %collective-permute-start.1) | collective-permute-done | bytes 65568 | tf_op jit(solution)/shard_map/ppermute | solution.py:485
  15.7 0.2 edge_columns.1
  15.9 1.3 %collective-permute-start.2 = (bf16[144,128]{1,0:T(8,128)(2,1)S(1)}, bf16[144,128]{1,0:T(8,128)(2,1)S(1)}, u32[]{:S(2)}, u32[]{:S(2)}) collective-permute-start(bf16[144,128]{1,0:T(8,128)(2,1)S(1)} %get-tuple-element.19), channel_id=1, source_target_pairs={{0,1},{1,2},{2,3},{3,0},{4,5},{5,6},{6,7},{7,4},{8,9},{9,10},{10,1... | collective-permute-start | bytes 110600 | tf_op jit(solution)/shard_map/ppermute | solution.py:485
  17.3 1.5 %collective-permute-start.3 = (bf16[144,128]{1,0:T(8,128)(2,1)S(1)}, bf16[144,128]{1,0:T(8,128)(2,1)S(1)}, u32[]{:S(2)}, u32[]{:S(2)}) collective-permute-start(bf16[144,128]{1,0:T(8,128)(2,1)S(1)} %get-tuple-element.20), channel_id=1, source_target_pairs={{0,3},{1,0},{2,1},{3,2},{4,7},{5,4},{6,5},{7,6},{8,11},{9,8},{10,9... | collective-permute-start | bytes 110600 | tf_op jit(solution)/shard_map/ppermute | solution.py:485
  18.8 0.0 copy-done.9
  18.8 0.1 pad_add_fusion.words
  18.9 0.0 copy-done.5
  18.9 0.1 broadcast_in_dim.46
  18.9 0.0 copy-start.4
  18.9 1.6 %copy-done.4 = bf16[64,128,128]{2,1,0:T(8,128)(2,1)S(1)} copy-done((bf16[64,128,128]{2,1,0:T(8,128)(2,1)S(1)}, bf16[64,128,128]{2,1,0:T(8,128)(2,1)}, u32[]{:S(2)}) %copy-start.4) | copy-done | bytes 2097176
  20.5 0.0 copy-start.1
  20.5 0.0 copy-start.3
  20.5 1.0 %turn_blocks.1.weights = bf16[64,128,128]{2,1,0:T(8,128)(2,1)S(1)} custom-call(bf16[64,128,128]{2,1,0:T(8,128)(2,1)S(1)} %copy-done.4), custom_call_target="tpu_custom_call" | custom-call | tf_op jit(solution)/shard_map/turn_blocks/pallas_call | solution.py:420
  21.5 0.0 copy-start.10
  21.5 0.0 collective-permute-done.2.from_left
  21.5 0.0 collective-permute-done.3.from_right
  21.6 0.1 broadcast_in_dim.45.rates
  21.6 0.1 broadcast_in_dim.47.weights
  21.7 0.1 copy-done.1
  21.8 0.1 copy-done.3
  21.9 4.7 %substeps.1 = (f32[16,64,128]{2,1,0:T(8,128)}, f32[8,64,128]{2,1,0:T(8,128)S(1)}, bf16[512,128]{1,0:T(8,128)(2,1)S(1)}, f32[64,128]{1,0:T(8,128)S(1)}) custom-call(f32[16,128]{1,0:T(8,128)S(1)} %broadcast_in_dim.45.rates, f32[128,128]{1,0:T(8,128)S(1)} %broadcast_in_dim.47.weights, f32[3,8,128]{2,1,0:T(8,128)S(1)} %pad_maximum_fusion.masks, ...), custom_call_target="tpu_custom_call" | custom-call | tf_op jit(solution)/shard_map/substeps/pallas_call | solution.py:394
  26.6 8.9 %all_gather.3.gathered = bf16[2048,128]{1,0:T(8,128)(2,1)S(1)} all-gather(bf16[512,128]{1,0:T(8,128)(2,1)S(1)} %get-tuple-element.22), channel_id=1, replica_groups=mesh['grp'=4,'gx'=16,'gy'=4] {'grp'}, dimensions={0}, use_global_device_ids=true | all-gather | bytes 655360 | tf_op jit(solution)/shard_map/all_gather | solution.py:498
  35.5 0.0 copy-done.10
  35.5 0.1 broadcast_in_dim.55.heat
  35.6 4.0 %remap.1 = (f32[8,64,128]{2,1,0:T(8,128)}, f32[64,128]{1,0:T(8,128)}) custom-call(s32[833]{0:T(1024)S(1)} %pad_add_fusion.words, f32[8,128]{1,0:T(8,128)S(1)} %broadcast_in_dim.55.heat, bf16[2048,128]{1,0:T(8,128)(2,1)S(1)} %all_gather.3.gathered, bf16[64,128,128]{2,1,0:T(8,128)(2,1)S(1)} %turn_blocks.1.weights, f32[8,64,128]{2,1,0:T(8,128)S(1)} %get-tuple-element.23.fluxes, ...), custom_call_target="tpu_custom_call" | custom-call | tf_op jit(solution)/shard_map/remap/pallas_call | solution.py:432
  (8 shorter events, 0.0 us)
Async XLA Ops:
  0.6 11.9 %copy-start.8 = (f32[2,16]{1,0:T(2,128)S(1)}, f32[2,16]{1,0:T(2,128)}, u32[]{:S(2)}) copy-start(f32[2,16]{1,0:T(2,128)} %param.11) | copy-start | bytes 388
  0.6 11.9 %copy-start.6 = (s32[1,1,64,6]{2,1,3,0:T(1,128)S(1)}, s32[1,1,64,6]{2,1,3,0:T(1,128)}, u32[]{:S(2)}) copy-start(s32[1,1,64,6]{2,1,3,0:T(1,128)} %param.15) | copy-start | bytes 4612
  0.7 11.9 %copy-start.7 = (s32[1,1,64,6]{2,1,3,0:T(1,128)S(1)}, s32[1,1,64,6]{2,1,3,0:T(1,128)}, u32[]{:S(2)}) copy-start(s32[1,1,64,6]{2,1,3,0:T(1,128)} %param.16) | copy-start | bytes 4612
  0.7 18.1 %copy-start.9 = (s32[1,1,64]{2,1,0:T(1,128)S(1)}, s32[1,1,64]{2,1,0:T(1,128)}, u32[]{:S(2)}) copy-start(s32[1,1,64]{2,1,0:T(1,128)} %param.17) | copy-start | bytes 772
  0.7 18.2 %copy-start.5 = (f32[8,16]{1,0:T(8,128)S(1)}, f32[8,16]{1,0:T(8,128)}, u32[]{:S(2)}) copy-start(f32[8,16]{1,0:T(8,128)} %param.12) | copy-start | bytes 1540
  2.4 10.5 %collective-permute-start = (bf16[256,128]{1,0:T(8,128)(2,1)}, bf16[256,128]{1,0:T(8,128)(2,1)S(1)}, u32[]{:S(2)}, u32[]{:S(2)}) collective-permute-start(bf16[256,128]{1,0:T(8,128)(2,1)} %get-tuple-element.15), channel_id=1, source_target_pairs={{0,252},{4,0},{8,4},{12,8},{16,12},{20,16},{24,20},{28,24},{32,28}... | collective-permute-start | bytes 196616 | tf_op jit(solution)/shard_map/ppermute | solution.py:485
  9.3 6.5 %collective-permute-start.1 = (bf16[256,128]{1,0:T(8,128)(2,1)}, bf16[256,128]{1,0:T(8,128)(2,1)S(1)}, u32[]{:S(2)}, u32[]{:S(2)}) collective-permute-start(bf16[256,128]{1,0:T(8,128)(2,1)} %get-tuple-element.16), channel_id=1, source_target_pairs={{0,4},{4,8},{8,12},{12,16},{16,20},{20,24},{24,28},{28,32},{32,36}... | collective-permute-start | bytes 196616 | tf_op jit(solution)/shard_map/ppermute | solution.py:485
  9.3 1.2 %copy-start = (f32[2,16,64,128]{3,2,1,0:T(8,128)S(1)}, f32[2,16,64,128]{3,2,1,0:T(8,128)}, u32[]{:S(2)}) copy-start(f32[2,16,64,128]{3,2,1,0:T(8,128)} %winds.5) | copy-start | bytes 3145732
  10.5 1.0 %copy-start.2 = (f32[16,64,128]{2,1,0:T(8,128)S(1)}, f32[16,64,128]{2,1,0:T(8,128)}, u32[]{:S(2)}) copy-start(f32[16,64,128]{2,1,0:T(8,128)} %state.5) | copy-start | bytes 1572868
  15.9 5.6 %collective-permute-start.2 = (bf16[144,128]{1,0:T(8,128)(2,1)S(1)}, bf16[144,128]{1,0:T(8,128)(2,1)S(1)}, u32[]{:S(2)}, u32[]{:S(2)}) collective-permute-start(bf16[144,128]{1,0:T(8,128)(2,1)S(1)} %get-tuple-element.19), channel_id=1, source_target_pairs={{0,1},{1,2},{2,3},{3,0},{4,5},{5,6},{6,7},{7,4},{8,9},{9,10},{10,1... | collective-permute-start | bytes 110600 | tf_op jit(solution)/shard_map/ppermute | solution.py:485
  17.3 4.3 %collective-permute-start.3 = (bf16[144,128]{1,0:T(8,128)(2,1)S(1)}, bf16[144,128]{1,0:T(8,128)(2,1)S(1)}, u32[]{:S(2)}, u32[]{:S(2)}) collective-permute-start(bf16[144,128]{1,0:T(8,128)(2,1)S(1)} %get-tuple-element.20), channel_id=1, source_target_pairs={{0,3},{1,0},{2,1},{3,2},{4,7},{5,4},{6,5},{7,6},{8,11},{9,8},{10,9... | collective-permute-start | bytes 110600 | tf_op jit(solution)/shard_map/ppermute | solution.py:485
  18.9 1.6 %copy-start.4 = (bf16[64,128,128]{2,1,0:T(8,128)(2,1)S(1)}, bf16[64,128,128]{2,1,0:T(8,128)(2,1)}, u32[]{:S(2)}) copy-start(bf16[64,128,128]{2,1,0:T(8,128)(2,1)} %blocks.1) | copy-start | bytes 6291460
  20.5 1.2 %copy-start.1 = (f32[2,16,64,128]{3,2,1,0:T(8,128)S(1)}, f32[2,16,64,128]{3,2,1,0:T(8,128)}, u32[]{:S(2)}) copy-start(f32[2,16,64,128]{3,2,1,0:T(8,128)} %winds.5) | copy-start | bytes 3145732
  20.5 1.4 %copy-start.3 = (f32[16,64,128]{2,1,0:T(8,128)S(1)}, f32[16,64,128]{2,1,0:T(8,128)}, u32[]{:S(2)}) copy-start(f32[16,64,128]{2,1,0:T(8,128)} %state.5) | copy-start | bytes 1572868
  21.5 14.0 %copy-start.10 = (f32[8]{0:T(128)S(1)}, f32[8]{0:T(128)}, u32[]{:S(2)}) copy-start(f32[8]{0:T(128)} %param.13) | copy-start | bytes 100

commit v4 on v3

--- a/solution.py
+++ b/solution.py
@@ -17,7 +17,6 @@
 UNROLL = 4
 BLOCK = 8
 FLUX_ROWS = 32
-STEPS = 4
 CHUNK = 32
 F32 = jnp.float32
 BF16 = jnp.bfloat16
@@ -126,11 +125,58 @@
     return c * s + d * ((n + so) + (w + e)) - 0.5 * drift
 
 
-def substeps_kernel(rates, weights, masks, state, winds, halo, strip0, from_left, from_right,
+def first_step_kernel(rates, masks, state, winds, halo, partial, cells):
+    own = slice(BASE, BASE + ROWS)
+    high, low = slice(BASE - 8, BASE), slice(BASE + ROWS, BASE + ROWS + 8)
+    upper = sub_ids() < 4
+    lane = lane_ids()
+    row_one = masks[0]
+
+    def copy_level(l, carry):
+        h = pl.multiple_of(8 * l, 8)
+        cells[l, own] = state[l]
+        x = halo[0, pl.ds(h, 8), :]
+        cells[l, high] = x
+        cells[l, low] = x
+        return carry
+
+    lax.fori_loop(0, LEVELS, copy_level, 0, unroll=2)
+
+    def level(l, carry):
+        h = pl.multiple_of(8 * l, 8)
+        d = rates[pl.ds(l, 1), :]
+        for t in range(TILES + 1):
+            k = slice(8 * t, 8 * t + 8)
+            r = BASE + 8 * t
+            if t < TILES:
+                s, no, so = cells[l, r : r + 8, :], cells[l, r - 1 : r + 7, :], cells[l, r + 1 : r + 9, :]
+                u, v = winds[0, l, k, :], winds[1, l, k, :]
+            else:
+                s, no, so = halo_rows(lambda r: cells[l, r : r + 8, :], upper)
+                u, v = halo[1, pl.ds(h, 8), :], halo[2, pl.ds(h, 8), :]
+                d = d * row_one
+            w = jnp.where(lane == 0, 0.0, pltpu.roll(s, 1, 1))
+            e = jnp.where(lane == COLS - 1, 0.0, pltpu.roll(s, COLS - 1, 1))
+            partial[l, k, :] = stencil(s, no, so, w, e, u, v, d, 1.0 - 4.0 * d)
+        return carry
+
+    lax.fori_loop(0, LEVELS, level, 0, unroll=4)
+
+
+def halo_rows(load, upper):
+    d, u = BASE + ROWS, BASE - 8
+    return (
+        load(d),
+        jnp.where(upper, load(d - 1), load(u - 1)),
+        jnp.where(upper, load(d + 1), load(u + 1)),
+    )
+
+
+def substeps_kernel(rates, weights, masks, partial, winds, halo, strip0, from_left, from_right,
                     state_out, fluxes, rounded, top,
-                    cells0, cells1, cells2, cells3, ready,
+                    cells1, cells2, cells3, ready,
                     lefts, rights, sides, left_winds, right_winds, left, right, sems):
-    cells = (cells0, cells1, cells2, cells3)
+    cells = (None, cells1, cells2, cells3)
     upper = sub_ids() < 4
     n = ROWS + 8
     own = slice(BASE, BASE + ROWS)
@@ -139,14 +185,6 @@
     place = lane & 7
     first = place < 4
     row_one, side_one, rate = masks[0], masks[1], masks[2]
-
-    def halo_rows(load):
-        d, u = BASE + ROWS, BASE - 8
-        return (
-            load(d),
-            jnp.where(upper, load(d - 1), load(u - 1)),
-            jnp.where(upper, load(d + 1), load(u + 1)),
-        )
 
     def put(buf, t, x):
         if t < TILES:
@@ -164,7 +202,7 @@
         b = (b + pltpu.roll(b, 4, 1)) * side_one
         put(lefts[0], t, jnp.where(first, a, strip0[0, r]))
         put(rights[0], t, jnp.where(first, strip0[0, r], b))
-        put(sides[0], t, jnp.where(first, a, b))
+        put(sides[0], t, jnp.where(place == 4, pltpu.roll(a, 1, 1), pltpu.roll(b, COLS - 1, 1)))
         a, b = left[q], right[q]
         left_winds[0, r] = jnp.where(first, a * side_one, strip0[1, r])
         right_winds[0, r] = jnp.where(first, strip0[1, r], b * side_one)
@@ -181,7 +219,7 @@
                 if t < TILES:
                     s, no, so = strip[r : r + 8], strip[r - 1 : r + 7], strip[r + 1 : r + 9]
                 else:
-                    s, no, so = halo_rows(lambda r: strip[r : r + 8])
+                    s, no, so = halo_rows(lambda r: strip[r : r + 8], upper)
                     d = d * row_one
                 w, e = pltpu.roll(s, 1, 1), pltpu.roll(s, COLS - 1, 1)
                 new.append(stencil(s, no, so, w, e, wind[0, k], wind[1, k], d, 1.0 - 4.0 * d))
@@ -190,16 +228,6 @@
                 put(rights[step + 1], t, new[1])
             put(sides[step + 1], t, jnp.where(first, new[0], new[1]))
 
-    def copy_level(l, carry):
-        h = pl.multiple_of(8 * l, 8)
-        cells0[l, own] = state[l]
-        x = halo[0, pl.ds(h, 8), :]
-        cells0[l, high] = x
-        cells0[l, low] = x
-        return carry
-
-    lax.fori_loop(0, LEVELS, copy_level, 0, unroll=2)
-
     def beside(s, side, last, first):
         return (
             pltpu.roll(jnp.where(last, side, s), 1, 1),
@@ -209,10 +237,28 @@
     wide = lax.broadcasted_iota(jnp.int32, (BLOCK, COLS), 1)
     last_wide, first_wide = wide == COLS - 1, wide == 0
     last_lane, first_lane = lane == COLS - 1, lane == 0
+    edge_one = jnp.where(last_lane | first_lane, 1.0, 0.0)
+    edge_half = jnp.where(first_lane, 0.5, jnp.where(last_lane, -0.5, 0.0))
 
     for step in range(SUBSTEPS):
         last = step == SUBSTEPS - 1
         src, strip = cells[step], sides[step]
+
+        def beyond(l, carry):
+            h = pl.multiple_of(8 * l, 8)
+            d = rates[pl.ds(l, 1), :] * edge_one
+            turn = COLS - 4 - 8 * l
+            for t in range(TILES + 1):
+                k = slice(8 * t, 8 * t + 8)
+                r = BASE + 8 * t
+                side = pltpu.roll(strip[r : r + 8], turn, 1)
+                if t < TILES:
+                    cells1[l, r : r + 8, :] = partial[l, k, :] + side * (d + edge_half * winds[0, l, k, :])
+                else:
+                    y = partial[l, k, :] + side * (d * row_one + edge_half * halo[1, pl.ds(h, 8), :])
+                    cells1[l, high, :] = y
+                    cells1[l, low, :] = y
+            return carry
 
         def level(l, carry):
             h = pl.multiple_of(8 * l, 8)
@@ -232,7 +278,7 @@
                     cells[step + 1][l, r : r + BLOCK, :] = x
             if last:
                 return carry
-            s, no, so = halo_rows(lambda r: src[l, r : r + 8, :])
+            s, no, so = halo_rows(lambda r: src[l, r : r + 8, :], upper)
             w, e = beside(s, pltpu.roll(strip[low], turn, 1), last_lane, first_lane)
             d = d * row_one
             y = stencil(s, no, so, w, e, halo[1, pl.ds(h, 8), :], halo[2, pl.ds(h, 8), :], d, 1.0 - 4.0 * d)
@@ -240,8 +286,7 @@
             cells[step + 1][l, low, :] = y
             return carry
 
-        if step < STEPS:
-            lax.fori_loop(0, LEVELS, level, 0, unroll=UNROLL)
+        lax.fori_loop(0, LEVELS, level if step else beyond, 0, unroll=UNROLL)
 
     send = pltpu.make_async_copy(ready, state_out, sems.at[0])
     send.start()
@@ -333,11 +378,17 @@
             copy.wait()
 
 
-WIDE = pltpu.CompilerParams(vmem_limit_bytes=63 * 2**20 + 2**19)
+WIDE = pltpu.CompilerParams(vmem_limit_bytes=53 * 2**20 + 5 * 2**17)
 LIMIT = pltpu.CompilerParams(vmem_limit_bytes=16 * 2**20)
 N = ROWS + 8
 SHEET = jax.ShapeDtypeStruct((2 * LEVELS * 8, COLS), BF16)
 COLUMNS = jax.ShapeDtypeStruct((2 * N, COLS), BF16)
+
+
+def cost(microseconds):
+    return pl.CostEstimate(
+        flops=int(1e9 * microseconds), bytes_accessed=int(3.6e6 * microseconds), transcendentals=0
+    )
 
 
 def f32(*shape):
@@ -357,6 +408,7 @@
             pltpu.SemaphoreType.DMA((4,)),
         ],
         compiler_params=WIDE,
+        cost_estimate=cost(1.1),
         name="edge_rows",
     )(state, winds)
 
@@ -368,6 +420,7 @@
         out_specs=VMEM,
         out_shape=f32(3, ROWS, COLS),
         compiler_params=LIMIT,
+        cost_estimate=cost(1.0),
         name="own_strips",
     )(state, winds)
 
@@ -386,11 +439,25 @@
             pltpu.VMEM((2 * N, COLS), F32),
         ],
         compiler_params=LIMIT,
+        cost_estimate=cost(0.2),
         name="edge_columns",
     )(masks, from_below, from_above, own)
 
 
-def substeps(rates, weights, masks, state, winds, halo, strip0, from_left, from_right):
+def first_step(rates, masks, state, winds, halo):
+    return pl.pallas_call(
+        first_step_kernel,
+        in_specs=[VMEM] * 5,
+        out_specs=VMEM,
+        out_shape=f32(LEVELS, N, COLS),
+        scratch_shapes=[pltpu.VMEM((LEVELS, DEEP, COLS), F32)],
+        compiler_params=LIMIT,
+        cost_estimate=cost(1.0),
+        name="first_step",
+    )(rates, masks, state, winds, halo)
+
+
+def substeps(rates, weights, masks, partial, winds, halo, strip0, from_left, from_right):
     return pl.pallas_call(
         substeps_kernel,
         in_specs=[VMEM] * 9,
@@ -402,7 +469,7 @@
             f32(ROWS, COLS),
         ],
         scratch_shapes=[
-            *[pltpu.VMEM((LEVELS, DEEP, COLS), F32)] * 4,
+            *[pltpu.VMEM((LEVELS, DEEP, COLS), F32)] * 3,
             pltpu.VMEM((LEVELS, ROWS, COLS), F32),
             [pltpu.VMEM((DEEP, COLS), F32)] * 3,
             [pltpu.VMEM((DEEP, COLS), F32)] * 3,
@@ -413,7 +480,7 @@
         ],
         compiler_params=LIMIT,
         name="substeps",
-    )(rates, weights, masks, state, winds, halo, strip0, from_left, from_right)
+    )(rates, weights, masks, partial, winds, halo, strip0, from_left, from_right)
 
 
 def turn_blocks(blocks):
@@ -423,6 +490,7 @@
         out_specs=VMEM,
         out_shape=jax.ShapeDtypeStruct(blocks.shape, BF16),
         compiler_params=LIMIT,
+        cost_estimate=cost(1.0),
         name="turn_blocks",
     )(blocks)
 
@@ -491,9 +559,10 @@
     halo, strip0, to_right, to_left = edge_columns(masks, from_below, from_above, own)
     from_left = ring(to_right, "gy", 1)
     from_right = ring(to_left, "gy", -1)
+    partial = first_step(rates, masks, state, winds, halo)
     turned = turn_blocks(remap_blocks)
     state_out, fluxes, rounded, top_level = substeps(
-        rates, weights, masks, state, winds, halo, strip0, from_left, from_right
+        rates, weights, masks, partial, winds, halo, strip0, from_left, from_right
     )
     gathered = lax.all_gather(rounded, "grp", axis=0, tiled=True)
     fluxes, boundary = remap(

time: 39.9 us -> 37.8 us (0.947)
  local copies, waits for them, and re-layouts: 4.61 us -> 0.58 us
  waiting for transfers between devices: 2.77 us -> 4.19 us
  blocking collectives: 8.95 us -> 9.97 us
  Pallas kernels: 12.6 us -> 12.2 us
    unnamed x23 -> x21, local copies, waits for them, and re-layouts: 4.09 us -> 0.06 us
    ppermute x4, waiting for transfers between devices: 2.77 us -> 4.19 us  [ring(): lax.ppermute(x, axis, [(i, (i + shift) % count) for i in range(count)])]
    all_gather x1, blocking collectives: 8.95 us -> 9.97 us  [body(): gathered = lax.all_gather(rounded, 'grp', axis=0, tiled=True)]
    pallas_call x0 -> x1, Pallas kernels: none -> 0.66 us  [first_step(): pl.pallas_call(first_step_kernel, in_specs=[VMEM] * 5, out_specs=VMEM, ou...]
    pallas_call x1, Pallas kernels: 1.74 us -> 1.19 us  [edge_rows(): pl.pallas_call(edge_rows_kernel, in_specs=[HBM, HBM], out_specs=[VMEM, VM...]
    pallas_call x1, Pallas kernels: 4.68 us -> 4.2 us  [substeps(): pl.pallas_call(substeps_kernel, in_specs=[VMEM] * 9, out_specs=[ANY] + [V...]
  transfers between devices with their start and end apart: 4 -> 4, of which waited for: 1 -> 2; matrix products, arithmetic and copies ran while one was open for 1% -> 2% of each run, Pallas kernels for 5% -> 7%
where the time goes in v4:
time: 37.8 us; the launch traced here: 37.7 us
  Pallas kernels  12.2 us (32%)
  blocking collectives  9.97 us (26%)
  starting transfers between devices  9.73 us (26%)
  waiting for transfers between devices  4.19 us (11%)
  between operations  0.86 us (2%)
  local copies, waits for them, and re-layouts  0.58 us (2%)
    all_gather x1, blocking collectives, body(): gathered = lax.all_gather(rounded, 'grp', axis=0, tiled=True)  9.97 us
    ppermute x4, starting transfers between devices, ring(): lax.ppermute(x, axis, [(i, (i + shift) % count) for i in range(count)])  9.73 us
    pallas_call x1, Pallas kernels, substeps(): pl.pallas_call(substeps_kernel, in_specs=[VMEM] * 9, out_specs=[ANY] + [V...  4.2 us
    ppermute x4, waiting for transfers between devices, ring(): lax.ppermute(x, axis, [(i, (i + shift) % count) for i in range(count)])  4.19 us
    pallas_call x1, Pallas kernels, remap(): pl.pallas_call(remap_kernel, in_specs=[ANY] + [VMEM] * 5, out_specs=[ANY]...  4.03 us
    pallas_call x1, Pallas kernels, edge_rows(): pl.pallas_call(edge_rows_kernel, in_specs=[HBM, HBM], out_specs=[VMEM, VM...  1.19 us
    pallas_call x1, Pallas kernels, turn_blocks(): pl.pallas_call(turn_blocks_kernel, in_specs=[VMEM], out_specs=VMEM, out_s...  0.98 us
    pallas_call x1, Pallas kernels, own_strips(): pl.pallas_call(own_strips_kernel, in_specs=[VMEM, VMEM], out_specs=VMEM,...  0.95 us
  transfers between devices with their start and end apart: 4, of which 2 were waited for; matrix products, arithmetic and copies ran while one was open for 2% of the time, Pallas kernels for 7%

profile of v4, /device:TPU:5, one launch (start us, length us, event | category | flops | bytes accessed | tf_op | source)
XLA Modules:
  0.0 37.7 jit_solution(5910679479437459360)
XLA Ops:
  0.6 0.0 copy-start.1
  0.6 0.0 copy-start.2
  0.7 1.2 %edge_rows.1 = (bf16[256,128]{1,0:T(8,128)(2,1)S(1)}, bf16[256,128]{1,0:T(8,128)(2,1)S(1)}) custom-call(f32[16,64,128]{2,1,0:T(8,128)} %state.5, f32[2,16,64,128]{3,2,1,0:T(8,128)} %winds.7), custom_call_target="tpu_custom_call" | custom-call | flops 1100000000 | bytes 3960000 | tf_op jit(solution)/shard_map/edge_rows/pallas_call | solution.py:399
  1.8 0.0 copy-start.7
  1.9 0.0 copy-start.4
  1.9 0.0 copy-start.5
  1.9 0.0 copy-start.6
  1.9 0.0 copy-start.8
  1.9 0.0 copy-start
  1.9 6.9 %collective-permute-start = (bf16[256,128]{1,0:T(8,128)(2,1)S(1)}, bf16[256,128]{1,0:T(8,128)(2,1)S(1)}, u32[]{:S(2)}, u32[]{:S(2)}) collective-permute-start(bf16[256,128]{1,0:T(8,128)(2,1)S(1)} %get-tuple-element.15), channel_id=1, source_target_pairs={{0,252},{4,0},{8,4},{12,8},{16,12},{20,16},{24,20},{28,24},{32,28}... | collective-permute-start | bytes 196616 | tf_op jit(solution)/shard_map/ppermute | solution.py:553
  8.8 0.0 collective-permute-start.1
  8.8 0.0 copy-done.1
  8.8 0.0 copy-done.2
  8.8 0.9 %own_strips.1.own = f32[3,64,128]{2,1,0:T(8,128)S(1)} custom-call(f32[16,64,128]{2,1,0:T(8,128)S(1)} %copy-done.2, f32[2,16,64,128]{3,2,1,0:T(8,128)S(1)} %copy-done.1), custom_call_target="tpu_custom_call" | custom-call | flops 1000000000 | bytes 3600000 | tf_op jit(solution)/shard_map/own_strips/pallas_call | solution.py:417
  9.8 0.0 copy-done.7
  9.8 0.0 copy-done.4
  9.8 0.1 broadcast_in_dim.46
  9.9 0.0 copy-done.5
  9.9 0.0 copy-done.6
  9.9 0.1 broadcast_in_dim.52
  10.0 0.1 mul.15
  10.1 0.1 add_bitcast_fusion
  10.2 0.0 copy-done.8
  10.2 0.1 pad_add_fusion.words
  10.3 0.1 iota.13
  10.3 0.0 copy-done
  10.4 0.0 copy-start.3
  10.4 1.0 %turn_blocks.1.weights = bf16[64,128,128]{2,1,0:T(8,128)(2,1)S(1)} custom-call(bf16[64,128,128]{2,1,0:T(8,128)(2,1)S(1)} %copy-done), custom_call_target="tpu_custom_call" | custom-call | flops 1000000000 | bytes 3600000 | tf_op jit(solution)/shard_map/turn_blocks/pallas_call | solution.py:487
  11.3 0.0 collective-permute-done.from_below
  11.4 3.7 %collective-permute-done.1.from_above = bf16[256,128]{1,0:T(8,128)(2,1)S(1)} collective-permute-done((bf16[256,128]{1,0:T(8,128)(2,1)S(1)}, bf16[256,128]{1,0:T(8,128)(2,1)S(1)}, u32[]{:S(2)}, u32[]{:S(2)}) %collective-permute-start.1) | collective-permute-done | bytes 65568 | tf_op jit(solution)/shard_map/ppermute | solution.py:553
  15.0 0.2 edge_columns.1
  15.2 1.3 %collective-permute-start.2 = (bf16[144,128]{1,0:T(8,128)(2,1)S(1)}, bf16[144,128]{1,0:T(8,128)(2,1)S(1)}, u32[]{:S(2)}, u32[]{:S(2)}) collective-permute-start(bf16[144,128]{1,0:T(8,128)(2,1)S(1)} %get-tuple-element.19), channel_id=1, source_target_pairs={{0,1},{1,2},{2,3},{3,0},{4,5},{5,6},{6,7},{7,4},{8,9},{9,10},{10,1... | collective-permute-start | bytes 110600 | tf_op jit(solution)/shard_map/ppermute | solution.py:553
  16.5 1.5 %collective-permute-start.3 = (bf16[144,128]{1,0:T(8,128)(2,1)S(1)}, bf16[144,128]{1,0:T(8,128)(2,1)S(1)}, u32[]{:S(2)}, u32[]{:S(2)}) collective-permute-start(bf16[144,128]{1,0:T(8,128)(2,1)S(1)} %get-tuple-element.20), channel_id=1, source_target_pairs={{0,3},{1,0},{2,1},{3,2},{4,7},{5,4},{6,5},{7,6},{8,11},{9,8},{10,9... | collective-permute-start | bytes 110600 | tf_op jit(solution)/shard_map/ppermute | solution.py:553
  18.1 0.1 broadcast_in_dim.45.rates
  18.1 0.0 copy-done.3
  18.1 0.7 %first_step.1.partial = f32[16,72,128]{2,1,0:T(8,128)S(1)} custom-call(f32[16,128]{1,0:T(8,128)S(1)} %broadcast_in_dim.45.rates, f32[3,8,128]{2,1,0:T(8,128)S(1)} %pad_maximum_fusion.masks, f32[16,64,128]{2,1,0:T(8,128)S(1)} %copy-done.3, f32[2,16,64,128]{3,2,1,0:T(8,128)S(1)} %copy-done.1, f32[3,128,128]{2,1,0:T(8,128)S(1)} %get-tuple-element.17.halo), custom_call_target="tpu_custom_call" | custom-call | flops 1000000000 | bytes 3600000 | tf_op jit(solution)/shard_map/first_step/pallas_call | solution.py:448
  18.8 0.0 copy-start.9
  18.8 0.5 %collective-permute-done.2.from_left = bf16[144,128]{1,0:T(8,128)(2,1)S(1)} collective-permute-done((bf16[144,128]{1,0:T(8,128)(2,1)S(1)}, bf16[144,128]{1,0:T(8,128)(2,1)S(1)}, u32[]{:S(2)}, u32[]{:S(2)}) %collective-permute-start.2) | collective-permute-done | bytes 36896 | tf_op jit(solution)/shard_map/ppermute | solution.py:553
  19.3 0.0 collective-permute-done.3.from_right
  19.3 0.1 broadcast_in_dim.47.weights
  19.4 4.2 %substeps.1 = (f32[16,64,128]{2,1,0:T(8,128)}, f32[8,64,128]{2,1,0:T(8,128)S(1)}, bf16[512,128]{1,0:T(8,128)(2,1)S(1)}, f32[64,128]{1,0:T(8,128)S(1)}) custom-call(f32[16,128]{1,0:T(8,128)S(1)} %broadcast_in_dim.45.rates, f32[128,128]{1,0:T(8,128)S(1)} %broadcast_in_dim.47.weights, f32[3,8,128]{2,1,0:T(8,128)S(1)} %pad_maximum_fusion.masks, ...), custom_call_target="tpu_custom_call" | custom-call | tf_op jit(solution)/shard_map/substeps/pallas_call | solution.py:461
  23.6 10.0 %all_gather.3.gathered = bf16[2048,128]{1,0:T(8,128)(2,1)S(1)} all-gather(bf16[512,128]{1,0:T(8,128)(2,1)S(1)} %get-tuple-element.22), channel_id=1, replica_groups=mesh['grp'=4,'gx'=16,'gy'=4] {'grp'}, dimensions={0}, use_global_device_ids=true | all-gather | bytes 655360 | tf_op jit(solution)/shard_map/all_gather | solution.py:567
  33.6 0.0 copy-done.9
  33.6 0.1 broadcast_in_dim.55.heat
  33.7 4.0 %remap.1 = (f32[8,64,128]{2,1,0:T(8,128)}, f32[64,128]{1,0:T(8,128)}) custom-call(s32[833]{0:T(1024)S(1)} %pad_add_fusion.words, f32[8,128]{1,0:T(8,128)S(1)} %broadcast_in_dim.55.heat, bf16[2048,128]{1,0:T(8,128)(2,1)S(1)} %all_gather.3.gathered, bf16[64,128,128]{2,1,0:T(8,128)(2,1)S(1)} %turn_blocks.1.weights, f32[8,64,128]{2,1,0:T(8,128)S(1)} %get-tuple-element.23.fluxes, ...), custom_call_target="tpu_custom_call" | custom-call | tf_op jit(solution)/shard_map/remap/pallas_call | solution.py:500
  (8 shorter events, 0.0 us)
Async XLA Ops:
  0.6 8.2 %copy-start.1 = (f32[2,16,64,128]{3,2,1,0:T(8,128)S(1)}, f32[2,16,64,128]{3,2,1,0:T(8,128)}, u32[]{:S(2)}) copy-start(f32[2,16,64,128]{3,2,1,0:T(8,128)} %winds.7) | copy-start | bytes 3145732
  0.6 8.1 %copy-start.2 = (f32[16,64,128]{2,1,0:T(8,128)S(1)}, f32[16,64,128]{2,1,0:T(8,128)}, u32[]{:S(2)}) copy-start(f32[16,64,128]{2,1,0:T(8,128)} %state.5) | copy-start | bytes 1572868
  1.8 7.9 %copy-start.7 = (f32[2,16]{1,0:T(2,128)S(1)}, f32[2,16]{1,0:T(2,128)}, u32[]{:S(2)}) copy-start(f32[2,16]{1,0:T(2,128)} %param.11) | copy-start | bytes 388
  1.9 7.9 %copy-start.4 = (f32[8,16]{1,0:T(8,128)S(1)}, f32[8,16]{1,0:T(8,128)}, u32[]{:S(2)}) copy-start(f32[8,16]{1,0:T(8,128)} %param.12) | copy-start | bytes 1540
  1.9 8.0 %copy-start.5 = (s32[1,1,64,6]{2,1,3,0:T(1,128)S(1)}, s32[1,1,64,6]{2,1,3,0:T(1,128)}, u32[]{:S(2)}) copy-start(s32[1,1,64,6]{2,1,3,0:T(1,128)} %param.15) | copy-start | bytes 4612
  1.9 8.0 %copy-start.6 = (s32[1,1,64,6]{2,1,3,0:T(1,128)S(1)}, s32[1,1,64,6]{2,1,3,0:T(1,128)}, u32[]{:S(2)}) copy-start(s32[1,1,64,6]{2,1,3,0:T(1,128)} %param.16) | copy-start | bytes 4612
  1.9 8.3 %copy-start.8 = (s32[1,1,64]{2,1,0:T(1,128)S(1)}, s32[1,1,64]{2,1,0:T(1,128)}, u32[]{:S(2)}) copy-start(s32[1,1,64]{2,1,0:T(1,128)} %param.17) | copy-start | bytes 772
  1.9 8.4 %copy-start = (bf16[64,128,128]{2,1,0:T(8,128)(2,1)S(1)}, bf16[64,128,128]{2,1,0:T(8,128)(2,1)}, u32[]{:S(2)}) copy-start(bf16[64,128,128]{2,1,0:T(8,128)(2,1)} %blocks.1) | copy-start | bytes 6291460
  1.9 9.4 %collective-permute-start = (bf16[256,128]{1,0:T(8,128)(2,1)S(1)}, bf16[256,128]{1,0:T(8,128)(2,1)S(1)}, u32[]{:S(2)}, u32[]{:S(2)}) collective-permute-start(bf16[256,128]{1,0:T(8,128)(2,1)S(1)} %get-tuple-element.15), channel_id=1, source_target_pairs={{0,252},{4,0},{8,4},{12,8},{16,12},{20,16},{24,20},{28,24},{32,28}... | collective-permute-start | bytes 196616 | tf_op jit(solution)/shard_map/ppermute | solution.py:553
  8.8 6.2 %collective-permute-start.1 = (bf16[256,128]{1,0:T(8,128)(2,1)S(1)}, bf16[256,128]{1,0:T(8,128)(2,1)S(1)}, u32[]{:S(2)}, u32[]{:S(2)}) collective-permute-start(bf16[256,128]{1,0:T(8,128)(2,1)S(1)} %get-tuple-element.16), channel_id=1, source_target_pairs={{0,4},{4,8},{8,12},{12,16},{16,20},{20,24},{24,28},{28,32},{32,36}... | collective-permute-start | bytes 196616 | tf_op jit(solution)/shard_map/ppermute | solution.py:553
  10.4 7.8 %copy-start.3 = (f32[16,64,128]{2,1,0:T(8,128)S(1)}, f32[16,64,128]{2,1,0:T(8,128)}, u32[]{:S(2)}) copy-start(f32[16,64,128]{2,1,0:T(8,128)} %state.5) | copy-start | bytes 1572868
  15.2 4.1 %collective-permute-start.2 = (bf16[144,128]{1,0:T(8,128)(2,1)S(1)}, bf16[144,128]{1,0:T(8,128)(2,1)S(1)}, u32[]{:S(2)}, u32[]{:S(2)}) collective-permute-start(bf16[144,128]{1,0:T(8,128)(2,1)S(1)} %get-tuple-element.19), channel_id=1, source_target_pairs={{0,1},{1,2},{2,3},{3,0},{4,5},{5,6},{6,7},{7,4},{8,9},{9,10},{10,1... | collective-permute-start | bytes 110600 | tf_op jit(solution)/shard_map/ppermute | solution.py:553
  16.5 2.8 %collective-permute-start.3 = (bf16[144,128]{1,0:T(8,128)(2,1)S(1)}, bf16[144,128]{1,0:T(8,128)(2,1)S(1)}, u32[]{:S(2)}, u32[]{:S(2)}) collective-permute-start(bf16[144,128]{1,0:T(8,128)(2,1)S(1)} %get-tuple-element.20), channel_id=1, source_target_pairs={{0,3},{1,0},{2,1},{3,2},{4,7},{5,4},{6,5},{7,6},{8,11},{9,8},{10,9... | collective-permute-start | bytes 110600 | tf_op jit(solution)/shard_map/ppermute | solution.py:553
  18.8 14.8 %copy-start.9 = (f32[8]{0:T(128)S(1)}, f32[8]{0:T(128)}, u32[]{:S(2)}) copy-start(f32[8]{0:T(128)} %param.13) | copy-start | bytes 100

commit v5 on v4

--- a/solution.py
+++ b/solution.py
@@ -15,7 +15,6 @@
 BASE = 16
 DEEP = ROWS + 32
 UNROLL = 4
-BLOCK = 8
 FLUX_ROWS = 32
 CHUNK = 32
 F32 = jnp.float32
@@ -125,7 +124,7 @@
     return c * s + d * ((n + so) + (w + e)) - 0.5 * drift
 
 
-def first_step_kernel(rates, masks, state, winds, halo, partial, cells):
+def inner_steps_kernel(rates, masks, state, winds, halo, last, total, cells0, cells1, cells2, cells3):
     own = slice(BASE, BASE + ROWS)
     high, low = slice(BASE - 8, BASE), slice(BASE + ROWS, BASE + ROWS + 8)
     upper = sub_ids() < 4
@@ -134,33 +133,47 @@
 
     def copy_level(l, carry):
         h = pl.multiple_of(8 * l, 8)
-        cells[l, own] = state[l]
+        cells0[l, own] = state[l]
         x = halo[0, pl.ds(h, 8), :]
-        cells[l, high] = x
-        cells[l, low] = x
+        cells0[l, high] = x
+        cells0[l, low] = x
         return carry
 
     lax.fori_loop(0, LEVELS, copy_level, 0, unroll=2)
 
-    def level(l, carry):
-        h = pl.multiple_of(8 * l, 8)
-        d = rates[pl.ds(l, 1), :]
-        for t in range(TILES + 1):
-            k = slice(8 * t, 8 * t + 8)
-            r = BASE + 8 * t
-            if t < TILES:
-                s, no, so = cells[l, r : r + 8, :], cells[l, r - 1 : r + 7, :], cells[l, r + 1 : r + 9, :]
-                u, v = winds[0, l, k, :], winds[1, l, k, :]
-            else:
-                s, no, so = halo_rows(lambda r: cells[l, r : r + 8, :], upper)
-                u, v = halo[1, pl.ds(h, 8), :], halo[2, pl.ds(h, 8), :]
-                d = d * row_one
-            w = jnp.where(lane == 0, 0.0, pltpu.roll(s, 1, 1))
-            e = jnp.where(lane == COLS - 1, 0.0, pltpu.roll(s, COLS - 1, 1))
-            partial[l, k, :] = stencil(s, no, so, w, e, u, v, d, 1.0 - 4.0 * d)
-        return carry
-
-    lax.fori_loop(0, LEVELS, level, 0, unroll=4)
+    def step(src, dst):
+        def level(l, carry):
+            h = pl.multiple_of(8 * l, 8)
+            d = rates[pl.ds(l, 1), :]
+            for t in range(TILES if dst is None else TILES + 1):
+                k = slice(8 * t, 8 * t + 8)
+                r = BASE + 8 * t
+                if t < TILES:
+                    s, no, so = src[l, r : r + 8, :], src[l, r - 1 : r + 7, :], src[l, r + 1 : r + 9, :]
+                    u, v = winds[0, l, k, :], winds[1, l, k, :]
+                else:
+                    s, no, so = halo_rows(lambda r: src[l, r : r + 8, :], upper)
+                    u, v = halo[1, pl.ds(h, 8), :], halo[2, pl.ds(h, 8), :]
+                    d = d * row_one
+                w = jnp.where(lane == 0, 0.0, pltpu.roll(s, 1, 1))
+                e = jnp.where(lane == COLS - 1, 0.0, pltpu.roll(s, COLS - 1, 1))
+                x = stencil(s, no, so, w, e, u, v, d, 1.0 - 4.0 * d)
+                if dst is None:
+                    last[l, k, :] = x
+                    total[l, k, :] = (cells1[l, r : r + 8, :] + cells2[l, r : r + 8, :]) + (s + x)
+                elif t < TILES:
+                    dst[l, r : r + 8, :] = x
+                else:
+                    dst[l, high, :] = x
+                    dst[l, low, :] = x
+            return carry
+
+        lax.fori_loop(0, LEVELS, level, 0, unroll=UNROLL)
+
+    step(cells0, cells1)
+    step(cells1, cells2)
+    step(cells2, cells3)
+    step(cells3, None)
 
 
 def halo_rows(load, upper):
@@ -172,11 +185,9 @@
     )
 
 
-def substeps_kernel(rates, weights, masks, partial, winds, halo, strip0, from_left, from_right,
-                    state_out, fluxes, rounded, top,
-                    cells1, cells2, cells3, ready,
-                    lefts, rights, sides, left_winds, right_winds, left, right, sems):
-    cells = (None, cells1, cells2, cells3)
+def columns_kernel(weights, masks, inner_last, inner_total, strip0, from_left, from_right,
+                   state_out, fluxes, rounded, top,
+                   ready, lefts, rights, beyond, extras, left_winds, right_winds, left, right, extra_total, sems):
     upper = sub_ids() < 4
     n = ROWS + 8
     own = slice(BASE, BASE + ROWS)
@@ -202,7 +213,7 @@
         b = (b + pltpu.roll(b, 4, 1)) * side_one
         put(lefts[0], t, jnp.where(first, a, strip0[0, r]))
         put(rights[0], t, jnp.where(first, strip0[0, r], b))
-        put(sides[0], t, jnp.where(place == 4, pltpu.roll(a, 1, 1), pltpu.roll(b, COLS - 1, 1)))
+        beyond[0][r] = jnp.where(first, a, b)
         a, b = left[q], right[q]
         left_winds[0, r] = jnp.where(first, a * side_one, strip0[1, r])
         right_winds[0, r] = jnp.where(first, strip0[1, r], b * side_one)
@@ -226,78 +237,44 @@
             if step < SUBSTEPS - 2:
                 put(lefts[step + 1], t, new[0])
                 put(rights[step + 1], t, new[1])
-            put(sides[step + 1], t, jnp.where(first, new[0], new[1]))
-
-    def beside(s, side, last, first):
-        return (
-            pltpu.roll(jnp.where(last, side, s), 1, 1),
-            pltpu.roll(jnp.where(first, side, s), COLS - 1, 1),
-        )
-
-    wide = lax.broadcasted_iota(jnp.int32, (BLOCK, COLS), 1)
-    last_wide, first_wide = wide == COLS - 1, wide == 0
-    last_lane, first_lane = lane == COLS - 1, lane == 0
-    edge_one = jnp.where(last_lane | first_lane, 1.0, 0.0)
-    edge_half = jnp.where(first_lane, 0.5, jnp.where(last_lane, -0.5, 0.0))
+            beyond[step + 1][k] = jnp.where(first, new[0], new[1])
 
     for step in range(SUBSTEPS):
         last = step == SUBSTEPS - 1
-        src, strip = cells[step], sides[step]
-
-        def beyond(l, carry):
-            h = pl.multiple_of(8 * l, 8)
-            d = rates[pl.ds(l, 1), :] * edge_one
-            turn = COLS - 4 - 8 * l
-            for t in range(TILES + 1):
-                k = slice(8 * t, 8 * t + 8)
-                r = BASE + 8 * t
-                side = pltpu.roll(strip[r : r + 8], turn, 1)
-                if t < TILES:
-                    cells1[l, r : r + 8, :] = partial[l, k, :] + side * (d + edge_half * winds[0, l, k, :])
-                else:
-                    y = partial[l, k, :] + side * (d * row_one + edge_half * halo[1, pl.ds(h, 8), :])
-                    cells1[l, high, :] = y
-                    cells1[l, low, :] = y
-            return carry
-
-        def level(l, carry):
-            h = pl.multiple_of(8 * l, 8)
-            d = rates[pl.ds(l, 1), :]
-            c = 1.0 - 4.0 * d
-            turn = COLS - 4 - 8 * l
-            for t in range(ROWS // BLOCK):
-                k = slice(BLOCK * t, BLOCK * (t + 1))
-                r = BASE + BLOCK * t
-                s = src[l, r : r + BLOCK, :]
-                w, e = beside(s, pltpu.roll(strip[r : r + BLOCK], turn, 1), last_wide, first_wide)
-                x = stencil(s, src[l, r - 1 : r + BLOCK - 1, :], src[l, r + 1 : r + BLOCK + 1, :],
-                            w, e, winds[0, l, k, :], winds[1, l, k, :], d, c)
-                if last:
-                    ready[l, k, :] = x
-                else:
-                    cells[step + 1][l, r : r + BLOCK, :] = x
-            if last:
-                return carry
-            s, no, so = halo_rows(lambda r: src[l, r : r + 8, :], upper)
-            w, e = beside(s, pltpu.roll(strip[low], turn, 1), last_lane, first_lane)
-            d = d * row_one
-            y = stencil(s, no, so, w, e, halo[1, pl.ds(h, 8), :], halo[2, pl.ds(h, 8), :], d, 1.0 - 4.0 * d)
-            cells[step + 1][l, high, :] = y
-            cells[step + 1][l, low, :] = y
-            return carry
-
-        lax.fori_loop(0, LEVELS, level if step else beyond, 0, unroll=UNROLL)
+        for t in range(TILES if last else TILES + 1):
+            r, k = BASE + 8 * t, slice(8 * t, 8 * t + 8)
+            side = beyond[step][k]
+            d = rate if t < TILES else rate * row_one
+            if step == 0:
+                s = no = so = jnp.zeros((8, COLS), F32)
+            elif t < TILES:
+                old = extras[step - 1]
+                s, no, so = old[r : r + 8], old[r - 1 : r + 7], old[r + 1 : r + 9]
+            else:
+                s, no, so = halo_rows(lambda r: extras[step - 1][r : r + 8], upper)
+            w = pltpu.roll(jnp.where(place == 3, side, jnp.where(place == 7, 0.0, s)), 1, 1)
+            e = pltpu.roll(jnp.where(place == 4, side, jnp.where(place == 0, 0.0, s)), COLS - 1, 1)
+            x = stencil(s, no, so, w, e, strip0[1, k], strip0[2, k], d, 1.0 - 4.0 * d)
+            put(extras[step], t, x)
+            if t < TILES:
+                extra_total[k] = x if step == 0 else extra_total[k] + x
+
+    def edges(x, l):
+        lanes = lax.broadcasted_iota(jnp.int32, x.shape, 1)
+        return jnp.where((lanes < 4) | (lanes >= COLS - 4), pltpu.roll(x, COLS - 4 - 8 * l, 1), 0.0)
+
+    for l in range(LEVELS):
+        ready[l] = inner_last[l] + edges(extras[SUBSTEPS - 1][own], l)
 
     send = pltpu.make_async_copy(ready, state_out, sems.at[0])
     send.start()
 
     def flux(t, carry):
         r = pl.multiple_of(FLUX_ROWS * t, FLUX_ROWS)
-        at = pl.ds(BASE + r, FLUX_ROWS)
         out = pl.ds(r, FLUX_ROWS)
         sums = [None] * FIELDS
         for l in range(LEVELS):
-            x = (cells1[l, at, :] + cells2[l, at, :]) + (cells3[l, at, :] + ready[l, out, :])
+            x = inner_total[l, out, :] + edges(extra_total[out, :], l)
             for f in range(FIELDS):
                 k = f * LEVELS + l
                 term = weights[k : k + 1, :] * x
@@ -444,23 +421,23 @@
     )(masks, from_below, from_above, own)
 
 
-def first_step(rates, masks, state, winds, halo):
-    return pl.pallas_call(
-        first_step_kernel,
+def inner_steps(rates, masks, state, winds, halo):
+    return pl.pallas_call(
+        inner_steps_kernel,
         in_specs=[VMEM] * 5,
-        out_specs=VMEM,
-        out_shape=f32(LEVELS, N, COLS),
-        scratch_shapes=[pltpu.VMEM((LEVELS, DEEP, COLS), F32)],
+        out_specs=[VMEM] * 2,
+        out_shape=[f32(LEVELS, ROWS, COLS)] * 2,
+        scratch_shapes=[pltpu.VMEM((LEVELS, DEEP, COLS), F32)] * 4,
         compiler_params=LIMIT,
-        cost_estimate=cost(1.0),
-        name="first_step",
+        cost_estimate=cost(2.5),
+        name="inner_steps",
     )(rates, masks, state, winds, halo)
 
 
-def substeps(rates, weights, masks, partial, winds, halo, strip0, from_left, from_right):
-    return pl.pallas_call(
-        substeps_kernel,
-        in_specs=[VMEM] * 9,
+def columns(weights, masks, inner_last, inner_total, strip0, from_left, from_right):
+    return pl.pallas_call(
+        columns_kernel,
+        in_specs=[VMEM] * 7,
         out_specs=[ANY] + [VMEM] * 3,
         out_shape=[
             f32(LEVELS, ROWS, COLS),
@@ -469,18 +446,19 @@
             f32(ROWS, COLS),
         ],
         scratch_shapes=[
-            *[pltpu.VMEM((LEVELS, DEEP, COLS), F32)] * 3,
             pltpu.VMEM((LEVELS, ROWS, COLS), F32),
             [pltpu.VMEM((DEEP, COLS), F32)] * 3,
             [pltpu.VMEM((DEEP, COLS), F32)] * 3,
+            [pltpu.VMEM((N, COLS), F32)] * 4,
             [pltpu.VMEM((DEEP, COLS), F32)] * 4,
             *[pltpu.VMEM((2, N, COLS), F32)] * 2,
             *[pltpu.VMEM((2 * N, COLS), F32)] * 2,
+            pltpu.VMEM((ROWS, COLS), F32),
             pltpu.SemaphoreType.DMA((1,)),
         ],
         compiler_params=LIMIT,
-        name="substeps",
-    )(rates, weights, masks, partial, winds, halo, strip0, from_left, from_right)
+        name="columns",
+    )(weights, masks, inner_last, inner_total, strip0, from_left, from_right)
 
 
 def turn_blocks(blocks):
@@ -559,10 +537,10 @@
     halo, strip0, to_right, to_left = edge_columns(masks, from_below, from_above, own)
     from_left = ring(to_right, "gy", 1)
     from_right = ring(to_left, "gy", -1)
-    partial = first_step(rates, masks, state, winds, halo)
+    inner_last, inner_total = inner_steps(rates, masks, state, winds, halo)
     turned = turn_blocks(remap_blocks)
-    state_out, fluxes, rounded, top_level = substeps(
-        rates, weights, masks, partial, winds, halo, strip0, from_left, from_right
+    state_out, fluxes, rounded, top_level = columns(
+        weights, masks, inner_last, inner_total, strip0, from_left, from_right
     )
     gathered = lax.all_gather(rounded, "grp", axis=0, tiled=True)
     fluxes, boundary = remap(

time: 37.8 us -> 35.4 us (0.937)
  blocking collectives: 9.97 us -> 8.95 us
  Pallas kernels: 12.2 us -> 11.3 us
  waiting for transfers between devices: 4.19 us -> 3.67 us
    all_gather x1, blocking collectives: 9.97 us -> 8.95 us  [body(): gathered = lax.all_gather(rounded, 'grp', axis=0, tiled=True)]
    pallas_call x2, Pallas kernels: 4.86 us -> 3.96 us  [the longest x1 2.45 us: inner_steps(): pl.pallas_call(inner_steps_kernel, in_specs=[VMEM] * 5, out_specs=[VMEM]...]
    ppermute x4, waiting for transfers between devices: 4.19 us -> 3.67 us  [ring(): lax.ppermute(x, axis, [(i, (i + shift) % count) for i in range(count)])]
  transfers between devices with their start and end apart: 4 -> 4, of which waited for: 2 -> 1; matrix products, arithmetic and copies ran while one was open for 2% -> 2% of each run, Pallas kernels for 7% -> 12%
where the time goes in v5:
time: 35.4 us; the launch traced here: 35.3 us
  Pallas kernels  11.3 us (32%)
  starting transfers between devices  9.73 us (27%)
  blocking collectives  8.95 us (25%)
  waiting for transfers between devices  3.67 us (10%)
  between operations  0.87 us (2%)
  local copies, waits for them, and re-layouts  0.58 us (2%)
    ppermute x4, starting transfers between devices, ring(): lax.ppermute(x, axis, [(i, (i + shift) % count) for i in range(count)])  9.73 us
    all_gather x1, blocking collectives, body(): gathered = lax.all_gather(rounded, 'grp', axis=0, tiled=True)  8.95 us
    pallas_call x1, Pallas kernels, remap(): pl.pallas_call(remap_kernel, in_specs=[ANY] + [VMEM] * 5, out_specs=[ANY]...  4.02 us
    ppermute x4, waiting for transfers between devices, ring(): lax.ppermute(x, axis, [(i, (i + shift) % count) for i in range(count)])  3.67 us
    pallas_call x1, Pallas kernels, inner_steps(): pl.pallas_call(inner_steps_kernel, in_specs=[VMEM] * 5, out_specs=[VMEM]...  2.45 us
    pallas_call x1, Pallas kernels, columns(): pl.pallas_call(columns_kernel, in_specs=[VMEM] * 7, out_specs=[ANY] + [VM...  1.51 us
    pallas_call x1, Pallas kernels, edge_rows(): pl.pallas_call(edge_rows_kernel, in_specs=[HBM, HBM], out_specs=[VMEM, VM...  1.19 us
    pallas_call x1, Pallas kernels, turn_blocks(): pl.pallas_call(turn_blocks_kernel, in_specs=[VMEM], out_specs=VMEM, out_s...  0.98 us
  transfers between devices with their start and end apart: 4, of which 1 were waited for; matrix products, arithmetic and copies ran while one was open for 2% of the time, Pallas kernels for 12%

profile of v5, /device:TPU:5, one launch (start us, length us, event | category | flops | bytes accessed | tf_op | source)
XLA Modules:
  0.0 35.3 jit_solution(3411536714966164005)
XLA Ops:
  0.6 0.0 copy-start.1
  0.6 0.0 copy-start.2
  0.7 1.2 %edge_rows.1 = (bf16[256,128]{1,0:T(8,128)(2,1)S(1)}, bf16[256,128]{1,0:T(8,128)(2,1)S(1)}) custom-call(f32[16,64,128]{2,1,0:T(8,128)} %state.5, f32[2,16,64,128]{3,2,1,0:T(8,128)} %winds.5), custom_call_target="tpu_custom_call" | custom-call | flops 1100000000 | bytes 3960000 | tf_op jit(solution)/shard_map/edge_rows/pallas_call | solution.py:376
  1.8 0.0 copy-start.7
  1.9 0.0 copy-start.4
  1.9 0.0 copy-start.5
  1.9 0.0 copy-start.6
  1.9 0.0 copy-start.8
  1.9 0.0 copy-start
  1.9 6.9 %collective-permute-start = (bf16[256,128]{1,0:T(8,128)(2,1)S(1)}, bf16[256,128]{1,0:T(8,128)(2,1)S(1)}, u32[]{:S(2)}, u32[]{:S(2)}) collective-permute-start(bf16[256,128]{1,0:T(8,128)(2,1)S(1)} %get-tuple-element.17), channel_id=1, source_target_pairs={{0,252},{4,0},{8,4},{12,8},{16,12},{20,16},{24,20},{28,24},{32,28}... | collective-permute-start | bytes 196616 | tf_op jit(solution)/shard_map/ppermute | solution.py:531
  8.8 0.0 collective-permute-start.1
  8.8 0.0 copy-done.1
  8.8 0.0 copy-done.2
  8.8 0.9 %own_strips.1.own = f32[3,64,128]{2,1,0:T(8,128)S(1)} custom-call(f32[16,64,128]{2,1,0:T(8,128)S(1)} %copy-done.2, f32[2,16,64,128]{3,2,1,0:T(8,128)S(1)} %copy-done.1), custom_call_target="tpu_custom_call" | custom-call | flops 1000000000 | bytes 3600000 | tf_op jit(solution)/shard_map/own_strips/pallas_call | solution.py:394
  9.8 0.0 copy-done.7
  9.8 0.0 copy-done.4
  9.8 0.1 broadcast_in_dim.45
  9.9 0.0 copy-done.5
  9.9 0.0 copy-done.6
  9.9 0.1 broadcast_in_dim.51
  10.0 0.1 mul.15
  10.1 0.1 add_bitcast_fusion
  10.2 0.0 copy-done.8
  10.2 0.1 pad_add_fusion.words
  10.3 0.1 iota.13
  10.3 0.0 copy-done
  10.4 0.0 copy-start.3
  10.4 1.0 %turn_blocks.1.weights = bf16[64,128,128]{2,1,0:T(8,128)(2,1)S(1)} custom-call(bf16[64,128,128]{2,1,0:T(8,128)(2,1)S(1)} %copy-done), custom_call_target="tpu_custom_call" | custom-call | flops 1000000000 | bytes 3600000 | tf_op jit(solution)/shard_map/turn_blocks/pallas_call | solution.py:465
  11.3 0.0 collective-permute-done.from_below
  11.4 3.7 %collective-permute-done.1.from_above = bf16[256,128]{1,0:T(8,128)(2,1)S(1)} collective-permute-done((bf16[256,128]{1,0:T(8,128)(2,1)S(1)}, bf16[256,128]{1,0:T(8,128)(2,1)S(1)}, u32[]{:S(2)}, u32[]{:S(2)}) %collective-permute-start.1) | collective-permute-done | bytes 65568 | tf_op jit(solution)/shard_map/ppermute | solution.py:531
  15.0 0.2 edge_columns.1
  15.2 1.3 %collective-permute-start.2 = (bf16[144,128]{1,0:T(8,128)(2,1)S(1)}, bf16[144,128]{1,0:T(8,128)(2,1)S(1)}, u32[]{:S(2)}, u32[]{:S(2)}) collective-permute-start(bf16[144,128]{1,0:T(8,128)(2,1)S(1)} %get-tuple-element.23), channel_id=1, source_target_pairs={{0,1},{1,2},{2,3},{3,0},{4,5},{5,6},{6,7},{7,4},{8,9},{9,10},{10,1... | collective-permute-start | bytes 110600 | tf_op jit(solution)/shard_map/ppermute | solution.py:531
  16.5 1.5 %collective-permute-start.3 = (bf16[144,128]{1,0:T(8,128)(2,1)S(1)}, bf16[144,128]{1,0:T(8,128)(2,1)S(1)}, u32[]{:S(2)}, u32[]{:S(2)}) collective-permute-start(bf16[144,128]{1,0:T(8,128)(2,1)S(1)} %get-tuple-element.24), channel_id=1, source_target_pairs={{0,3},{1,0},{2,1},{3,2},{4,7},{5,4},{6,5},{7,6},{8,11},{9,8},{10,9... | collective-permute-start | bytes 110600 | tf_op jit(solution)/shard_map/ppermute | solution.py:531
  18.1 0.1 broadcast_in_dim.52.rates
  18.1 0.0 copy-done.3
  18.1 0.0 copy-start.9
  18.1 2.5 %inner_steps.1 = (f32[16,64,128]{2,1,0:T(8,128)S(1)}, f32[16,64,128]{2,1,0:T(8,128)S(1)}) custom-call(f32[16,128]{1,0:T(8,128)S(1)} %broadcast_in_dim.52.rates, f32[3,8,128]{2,1,0:T(8,128)S(1)} %pad_maximum_fusion.masks, f32[16,64,128]{2,1,0:T(8,128)S(1)} %copy-done.3, f32[2,16,64,128]{3,2,1,0:T(8,128)S(1)} %copy-done.1, ...), custom_call_target="tpu_custom_call" | custom-call | flops 2500000000 | bytes 9000000 | tf_op jit(solution)/shard_map/inner_steps/pallas_call | solution.py:425
  20.6 0.0 collective-permute-done.2.from_left
  20.6 0.0 collective-permute-done.3.from_right
  20.6 0.1 broadcast_in_dim.46.weights
  20.7 1.5 %columns.1 = (f32[16,64,128]{2,1,0:T(8,128)}, f32[8,64,128]{2,1,0:T(8,128)S(1)}, bf16[512,128]{1,0:T(8,128)(2,1)S(1)}, f32[64,128]{1,0:T(8,128)S(1)}) custom-call(f32[128,128]{1,0:T(8,128)S(1)} %broadcast_in_dim.46.weights, f32[3,8,128]{2,1,0:T(8,128)S(1)} %pad_maximum_fusion.masks, f32[16,64,128]{2,1,0:T(8,128)S(1)} %get-tuple-element.20.inner_last, ...), custom_call_target="tpu_custom_call" | custom-call | tf_op jit(solution)/shard_map/columns/pallas_call | solution.py:438
  22.2 8.9 %all_gather.3.gathered = bf16[2048,128]{1,0:T(8,128)(2,1)S(1)} all-gather(bf16[512,128]{1,0:T(8,128)(2,1)S(1)} %get-tuple-element.26), channel_id=1, replica_groups=mesh['grp'=4,'gx'=16,'gy'=4] {'grp'}, dimensions={0}, use_global_device_ids=true | all-gather | bytes 655360 | tf_op jit(solution)/shard_map/all_gather | solution.py:545
  31.2 0.0 copy-done.9
  31.2 0.1 broadcast_in_dim.55.heat
  31.2 4.0 %remap.1 = (f32[8,64,128]{2,1,0:T(8,128)}, f32[64,128]{1,0:T(8,128)}) custom-call(s32[833]{0:T(1024)S(1)} %pad_add_fusion.words, f32[8,128]{1,0:T(8,128)S(1)} %broadcast_in_dim.55.heat, bf16[2048,128]{1,0:T(8,128)(2,1)S(1)} %all_gather.3.gathered, bf16[64,128,128]{2,1,0:T(8,128)(2,1)S(1)} %turn_blocks.1.weights, f32[8,64,128]{2,1,0:T(8,128)S(1)} %get-tuple-element.27.fluxes, ...), custom_call_target="tpu_custom_call" | custom-call | tf_op jit(solution)/shard_map/remap/pallas_call | solution.py:478
  (8 shorter events, 0.0 us)
Async XLA Ops:
  0.6 8.2 %copy-start.1 = (f32[2,16,64,128]{3,2,1,0:T(8,128)S(1)}, f32[2,16,64,128]{3,2,1,0:T(8,128)}, u32[]{:S(2)}) copy-start(f32[2,16,64,128]{3,2,1,0:T(8,128)} %winds.5) | copy-start | bytes 3145732
  0.6 8.1 %copy-start.2 = (f32[16,64,128]{2,1,0:T(8,128)S(1)}, f32[16,64,128]{2,1,0:T(8,128)}, u32[]{:S(2)}) copy-start(f32[16,64,128]{2,1,0:T(8,128)} %state.5) | copy-start | bytes 1572868
  1.8 7.9 %copy-start.7 = (f32[2,16]{1,0:T(2,128)S(1)}, f32[2,16]{1,0:T(2,128)}, u32[]{:S(2)}) copy-start(f32[2,16]{1,0:T(2,128)} %param.11) | copy-start | bytes 388
  1.9 7.9 %copy-start.4 = (f32[8,16]{1,0:T(8,128)S(1)}, f32[8,16]{1,0:T(8,128)}, u32[]{:S(2)}) copy-start(f32[8,16]{1,0:T(8,128)} %param.12) | copy-start | bytes 1540
  1.9 8.0 %copy-start.5 = (s32[1,1,64,6]{2,1,3,0:T(1,128)S(1)}, s32[1,1,64,6]{2,1,3,0:T(1,128)}, u32[]{:S(2)}) copy-start(s32[1,1,64,6]{2,1,3,0:T(1,128)} %param.15) | copy-start | bytes 4612
  1.9 8.0 %copy-start.6 = (s32[1,1,64,6]{2,1,3,0:T(1,128)S(1)}, s32[1,1,64,6]{2,1,3,0:T(1,128)}, u32[]{:S(2)}) copy-start(s32[1,1,64,6]{2,1,3,0:T(1,128)} %param.16) | copy-start | bytes 4612
  1.9 8.3 %copy-start.8 = (s32[1,1,64]{2,1,0:T(1,128)S(1)}, s32[1,1,64]{2,1,0:T(1,128)}, u32[]{:S(2)}) copy-start(s32[1,1,64]{2,1,0:T(1,128)} %param.17) | copy-start | bytes 772
  1.9 8.4 %copy-start = (bf16[64,128,128]{2,1,0:T(8,128)(2,1)S(1)}, bf16[64,128,128]{2,1,0:T(8,128)(2,1)}, u32[]{:S(2)}) copy-start(bf16[64,128,128]{2,1,0:T(8,128)(2,1)} %blocks.1) | copy-start | bytes 6291460
  1.9 9.4 %collective-permute-start = (bf16[256,128]{1,0:T(8,128)(2,1)S(1)}, bf16[256,128]{1,0:T(8,128)(2,1)S(1)}, u32[]{:S(2)}, u32[]{:S(2)}) collective-permute-start(bf16[256,128]{1,0:T(8,128)(2,1)S(1)} %get-tuple-element.17), channel_id=1, source_target_pairs={{0,252},{4,0},{8,4},{12,8},{16,12},{20,16},{24,20},{28,24},{32,28}... | collective-permute-start | bytes 196616 | tf_op jit(solution)/shard_map/ppermute | solution.py:531
  8.8 6.2 %collective-permute-start.1 = (bf16[256,128]{1,0:T(8,128)(2,1)S(1)}, bf16[256,128]{1,0:T(8,128)(2,1)S(1)}, u32[]{:S(2)}, u32[]{:S(2)}) collective-permute-start(bf16[256,128]{1,0:T(8,128)(2,1)S(1)} %get-tuple-element.18), channel_id=1, source_target_pairs={{0,4},{4,8},{8,12},{12,16},{16,20},{20,24},{24,28},{28,32},{32,36}... | collective-permute-start | bytes 196616 | tf_op jit(solution)/shard_map/ppermute | solution.py:531
  10.4 7.8 %copy-start.3 = (f32[16,64,128]{2,1,0:T(8,128)S(1)}, f32[16,64,128]{2,1,0:T(8,128)}, u32[]{:S(2)}) copy-start(f32[16,64,128]{2,1,0:T(8,128)} %state.5) | copy-start | bytes 1572868
  15.2 5.4 %collective-permute-start.2 = (bf16[144,128]{1,0:T(8,128)(2,1)S(1)}, bf16[144,128]{1,0:T(8,128)(2,1)S(1)}, u32[]{:S(2)}, u32[]{:S(2)}) collective-permute-start(bf16[144,128]{1,0:T(8,128)(2,1)S(1)} %get-tuple-element.23), channel_id=1, source_target_pairs={{0,1},{1,2},{2,3},{3,0},{4,5},{5,6},{6,7},{7,4},{8,9},{9,10},{10,1... | collective-permute-start | bytes 110600 | tf_op jit(solution)/shard_map/ppermute | solution.py:531
  16.5 4.1 %collective-permute-start.3 = (bf16[144,128]{1,0:T(8,128)(2,1)S(1)}, bf16[144,128]{1,0:T(8,128)(2,1)S(1)}, u32[]{:S(2)}, u32[]{:S(2)}) collective-permute-start(bf16[144,128]{1,0:T(8,128)(2,1)S(1)} %get-tuple-element.24), channel_id=1, source_target_pairs={{0,3},{1,0},{2,1},{3,2},{4,7},{5,4},{6,5},{7,6},{8,11},{9,8},{10,9... | collective-permute-start | bytes 110600 | tf_op jit(solution)/shard_map/ppermute | solution.py:531
  18.1 13.0 %copy-start.9 = (f32[8]{0:T(128)S(1)}, f32[8]{0:T(128)}, u32[]{:S(2)}) copy-start(f32[8]{0:T(128)} %param.13) | copy-start | bytes 100

commit v6 on v5

--- a/solution.py
+++ b/solution.py
@@ -14,7 +14,7 @@
 TILES = ROWS // 8
 BASE = 16
 DEEP = ROWS + 32
-UNROLL = 4
+UNROLL = 8
 FLUX_ROWS = 32
 CHUNK = 32
 F32 = jnp.float32
@@ -40,8 +40,10 @@
     fetches = [
         pltpu.make_async_copy(source, target, sems.at[i])
         for i, (source, target) in enumerate((
-            (winds.at[:, :, first], wi_top),
-            (winds.at[:, :, last], wi_low),
+            (winds.at[0, :, first], wi_top.at[0]),
+            (winds.at[1, :, first], wi_top.at[1]),
+            (winds.at[0, :, last], wi_low.at[0]),
+            (winds.at[1, :, last], wi_low.at[1]),
             (state.at[:, first], st_top),
             (state.at[:, last], st_low),
         ))
@@ -186,8 +188,8 @@
 
 
 def columns_kernel(weights, masks, inner_last, inner_total, strip0, from_left, from_right,
-                   state_out, fluxes, rounded, top,
-                   ready, lefts, rights, beyond, extras, left_winds, right_winds, left, right, extra_total, sems):
+                   ready, fluxes, rounded,
+                   lefts, rights, beyond, extras, left_winds, right_winds, left, right, extra_total):
     upper = sub_ids() < 4
     n = ROWS + 8
     own = slice(BASE, BASE + ROWS)
@@ -222,25 +224,24 @@
         right_winds[1, r] = jnp.where(first, strip0[2, r], b * side_one)
     left_rate = jnp.where(first, rate * side_one, rate)
     right_rate = jnp.where(first, rate, rate * side_one)
-    for step in range(SUBSTEPS - 1):
-        for t in range(TILES + 1):
-            r, k = BASE + 8 * t, slice(8 * t, 8 * t + 8)
-            new = []
-            for strip, wind, d in ((lefts[step], left_winds, left_rate), (rights[step], right_winds, right_rate)):
-                if t < TILES:
-                    s, no, so = strip[r : r + 8], strip[r - 1 : r + 7], strip[r + 1 : r + 9]
-                else:
-                    s, no, so = halo_rows(lambda r: strip[r : r + 8], upper)
-                    d = d * row_one
-                w, e = pltpu.roll(s, 1, 1), pltpu.roll(s, COLS - 1, 1)
-                new.append(stencil(s, no, so, w, e, wind[0, k], wind[1, k], d, 1.0 - 4.0 * d))
-            if step < SUBSTEPS - 2:
-                put(lefts[step + 1], t, new[0])
-                put(rights[step + 1], t, new[1])
-            beyond[step + 1][k] = jnp.where(first, new[0], new[1])
-
     for step in range(SUBSTEPS):
         last = step == SUBSTEPS - 1
+        if not last:
+            for t in range(TILES + 1):
+                r, k = BASE + 8 * t, slice(8 * t, 8 * t + 8)
+                new = []
+                for strip, wind, d in ((lefts[step], left_winds, left_rate), (rights[step], right_winds, right_rate)):
+                    if t < TILES:
+                        s, no, so = strip[r : r + 8], strip[r - 1 : r + 7], strip[r + 1 : r + 9]
+                    else:
+                        s, no, so = halo_rows(lambda r: strip[r : r + 8], upper)
+                        d = d * row_one
+                    w, e = pltpu.roll(s, 1, 1), pltpu.roll(s, COLS - 1, 1)
+                    new.append(stencil(s, no, so, w, e, wind[0, k], wind[1, k], d, 1.0 - 4.0 * d))
+                if step < SUBSTEPS - 2:
+                    put(lefts[step + 1], t, new[0])
+                    put(rights[step + 1], t, new[1])
+                beyond[step + 1][k] = jnp.where(first, new[0], new[1])
         for t in range(TILES if last else TILES + 1):
             r, k = BASE + 8 * t, slice(8 * t, 8 * t + 8)
             side = beyond[step][k]
@@ -263,17 +264,13 @@
         lanes = lax.broadcasted_iota(jnp.int32, x.shape, 1)
         return jnp.where((lanes < 4) | (lanes >= COLS - 4), pltpu.roll(x, COLS - 4 - 8 * l, 1), 0.0)
 
-    for l in range(LEVELS):
-        ready[l] = inner_last[l] + edges(extras[SUBSTEPS - 1][own], l)
-
-    send = pltpu.make_async_copy(ready, state_out, sems.at[0])
-    send.start()
-
     def flux(t, carry):
         r = pl.multiple_of(FLUX_ROWS * t, FLUX_ROWS)
         out = pl.ds(r, FLUX_ROWS)
+        inner = pl.ds(BASE + r, FLUX_ROWS)
         sums = [None] * FIELDS
         for l in range(LEVELS):
+            ready[l, out, :] = inner_last[l, out, :] + edges(extras[SUBSTEPS - 1][inner, :], l)
             x = inner_total[l, out, :] + edges(extra_total[out, :], l)
             for f in range(FIELDS):
                 k = f * LEVELS + l
@@ -286,8 +283,6 @@
         return carry
 
     lax.fori_loop(0, ROWS // FLUX_ROWS, flux, 0)
-    top[...] = ready[0]
-    send.wait()
 
 
 def turn_blocks_kernel(blocks, turned):
@@ -298,11 +293,13 @@
     lax.fori_loop(0, blocks.shape[0], turn, 0, unroll=8)
 
 
-def remap_kernel(words, heat, gathered, weights, fluxes, top, flux_out, boundary_out,
-                 table, patches, remapped, surface, table_sem, out_sems, flux_sems, surface_sems):
+def remap_kernel(words, heat, gathered, weights, fluxes, field, state_out, flux_out, boundary_out,
+                 table, patches, remapped, surface, state_sem, table_sem, out_sems, flux_sems, surface_sems):
     size = FIELDS * ROWS
     fetch = pltpu.make_async_copy(words, table, table_sem.at[0])
     fetch.start()
+    keep = pltpu.make_async_copy(field, state_out, state_sem.at[0])
+    keep.start()
     patches[...] = gathered[0 : 3 * size].astype(F32)
     fetch.wait()
     is_ocean = table[table.shape[0] - 1] == 1
@@ -330,7 +327,7 @@
                     jnp.concatenate(picked, 1), jnp.concatenate(chosen, 0), preferred_element_type=F32
                 )
                 remapped[:, o, :] = total * table[o].astype(F32)
-            warmth = top[at, :]
+            warmth = field[0, at, :]
             for f in range(FIELDS):
                 warmth = warmth + heat[f : f + 1] * remapped[f, at, :]
             surface[at, :] = warmth
@@ -354,6 +351,8 @@
         for copy in copies:
             copy.wait()
 
+    keep.wait()
+
 
 WIDE = pltpu.CompilerParams(vmem_limit_bytes=53 * 2**20 + 5 * 2**17)
 LIMIT = pltpu.CompilerParams(vmem_limit_bytes=16 * 2**20)
@@ -382,7 +381,7 @@
             *[pltpu.VMEM((LEVELS, 8, COLS), F32)] * 2,
             *[pltpu.VMEM((2, LEVELS, 8, COLS), F32)] * 2,
             *[pltpu.VMEM(SHEET.shape, F32)] * 2,
-            pltpu.SemaphoreType.DMA((4,)),
+            pltpu.SemaphoreType.DMA((6,)),
         ],
         compiler_params=WIDE,
         cost_estimate=cost(1.1),
@@ -438,15 +437,13 @@
     return pl.pallas_call(
         columns_kernel,
         in_specs=[VMEM] * 7,
-        out_specs=[ANY] + [VMEM] * 3,
+        out_specs=[VMEM] * 3,
         out_shape=[
             f32(LEVELS, ROWS, COLS),
             f32(FIELDS, ROWS, COLS),
             jax.ShapeDtypeStruct((FIELDS * ROWS, COLS), BF16),
-            f32(ROWS, COLS),
         ],
         scratch_shapes=[
-            pltpu.VMEM((LEVELS, ROWS, COLS), F32),
             [pltpu.VMEM((DEEP, COLS), F32)] * 3,
             [pltpu.VMEM((DEEP, COLS), F32)] * 3,
             [pltpu.VMEM((N, COLS), F32)] * 4,
@@ -454,7 +451,6 @@
             *[pltpu.VMEM((2, N, COLS), F32)] * 2,
             *[pltpu.VMEM((2 * N, COLS), F32)] * 2,
             pltpu.VMEM((ROWS, COLS), F32),
-            pltpu.SemaphoreType.DMA((1,)),
         ],
         compiler_params=LIMIT,
         name="columns",
@@ -473,18 +469,19 @@
     )(blocks)
 
 
-def remap(table, heat, gathered, weights, fluxes, top):
+def remap(table, heat, gathered, weights, fluxes, field):
     chunks = ROWS // CHUNK
     return pl.pallas_call(
         remap_kernel,
         in_specs=[ANY] + [VMEM] * 5,
-        out_specs=[ANY] * 2,
-        out_shape=[f32(FIELDS, ROWS, COLS), f32(ROWS, COLS)],
+        out_specs=[ANY] * 3,
+        out_shape=[f32(LEVELS, ROWS, COLS), f32(FIELDS, ROWS, COLS), f32(ROWS, COLS)],
         scratch_shapes=[
             pltpu.SMEM(table.shape, jnp.int32),
             pltpu.VMEM((3 * FIELDS * ROWS, COLS), F32),
             pltpu.VMEM((FIELDS, ROWS, COLS), F32),
             pltpu.VMEM((ROWS, COLS), F32),
+            pltpu.SemaphoreType.DMA((1,)),
             pltpu.SemaphoreType.DMA((1,)),
             pltpu.SemaphoreType.DMA((2,)),
             pltpu.SemaphoreType.DMA((chunks,)),
@@ -492,7 +489,7 @@
         ],
         compiler_params=LIMIT,
         name="remap",
-    )(table, heat, gathered, weights, fluxes, top)
+    )(table, heat, gathered, weights, fluxes, field)
 
 
 def body(
@@ -539,13 +536,11 @@
     from_right = ring(to_left, "gy", -1)
     inner_last, inner_total = inner_steps(rates, masks, state, winds, halo)
     turned = turn_blocks(remap_blocks)
-    state_out, fluxes, rounded, top_level = columns(
+    field, fluxes, rounded = columns(
         weights, masks, inner_last, inner_total, strip0, from_left, from_right
     )
     gathered = lax.all_gather(rounded, "grp", axis=0, tiled=True)
-    fluxes, boundary = remap(
-        table, heat, gathered, turned, fluxes, top_level
-    )
+    state_out, fluxes, boundary = remap(table, heat, gathered, turned, fluxes, field)
     return state_out, boundary, fluxes
 
 

time: 35.4 us -> 34.7 us (0.980)
  Pallas kernels: 11.3 us -> 10.2 us
    pallas_call x1, Pallas kernels: 2.45 us -> 1.86 us  [inner_steps(): pl.pallas_call(inner_steps_kernel, in_specs=[VMEM] * 5, out_specs=[VMEM]...]
    pallas_call x1, Pallas kernels: 1.51 us -> 1.03 us  [columns(): pl.pallas_call(columns_kernel, in_specs=[VMEM] * 7, out_specs=[VMEM] * 3,...]
  transfers between devices with their start and end apart: 4 -> 4, of which waited for: 1 -> 1; matrix products, arithmetic and copies ran while one was open for 2% -> 2% of each run, Pallas kernels for 12% -> 11%
where the time goes in v6:
time: 34.7 us; the launch traced here: 34.5 us
  Pallas kernels  10.2 us (29%)
  starting transfers between devices  9.73 us (28%)
  blocking collectives  9.28 us (27%)
  waiting for transfers between devices  3.66 us (11%)
  between operations  0.87 us (3%)
  local copies, waits for them, and re-layouts  0.58 us (2%)
    ppermute x4, starting transfers between devices, ring(): lax.ppermute(x, axis, [(i, (i + shift) % count) for i in range(count)])  9.73 us
    all_gather x1, blocking collectives, body(): gathered = lax.all_gather(rounded, 'grp', axis=0, tiled=True)  9.28 us
    pallas_call x1, Pallas kernels, remap(): pl.pallas_call(remap_kernel, in_specs=[ANY] + [VMEM] * 5, out_specs=[ANY]...  4.01 us
    ppermute x4, waiting for transfers between devices, ring(): lax.ppermute(x, axis, [(i, (i + shift) % count) for i in range(count)])  3.66 us
    pallas_call x1, Pallas kernels, inner_steps(): pl.pallas_call(inner_steps_kernel, in_specs=[VMEM] * 5, out_specs=[VMEM]...  1.86 us
    pallas_call x1, Pallas kernels, edge_rows(): pl.pallas_call(edge_rows_kernel, in_specs=[HBM, HBM], out_specs=[VMEM, VM...  1.21 us
    pallas_call x1, Pallas kernels, columns(): pl.pallas_call(columns_kernel, in_specs=[VMEM] * 7, out_specs=[VMEM] * 3,...  1.03 us
    pallas_call x1, Pallas kernels, turn_blocks(): pl.pallas_call(turn_blocks_kernel, in_specs=[VMEM], out_specs=VMEM, out_s...  0.98 us
  transfers between devices with their start and end apart: 4, of which 1 were waited for; matrix products, arithmetic and copies ran while one was open for 2% of the time, Pallas kernels for 11%

profile of v6, /device:TPU:5, one launch (start us, length us, event | category | flops | bytes accessed | tf_op | source)
XLA Modules:
  0.0 34.5 jit_solution(11107707528015230175)
XLA Ops:
  0.6 0.0 copy-start.1
  0.6 0.0 copy-start.2
  0.7 1.2 %edge_rows.1 = (bf16[256,128]{1,0:T(8,128)(2,1)S(1)}, bf16[256,128]{1,0:T(8,128)(2,1)S(1)}) custom-call(f32[16,64,128]{2,1,0:T(8,128)} %state.5, f32[2,16,64,128]{3,2,1,0:T(8,128)} %winds.5), custom_call_target="tpu_custom_call" | custom-call | flops 1100000000 | bytes 3960000 | tf_op jit(solution)/shard_map/edge_rows/pallas_call | solution.py:375
  1.9 0.0 copy-start.7
  1.9 0.0 copy-start.4
  1.9 0.0 copy-start.5
  1.9 0.0 copy-start.6
  1.9 0.0 copy-start.8
  1.9 0.0 copy-start
  1.9 6.9 %collective-permute-start = (bf16[256,128]{1,0:T(8,128)(2,1)S(1)}, bf16[256,128]{1,0:T(8,128)(2,1)S(1)}, u32[]{:S(2)}, u32[]{:S(2)}) collective-permute-start(bf16[256,128]{1,0:T(8,128)(2,1)S(1)} %get-tuple-element.17), channel_id=1, source_target_pairs={{0,252},{4,0},{8,4},{12,8},{16,12},{20,16},{24,20},{28,24},{32,28}... | collective-permute-start | bytes 196616 | tf_op jit(solution)/shard_map/ppermute | solution.py:528
  8.8 0.0 collective-permute-start.1
  8.8 0.0 copy-done.1
  8.8 0.0 copy-done.2
  8.8 0.9 %own_strips.1.own = f32[3,64,128]{2,1,0:T(8,128)S(1)} custom-call(f32[16,64,128]{2,1,0:T(8,128)S(1)} %copy-done.2, f32[2,16,64,128]{3,2,1,0:T(8,128)S(1)} %copy-done.1), custom_call_target="tpu_custom_call" | custom-call | flops 1000000000 | bytes 3600000 | tf_op jit(solution)/shard_map/own_strips/pallas_call | solution.py:393
  9.8 0.0 copy-done.7
  9.8 0.0 copy-done.4
  9.8 0.1 broadcast_in_dim.48
  9.9 0.0 copy-done.5
  9.9 0.0 copy-done.6
  9.9 0.1 broadcast_in_dim.54
  10.0 0.1 mul.17
  10.1 0.1 add_bitcast_fusion
  10.2 0.0 copy-done.8
  10.2 0.1 pad_add_fusion.words
  10.3 0.1 iota.13
  10.4 0.0 copy-done
  10.4 0.0 copy-start.3
  10.4 1.0 %turn_blocks.1.weights = bf16[64,128,128]{2,1,0:T(8,128)(2,1)S(1)} custom-call(bf16[64,128,128]{2,1,0:T(8,128)(2,1)S(1)} %copy-done), custom_call_target="tpu_custom_call" | custom-call | flops 1000000000 | bytes 3600000 | tf_op jit(solution)/shard_map/turn_blocks/pallas_call | solution.py:461
  11.4 0.0 collective-permute-done.from_below
  11.4 3.7 %collective-permute-done.1.from_above = bf16[256,128]{1,0:T(8,128)(2,1)S(1)} collective-permute-done((bf16[256,128]{1,0:T(8,128)(2,1)S(1)}, bf16[256,128]{1,0:T(8,128)(2,1)S(1)}, u32[]{:S(2)}, u32[]{:S(2)}) %collective-permute-start.1) | collective-permute-done | bytes 65568 | tf_op jit(solution)/shard_map/ppermute | solution.py:528
  15.0 0.2 edge_columns.1
  15.2 1.3 %collective-permute-start.2 = (bf16[144,128]{1,0:T(8,128)(2,1)S(1)}, bf16[144,128]{1,0:T(8,128)(2,1)S(1)}, u32[]{:S(2)}, u32[]{:S(2)}) collective-permute-start(bf16[144,128]{1,0:T(8,128)(2,1)S(1)} %get-tuple-element.23), channel_id=1, source_target_pairs={{0,1},{1,2},{2,3},{3,0},{4,5},{5,6},{6,7},{7,4},{8,9},{9,10},{10,1... | collective-permute-start | bytes 110600 | tf_op jit(solution)/shard_map/ppermute | solution.py:528
  16.6 1.5 %collective-permute-start.3 = (bf16[144,128]{1,0:T(8,128)(2,1)S(1)}, bf16[144,128]{1,0:T(8,128)(2,1)S(1)}, u32[]{:S(2)}, u32[]{:S(2)}) collective-permute-start(bf16[144,128]{1,0:T(8,128)(2,1)S(1)} %get-tuple-element.24), channel_id=1, source_target_pairs={{0,3},{1,0},{2,1},{3,2},{4,7},{5,4},{6,5},{7,6},{8,11},{9,8},{10,9... | collective-permute-start | bytes 110600 | tf_op jit(solution)/shard_map/ppermute | solution.py:528
  18.1 0.1 broadcast_in_dim.55.rates
  18.2 0.0 copy-done.3
  18.2 0.0 copy-start.9
  18.2 1.9 %inner_steps.1 = (f32[16,64,128]{2,1,0:T(8,128)S(1)}, f32[16,64,128]{2,1,0:T(8,128)S(1)}) custom-call(f32[16,128]{1,0:T(8,128)S(1)} %broadcast_in_dim.55.rates, f32[3,8,128]{2,1,0:T(8,128)S(1)} %pad_maximum_fusion.masks, f32[16,64,128]{2,1,0:T(8,128)S(1)} %copy-done.3, f32[2,16,64,128]{3,2,1,0:T(8,128)S(1)} %copy-done.1, ...), custom_call_target="tpu_custom_call" | custom-call | flops 2500000000 | bytes 9000000 | tf_op jit(solution)/shard_map/inner_steps/pallas_call | solution.py:424
  20.0 0.0 collective-permute-done.2.from_left
  20.0 0.0 collective-permute-done.3.from_right
  20.0 0.1 broadcast_in_dim.49.weights
  20.1 1.0 %columns.1 = (f32[16,64,128]{2,1,0:T(8,128)S(1)}, f32[8,64,128]{2,1,0:T(8,128)S(1)}, bf16[512,128]{1,0:T(8,128)(2,1)S(1)}) custom-call(f32[128,128]{1,0:T(8,128)S(1)} %broadcast_in_dim.49.weights, f32[3,8,128]{2,1,0:T(8,128)S(1)} %pad_maximum_fusion.masks, f32[16,64,128]{2,1,0:T(8,128)S(1)} %get-tuple-element.20.inner_last, ...), custom_call_target="tpu_custom_call" | custom-call | tf_op jit(solution)/shard_map/columns/pallas_call | solution.py:437
  21.2 9.3 %all_gather.3.gathered = bf16[2048,128]{1,0:T(8,128)(2,1)S(1)} all-gather(bf16[512,128]{1,0:T(8,128)(2,1)S(1)} %get-tuple-element.25), channel_id=1, replica_groups=mesh['grp'=4,'gx'=16,'gy'=4] {'grp'}, dimensions={0}, use_global_device_ids=true | all-gather | bytes 655360 | tf_op jit(solution)/shard_map/all_gather | solution.py:542
  30.4 0.0 copy-done.9
  30.4 0.1 broadcast_in_dim.47.heat
  30.5 4.0 %remap.1 = (f32[16,64,128]{2,1,0:T(8,128)}, f32[8,64,128]{2,1,0:T(8,128)}, f32[64,128]{1,0:T(8,128)}) custom-call(s32[833]{0:T(1024)S(1)} %pad_add_fusion.words, f32[8,128]{1,0:T(8,128)S(1)} %broadcast_in_dim.47.heat, bf16[2048,128]{1,0:T(8,128)(2,1)S(1)} %all_gather.3.gathered, bf16[64,128,128]{2,1,0:T(8,128)(2,1)S(1)} %turn_blocks.1.weights, ...), custom_call_target="tpu_custom_call" | custom-call | tf_op jit(solution)/shard_map/remap/pallas_call | solution.py:474
  (8 shorter events, 0.0 us)
Async XLA Ops:
  0.6 8.2 %copy-start.1 = (f32[2,16,64,128]{3,2,1,0:T(8,128)S(1)}, f32[2,16,64,128]{3,2,1,0:T(8,128)}, u32[]{:S(2)}) copy-start(f32[2,16,64,128]{3,2,1,0:T(8,128)} %winds.5) | copy-start | bytes 3145732
  0.6 8.2 %copy-start.2 = (f32[16,64,128]{2,1,0:T(8,128)S(1)}, f32[16,64,128]{2,1,0:T(8,128)}, u32[]{:S(2)}) copy-start(f32[16,64,128]{2,1,0:T(8,128)} %state.5) | copy-start | bytes 1572868
  1.9 7.9 %copy-start.7 = (f32[2,16]{1,0:T(2,128)S(1)}, f32[2,16]{1,0:T(2,128)}, u32[]{:S(2)}) copy-start(f32[2,16]{1,0:T(2,128)} %param.11) | copy-start | bytes 388
  1.9 7.9 %copy-start.4 = (f32[8,16]{1,0:T(8,128)S(1)}, f32[8,16]{1,0:T(8,128)}, u32[]{:S(2)}) copy-start(f32[8,16]{1,0:T(8,128)} %param.12) | copy-start | bytes 1540
  1.9 8.0 %copy-start.5 = (s32[1,1,64,6]{2,1,3,0:T(1,128)S(1)}, s32[1,1,64,6]{2,1,3,0:T(1,128)}, u32[]{:S(2)}) copy-start(s32[1,1,64,6]{2,1,3,0:T(1,128)} %param.15) | copy-start | bytes 4612
  1.9 8.0 %copy-start.6 = (s32[1,1,64,6]{2,1,3,0:T(1,128)S(1)}, s32[1,1,64,6]{2,1,3,0:T(1,128)}, u32[]{:S(2)}) copy-start(s32[1,1,64,6]{2,1,3,0:T(1,128)} %param.16) | copy-start | bytes 4612
  1.9 8.3 %copy-start.8 = (s32[1,1,64]{2,1,0:T(1,128)S(1)}, s32[1,1,64]{2,1,0:T(1,128)}, u32[]{:S(2)}) copy-start(s32[1,1,64]{2,1,0:T(1,128)} %param.17) | copy-start | bytes 772
  1.9 8.4 %copy-start = (bf16[64,128,128]{2,1,0:T(8,128)(2,1)S(1)}, bf16[64,128,128]{2,1,0:T(8,128)(2,1)}, u32[]{:S(2)}) copy-start(bf16[64,128,128]{2,1,0:T(8,128)(2,1)} %blocks.1) | copy-start | bytes 6291460
  1.9 9.4 %collective-permute-start = (bf16[256,128]{1,0:T(8,128)(2,1)S(1)}, bf16[256,128]{1,0:T(8,128)(2,1)S(1)}, u32[]{:S(2)}, u32[]{:S(2)}) collective-permute-start(bf16[256,128]{1,0:T(8,128)(2,1)S(1)} %get-tuple-element.17), channel_id=1, source_target_pairs={{0,252},{4,0},{8,4},{12,8},{16,12},{20,16},{24,20},{28,24},{32,28}... | collective-permute-start | bytes 196616 | tf_op jit(solution)/shard_map/ppermute | solution.py:528
  8.8 6.2 %collective-permute-start.1 = (bf16[256,128]{1,0:T(8,128)(2,1)S(1)}, bf16[256,128]{1,0:T(8,128)(2,1)S(1)}, u32[]{:S(2)}, u32[]{:S(2)}) collective-permute-start(bf16[256,128]{1,0:T(8,128)(2,1)S(1)} %get-tuple-element.18), channel_id=1, source_target_pairs={{0,4},{4,8},{8,12},{12,16},{16,20},{20,24},{24,28},{28,32},{32,36}... | collective-permute-start | bytes 196616 | tf_op jit(solution)/shard_map/ppermute | solution.py:528
  10.4 7.8 %copy-start.3 = (f32[16,64,128]{2,1,0:T(8,128)S(1)}, f32[16,64,128]{2,1,0:T(8,128)}, u32[]{:S(2)}) copy-start(f32[16,64,128]{2,1,0:T(8,128)} %state.5) | copy-start | bytes 1572868
  15.2 4.8 %collective-permute-start.2 = (bf16[144,128]{1,0:T(8,128)(2,1)S(1)}, bf16[144,128]{1,0:T(8,128)(2,1)S(1)}, u32[]{:S(2)}, u32[]{:S(2)}) collective-permute-start(bf16[144,128]{1,0:T(8,128)(2,1)S(1)} %get-tuple-element.23), channel_id=1, source_target_pairs={{0,1},{1,2},{2,3},{3,0},{4,5},{5,6},{6,7},{7,4},{8,9},{9,10},{10,1... | collective-permute-start | bytes 110600 | tf_op jit(solution)/shard_map/ppermute | solution.py:528
  16.6 3.5 %collective-permute-start.3 = (bf16[144,128]{1,0:T(8,128)(2,1)S(1)}, bf16[144,128]{1,0:T(8,128)(2,1)S(1)}, u32[]{:S(2)}, u32[]{:S(2)}) collective-permute-start(bf16[144,128]{1,0:T(8,128)(2,1)S(1)} %get-tuple-element.24), channel_id=1, source_target_pairs={{0,3},{1,0},{2,1},{3,2},{4,7},{5,4},{6,5},{7,6},{8,11},{9,8},{10,9... | collective-permute-start | bytes 110600 | tf_op jit(solution)/shard_map/ppermute | solution.py:528
  18.2 12.3 %copy-start.9 = (f32[8]{0:T(128)S(1)}, f32[8]{0:T(128)}, u32[]{:S(2)}) copy-start(f32[8]{0:T(128)} %param.13) | copy-start | bytes 100

commit v7 on v6

--- a/solution.py
+++ b/solution.py
@@ -14,7 +14,7 @@
 TILES = ROWS // 8
 BASE = 16
 DEEP = ROWS + 32
-UNROLL = 8
+UNROLL = 16
 FLUX_ROWS = 32
 CHUNK = 32
 F32 = jnp.float32
@@ -81,7 +81,7 @@
             strips[c, pl.ds(r, 8), :] = strip
         return carry
 
-    lax.fori_loop(0, TILES, row_tile, 0)
+    lax.fori_loop(0, TILES, row_tile, 0, unroll=8)
 
 
 def edge_columns_kernel(masks, from_below, from_above, own, halo, strip0, to_right, to_left,
@@ -290,7 +290,7 @@
         turned[i] = blocks[i].T
         return carry
 
-    lax.fori_loop(0, blocks.shape[0], turn, 0, unroll=8)
+    lax.fori_loop(0, blocks.shape[0], turn, 0, unroll=32)
 
 
 def remap_kernel(words, heat, gathered, weights, fluxes, field, state_out, flux_out, boundary_out,

time: 34.7 us -> 34.7 us (level)
  Pallas kernels: 10.2 us -> 8.91 us
  waiting for transfers between devices: 3.66 us -> 4.47 us
  blocking collectives: 9.28 us -> 9.78 us
    ppermute x4, waiting for transfers between devices: 3.66 us -> 4.47 us  [ring(): lax.ppermute(x, axis, [(i, (i + shift) % count) for i in range(count)])]
    all_gather x1, blocking collectives: 9.28 us -> 9.78 us  [body(): gathered = lax.all_gather(rounded, 'grp', axis=0, tiled=True)]
    pallas_call x1, Pallas kernels: 1.86 us -> 1.37 us  [inner_steps(): pl.pallas_call(inner_steps_kernel, in_specs=[VMEM] * 5, out_specs=[VMEM]...]
    pallas_call x1, Pallas kernels: 0.95 us -> 0.47 us  [own_strips(): pl.pallas_call(own_strips_kernel, in_specs=[VMEM, VMEM], out_specs=VMEM,...]
  transfers between devices with their start and end apart: 4 -> 4, of which waited for: 1 -> 1; matrix products, arithmetic and copies ran while one was open for 2% -> 2% of each run, Pallas kernels for 11% -> 7%
where the time goes in v7:
time: 34.7 us; the launch traced here: 34.5 us
  blocking collectives  9.78 us (28%)
  starting transfers between devices  9.73 us (28%)
  Pallas kernels  8.91 us (26%)
  waiting for transfers between devices  4.47 us (13%)
  between operations  0.87 us (3%)
  local copies, waits for them, and re-layouts  0.58 us (2%)
    all_gather x1, blocking collectives, body(): gathered = lax.all_gather(rounded, 'grp', axis=0, tiled=True)  9.78 us
    ppermute x4, starting transfers between devices, ring(): lax.ppermute(x, axis, [(i, (i + shift) % count) for i in range(count)])  9.73 us
    ppermute x4, waiting for transfers between devices, ring(): lax.ppermute(x, axis, [(i, (i + shift) % count) for i in range(count)])  4.47 us
    pallas_call x1, Pallas kernels, remap(): pl.pallas_call(remap_kernel, in_specs=[ANY] + [VMEM] * 5, out_specs=[ANY]...  4.01 us
    pallas_call x1, Pallas kernels, inner_steps(): pl.pallas_call(inner_steps_kernel, in_specs=[VMEM] * 5, out_specs=[VMEM]...  1.37 us
    pallas_call x1, Pallas kernels, edge_rows(): pl.pallas_call(edge_rows_kernel, in_specs=[HBM, HBM], out_specs=[VMEM, VM...  1.21 us
    pallas_call x1, Pallas kernels, columns(): pl.pallas_call(columns_kernel, in_specs=[VMEM] * 7, out_specs=[VMEM] * 3,...  1.03 us
  transfers between devices with their start and end apart: 4, of which 1 were waited for; matrix products, arithmetic and copies ran while one was open for 2% of the time, Pallas kernels for 7%

profile of v7, /device:TPU:5, one launch (start us, length us, event | category | flops | bytes accessed | tf_op | source)
XLA Modules:
  0.0 34.5 jit_solution(12233074152487303877)
XLA Ops:
  0.6 0.0 copy-start.1
  0.6 0.0 copy-start.2
  0.7 1.2 %edge_rows.1 = (bf16[256,128]{1,0:T(8,128)(2,1)S(1)}, bf16[256,128]{1,0:T(8,128)(2,1)S(1)}) custom-call(f32[16,64,128]{2,1,0:T(8,128)} %state.5, f32[2,16,64,128]{3,2,1,0:T(8,128)} %winds.5), custom_call_target="tpu_custom_call" | custom-call | flops 1100000000 | bytes 3960000 | tf_op jit(solution)/shard_map/edge_rows/pallas_call | solution.py:375
  1.9 0.0 copy-start.7
  1.9 0.0 copy-start.4
  1.9 0.0 copy-start.5
  1.9 0.0 copy-start.6
  1.9 0.0 copy-start.8
  1.9 0.0 copy-start
  1.9 6.9 %collective-permute-start = (bf16[256,128]{1,0:T(8,128)(2,1)S(1)}, bf16[256,128]{1,0:T(8,128)(2,1)S(1)}, u32[]{:S(2)}, u32[]{:S(2)}) collective-permute-start(bf16[256,128]{1,0:T(8,128)(2,1)S(1)} %get-tuple-element.17), channel_id=1, source_target_pairs={{0,252},{4,0},{8,4},{12,8},{16,12},{20,16},{24,20},{28,24},{32,28}... | collective-permute-start | bytes 196616 | tf_op jit(solution)/shard_map/ppermute | solution.py:528
  8.8 0.0 collective-permute-start.1
  8.8 0.0 copy-done.1
  8.8 0.0 copy-done.2
  8.8 0.5 %own_strips.1.own = f32[3,64,128]{2,1,0:T(8,128)S(1)} custom-call(f32[16,64,128]{2,1,0:T(8,128)S(1)} %copy-done.2, f32[2,16,64,128]{3,2,1,0:T(8,128)S(1)} %copy-done.1), custom_call_target="tpu_custom_call" | custom-call | flops 1000000000 | bytes 3600000 | tf_op jit(solution)/shard_map/own_strips/pallas_call | solution.py:393
  9.3 0.0 copy-done.7
  9.3 0.0 copy-done.4
  9.3 0.1 broadcast_in_dim.48
  9.4 0.0 copy-done.5
  9.4 0.0 copy-done.6
  9.5 0.1 broadcast_in_dim.54
  9.5 0.1 mul.17
  9.7 0.1 add_bitcast_fusion
  9.7 0.0 copy-done.8
  9.7 0.1 pad_add_fusion.words
  9.8 0.1 iota.13
  9.9 0.0 copy-done
  9.9 0.0 copy-start.3
  9.9 0.6 %turn_blocks.1.weights = bf16[64,128,128]{2,1,0:T(8,128)(2,1)S(1)} custom-call(bf16[64,128,128]{2,1,0:T(8,128)(2,1)S(1)} %copy-done), custom_call_target="tpu_custom_call" | custom-call | flops 1000000000 | bytes 3600000 | tf_op jit(solution)/shard_map/turn_blocks/pallas_call | solution.py:461
  10.6 0.0 collective-permute-done.from_below
  10.6 4.5 %collective-permute-done.1.from_above = bf16[256,128]{1,0:T(8,128)(2,1)S(1)} collective-permute-done((bf16[256,128]{1,0:T(8,128)(2,1)S(1)}, bf16[256,128]{1,0:T(8,128)(2,1)S(1)}, u32[]{:S(2)}, u32[]{:S(2)}) %collective-permute-start.1) | collective-permute-done | bytes 65568 | tf_op jit(solution)/shard_map/ppermute | solution.py:528
  15.0 0.2 edge_columns.1
  15.2 1.3 %collective-permute-start.2 = (bf16[144,128]{1,0:T(8,128)(2,1)S(1)}, bf16[144,128]{1,0:T(8,128)(2,1)S(1)}, u32[]{:S(2)}, u32[]{:S(2)}) collective-permute-start(bf16[144,128]{1,0:T(8,128)(2,1)S(1)} %get-tuple-element.23), channel_id=1, source_target_pairs={{0,1},{1,2},{2,3},{3,0},{4,5},{5,6},{6,7},{7,4},{8,9},{9,10},{10,1... | collective-permute-start | bytes 110600 | tf_op jit(solution)/shard_map/ppermute | solution.py:528
  16.6 1.5 %collective-permute-start.3 = (bf16[144,128]{1,0:T(8,128)(2,1)S(1)}, bf16[144,128]{1,0:T(8,128)(2,1)S(1)}, u32[]{:S(2)}, u32[]{:S(2)}) collective-permute-start(bf16[144,128]{1,0:T(8,128)(2,1)S(1)} %get-tuple-element.24), channel_id=1, source_target_pairs={{0,3},{1,0},{2,1},{3,2},{4,7},{5,4},{6,5},{7,6},{8,11},{9,8},{10,9... | collective-permute-start | bytes 110600 | tf_op jit(solution)/shard_map/ppermute | solution.py:528
  18.1 0.1 broadcast_in_dim.55.rates
  18.2 0.0 copy-done.3
  18.2 0.0 copy-start.9
  18.2 1.4 %inner_steps.1 = (f32[16,64,128]{2,1,0:T(8,128)S(1)}, f32[16,64,128]{2,1,0:T(8,128)S(1)}) custom-call(f32[16,128]{1,0:T(8,128)S(1)} %broadcast_in_dim.55.rates, f32[3,8,128]{2,1,0:T(8,128)S(1)} %pad_maximum_fusion.masks, f32[16,64,128]{2,1,0:T(8,128)S(1)} %copy-done.3, f32[2,16,64,128]{3,2,1,0:T(8,128)S(1)} %copy-done.1, ...), custom_call_target="tpu_custom_call" | custom-call | flops 2500000000 | bytes 9000000 | tf_op jit(solution)/shard_map/inner_steps/pallas_call | solution.py:424
  19.5 0.0 collective-permute-done.2.from_left
  19.5 0.0 collective-permute-done.3.from_right
  19.6 0.1 broadcast_in_dim.49.weights
  19.6 1.0 %columns.1 = (f32[16,64,128]{2,1,0:T(8,128)S(1)}, f32[8,64,128]{2,1,0:T(8,128)S(1)}, bf16[512,128]{1,0:T(8,128)(2,1)S(1)}) custom-call(f32[128,128]{1,0:T(8,128)S(1)} %broadcast_in_dim.49.weights, f32[3,8,128]{2,1,0:T(8,128)S(1)} %pad_maximum_fusion.masks, f32[16,64,128]{2,1,0:T(8,128)S(1)} %get-tuple-element.20.inner_last, ...), custom_call_target="tpu_custom_call" | custom-call | tf_op jit(solution)/shard_map/columns/pallas_call | solution.py:437
  20.7 9.8 %all_gather.3.gathered = bf16[2048,128]{1,0:T(8,128)(2,1)S(1)} all-gather(bf16[512,128]{1,0:T(8,128)(2,1)S(1)} %get-tuple-element.25), channel_id=1, replica_groups=mesh['grp'=4,'gx'=16,'gy'=4] {'grp'}, dimensions={0}, use_global_device_ids=true | all-gather | bytes 655360 | tf_op jit(solution)/shard_map/all_gather | solution.py:542
  30.4 0.0 copy-done.9
  30.4 0.1 broadcast_in_dim.47.heat
  30.5 4.0 %remap.1 = (f32[16,64,128]{2,1,0:T(8,128)}, f32[8,64,128]{2,1,0:T(8,128)}, f32[64,128]{1,0:T(8,128)}) custom-call(s32[833]{0:T(1024)S(1)} %pad_add_fusion.words, f32[8,128]{1,0:T(8,128)S(1)} %broadcast_in_dim.47.heat, bf16[2048,128]{1,0:T(8,128)(2,1)S(1)} %all_gather.3.gathered, bf16[64,128,128]{2,1,0:T(8,128)(2,1)S(1)} %turn_blocks.1.weights, ...), custom_call_target="tpu_custom_call" | custom-call | tf_op jit(solution)/shard_map/remap/pallas_call | solution.py:474
  (8 shorter events, 0.0 us)
Async XLA Ops:
  0.6 8.2 %copy-start.1 = (f32[2,16,64,128]{3,2,1,0:T(8,128)S(1)}, f32[2,16,64,128]{3,2,1,0:T(8,128)}, u32[]{:S(2)}) copy-start(f32[2,16,64,128]{3,2,1,0:T(8,128)} %winds.5) | copy-start | bytes 3145732
  0.6 8.2 %copy-start.2 = (f32[16,64,128]{2,1,0:T(8,128)S(1)}, f32[16,64,128]{2,1,0:T(8,128)}, u32[]{:S(2)}) copy-start(f32[16,64,128]{2,1,0:T(8,128)} %state.5) | copy-start | bytes 1572868
  1.9 7.4 %copy-start.7 = (f32[2,16]{1,0:T(2,128)S(1)}, f32[2,16]{1,0:T(2,128)}, u32[]{:S(2)}) copy-start(f32[2,16]{1,0:T(2,128)} %param.11) | copy-start | bytes 388
  1.9 7.5 %copy-start.4 = (f32[8,16]{1,0:T(8,128)S(1)}, f32[8,16]{1,0:T(8,128)}, u32[]{:S(2)}) copy-start(f32[8,16]{1,0:T(8,128)} %param.12) | copy-start | bytes 1540
  1.9 7.5 %copy-start.5 = (s32[1,1,64,6]{2,1,3,0:T(1,128)S(1)}, s32[1,1,64,6]{2,1,3,0:T(1,128)}, u32[]{:S(2)}) copy-start(s32[1,1,64,6]{2,1,3,0:T(1,128)} %param.15) | copy-start | bytes 4612
  1.9 7.5 %copy-start.6 = (s32[1,1,64,6]{2,1,3,0:T(1,128)S(1)}, s32[1,1,64,6]{2,1,3,0:T(1,128)}, u32[]{:S(2)}) copy-start(s32[1,1,64,6]{2,1,3,0:T(1,128)} %param.16) | copy-start | bytes 4612
  1.9 7.8 %copy-start.8 = (s32[1,1,64]{2,1,0:T(1,128)S(1)}, s32[1,1,64]{2,1,0:T(1,128)}, u32[]{:S(2)}) copy-start(s32[1,1,64]{2,1,0:T(1,128)} %param.17) | copy-start | bytes 772
  1.9 8.0 %copy-start = (bf16[64,128,128]{2,1,0:T(8,128)(2,1)S(1)}, bf16[64,128,128]{2,1,0:T(8,128)(2,1)}, u32[]{:S(2)}) copy-start(bf16[64,128,128]{2,1,0:T(8,128)(2,1)} %blocks.1) | copy-start | bytes 6291460
  1.9 8.6 %collective-permute-start = (bf16[256,128]{1,0:T(8,128)(2,1)S(1)}, bf16[256,128]{1,0:T(8,128)(2,1)S(1)}, u32[]{:S(2)}, u32[]{:S(2)}) collective-permute-start(bf16[256,128]{1,0:T(8,128)(2,1)S(1)} %get-tuple-element.17), channel_id=1, source_target_pairs={{0,252},{4,0},{8,4},{12,8},{16,12},{20,16},{24,20},{28,24},{32,28}... | collective-permute-start | bytes 196616 | tf_op jit(solution)/shard_map/ppermute | solution.py:528
  8.8 6.2 %collective-permute-start.1 = (bf16[256,128]{1,0:T(8,128)(2,1)S(1)}, bf16[256,128]{1,0:T(8,128)(2,1)S(1)}, u32[]{:S(2)}, u32[]{:S(2)}) collective-permute-start(bf16[256,128]{1,0:T(8,128)(2,1)S(1)} %get-tuple-element.18), channel_id=1, source_target_pairs={{0,4},{4,8},{8,12},{12,16},{16,20},{20,24},{24,28},{28,32},{32,36}... | collective-permute-start | bytes 196616 | tf_op jit(solution)/shard_map/ppermute | solution.py:528
  9.9 8.3 %copy-start.3 = (f32[16,64,128]{2,1,0:T(8,128)S(1)}, f32[16,64,128]{2,1,0:T(8,128)}, u32[]{:S(2)}) copy-start(f32[16,64,128]{2,1,0:T(8,128)} %state.5) | copy-start | bytes 1572868
  15.2 4.3 %collective-permute-start.2 = (bf16[144,128]{1,0:T(8,128)(2,1)S(1)}, bf16[144,128]{1,0:T(8,128)(2,1)S(1)}, u32[]{:S(2)}, u32[]{:S(2)}) collective-permute-start(bf16[144,128]{1,0:T(8,128)(2,1)S(1)} %get-tuple-element.23), channel_id=1, source_target_pairs={{0,1},{1,2},{2,3},{3,0},{4,5},{5,6},{6,7},{7,4},{8,9},{9,10},{10,1... | collective-permute-start | bytes 110600 | tf_op jit(solution)/shard_map/ppermute | solution.py:528
  16.6 3.0 %collective-permute-start.3 = (bf16[144,128]{1,0:T(8,128)(2,1)S(1)}, bf16[144,128]{1,0:T(8,128)(2,1)S(1)}, u32[]{:S(2)}, u32[]{:S(2)}) collective-permute-start(bf16[144,128]{1,0:T(8,128)(2,1)S(1)} %get-tuple-element.24), channel_id=1, source_target_pairs={{0,3},{1,0},{2,1},{3,2},{4,7},{5,4},{6,5},{7,6},{8,11},{9,8},{10,9... | collective-permute-start | bytes 110600 | tf_op jit(solution)/shard_map/ppermute | solution.py:528
  18.2 12.3 %copy-start.9 = (f32[8]{0:T(128)S(1)}, f32[8]{0:T(128)}, u32[]{:S(2)}) copy-start(f32[8]{0:T(128)} %param.13) | copy-start | bytes 100

commit v8 on v7

--- a/solution.py
+++ b/solution.py
@@ -16,7 +16,7 @@
 DEEP = ROWS + 32
 UNROLL = 16
 FLUX_ROWS = 32
-CHUNK = 32
+PARTS = ((0, 48), (48, 64))
 F32 = jnp.float32
 BF16 = jnp.bfloat16
 
@@ -307,16 +307,15 @@
     @pl.when(is_ocean)
     def _():
         def sends(i):
-            at = pl.ds(pl.multiple_of(i * CHUNK, CHUNK), CHUNK)
+            start, end = PARTS[i]
+            at = pl.ds(start, end - start)
             return (
                 pltpu.make_async_copy(remapped.at[:, at], flux_out.at[:, at], flux_sems.at[i]),
                 pltpu.make_async_copy(surface.at[at], boundary_out.at[at], surface_sems.at[i]),
             )
 
-        def chunk(i, carry):
-            at = pl.ds(pl.multiple_of(i * CHUNK, CHUNK), CHUNK)
-            for j in range(CHUNK):
-                o = i * CHUNK + j
+        for i, (begin, end) in enumerate(PARTS):
+            for o in range(begin, end):
                 picked, chosen = [], []
                 for entry in range(INTERSECTIONS):
                     at_entry = ROWS + 2 * ROWS * entry + o
@@ -327,16 +326,14 @@
                     jnp.concatenate(picked, 1), jnp.concatenate(chosen, 0), preferred_element_type=F32
                 )
                 remapped[:, o, :] = total * table[o].astype(F32)
+            at = slice(begin, end)
             warmth = field[0, at, :]
             for f in range(FIELDS):
                 warmth = warmth + heat[f : f + 1] * remapped[f, at, :]
             surface[at, :] = warmth
             for send in sends(i):
                 send.start()
-            return carry
-
-        lax.fori_loop(0, ROWS // CHUNK, chunk, 0)
-        for i in range(ROWS // CHUNK):
+        for i in range(len(PARTS)):
             for send in sends(i):
                 send.wait()
 
@@ -470,7 +467,7 @@
 
 
 def remap(table, heat, gathered, weights, fluxes, field):
-    chunks = ROWS // CHUNK
+    chunks = len(PARTS)
     return pl.pallas_call(
         remap_kernel,
         in_specs=[ANY] + [VMEM] * 5,

time: 34.7 us -> 34.7 us (level)
  no operation moved by 1% of the time
where the time goes in v8:
time: 34.7 us; the launch traced here: 34.4 us
  blocking collectives  9.78 us (28%)
  starting transfers between devices  9.73 us (28%)
  Pallas kernels  8.83 us (25%)
  waiting for transfers between devices  4.47 us (13%)
  between operations  0.87 us (3%)
  local copies, waits for them, and re-layouts  0.58 us (2%)
    all_gather x1, blocking collectives, body(): gathered = lax.all_gather(rounded, 'grp', axis=0, tiled=True)  9.78 us
    ppermute x4, starting transfers between devices, ring(): lax.ppermute(x, axis, [(i, (i + shift) % count) for i in range(count)])  9.73 us
    ppermute x4, waiting for transfers between devices, ring(): lax.ppermute(x, axis, [(i, (i + shift) % count) for i in range(count)])  4.47 us
    pallas_call x1, Pallas kernels, remap(): pl.pallas_call(remap_kernel, in_specs=[ANY] + [VMEM] * 5, out_specs=[ANY]...  3.93 us
    pallas_call x1, Pallas kernels, inner_steps(): pl.pallas_call(inner_steps_kernel, in_specs=[VMEM] * 5, out_specs=[VMEM]...  1.37 us
    pallas_call x1, Pallas kernels, edge_rows(): pl.pallas_call(edge_rows_kernel, in_specs=[HBM, HBM], out_specs=[VMEM, VM...  1.21 us
    pallas_call x1, Pallas kernels, columns(): pl.pallas_call(columns_kernel, in_specs=[VMEM] * 7, out_specs=[VMEM] * 3,...  1.03 us
  transfers between devices with their start and end apart: 4, of which 1 were waited for; matrix products, arithmetic and copies ran while one was open for 2% of the time, Pallas kernels for 7%

profile of v8, /device:TPU:5, one launch (start us, length us, event | category | flops | bytes accessed | tf_op | source)
XLA Modules:
  0.0 34.4 jit_solution(2898961554147602772)
XLA Ops:
  0.6 0.0 copy-start.1
  0.6 0.0 copy-start.2
  0.7 1.2 %edge_rows.1 = (bf16[256,128]{1,0:T(8,128)(2,1)S(1)}, bf16[256,128]{1,0:T(8,128)(2,1)S(1)}) custom-call(f32[16,64,128]{2,1,0:T(8,128)} %state.5, f32[2,16,64,128]{3,2,1,0:T(8,128)} %winds.5), custom_call_target="tpu_custom_call" | custom-call | flops 1100000000 | bytes 3960000 | tf_op jit(solution)/shard_map/edge_rows/pallas_call | solution.py:372
  1.9 0.0 copy-start.7
  1.9 0.0 copy-start.4
  1.9 0.0 copy-start.5
  1.9 0.0 copy-start.6
  1.9 0.0 copy-start.8
  1.9 0.0 copy-start
  1.9 6.9 %collective-permute-start = (bf16[256,128]{1,0:T(8,128)(2,1)S(1)}, bf16[256,128]{1,0:T(8,128)(2,1)S(1)}, u32[]{:S(2)}, u32[]{:S(2)}) collective-permute-start(bf16[256,128]{1,0:T(8,128)(2,1)S(1)} %get-tuple-element.17), channel_id=1, source_target_pairs={{0,252},{4,0},{8,4},{12,8},{16,12},{20,16},{24,20},{28,24},{32,28}... | collective-permute-start | bytes 196616 | tf_op jit(solution)/shard_map/ppermute | solution.py:525
  8.8 0.0 collective-permute-start.1
  8.8 0.0 copy-done.1
  8.8 0.0 copy-done.2
  8.8 0.5 %own_strips.1.own = f32[3,64,128]{2,1,0:T(8,128)S(1)} custom-call(f32[16,64,128]{2,1,0:T(8,128)S(1)} %copy-done.2, f32[2,16,64,128]{3,2,1,0:T(8,128)S(1)} %copy-done.1), custom_call_target="tpu_custom_call" | custom-call | flops 1000000000 | bytes 3600000 | tf_op jit(solution)/shard_map/own_strips/pallas_call | solution.py:390
  9.3 0.0 copy-done.7
  9.3 0.0 copy-done.4
  9.3 0.1 broadcast_in_dim.48
  9.4 0.0 copy-done.5
  9.4 0.0 copy-done.6
  9.5 0.1 broadcast_in_dim.54
  9.5 0.1 mul.17
  9.7 0.1 add_bitcast_fusion
  9.7 0.0 copy-done.8
  9.7 0.1 pad_add_fusion.words
  9.8 0.1 iota.13
  9.9 0.0 copy-done
  9.9 0.0 copy-start.3
  9.9 0.6 %turn_blocks.1.weights = bf16[64,128,128]{2,1,0:T(8,128)(2,1)S(1)} custom-call(bf16[64,128,128]{2,1,0:T(8,128)(2,1)S(1)} %copy-done), custom_call_target="tpu_custom_call" | custom-call | flops 1000000000 | bytes 3600000 | tf_op jit(solution)/shard_map/turn_blocks/pallas_call | solution.py:458
  10.6 0.0 collective-permute-done.from_below
  10.6 4.5 %collective-permute-done.1.from_above = bf16[256,128]{1,0:T(8,128)(2,1)S(1)} collective-permute-done((bf16[256,128]{1,0:T(8,128)(2,1)S(1)}, bf16[256,128]{1,0:T(8,128)(2,1)S(1)}, u32[]{:S(2)}, u32[]{:S(2)}) %collective-permute-start.1) | collective-permute-done | bytes 65568 | tf_op jit(solution)/shard_map/ppermute | solution.py:525
  15.0 0.2 edge_columns.1
  15.2 1.3 %collective-permute-start.2 = (bf16[144,128]{1,0:T(8,128)(2,1)S(1)}, bf16[144,128]{1,0:T(8,128)(2,1)S(1)}, u32[]{:S(2)}, u32[]{:S(2)}) collective-permute-start(bf16[144,128]{1,0:T(8,128)(2,1)S(1)} %get-tuple-element.23), channel_id=1, source_target_pairs={{0,1},{1,2},{2,3},{3,0},{4,5},{5,6},{6,7},{7,4},{8,9},{9,10},{10,1... | collective-permute-start | bytes 110600 | tf_op jit(solution)/shard_map/ppermute | solution.py:525
  16.6 1.5 %collective-permute-start.3 = (bf16[144,128]{1,0:T(8,128)(2,1)S(1)}, bf16[144,128]{1,0:T(8,128)(2,1)S(1)}, u32[]{:S(2)}, u32[]{:S(2)}) collective-permute-start(bf16[144,128]{1,0:T(8,128)(2,1)S(1)} %get-tuple-element.24), channel_id=1, source_target_pairs={{0,3},{1,0},{2,1},{3,2},{4,7},{5,4},{6,5},{7,6},{8,11},{9,8},{10,9... | collective-permute-start | bytes 110600 | tf_op jit(solution)/shard_map/ppermute | solution.py:525
  18.1 0.1 broadcast_in_dim.55.rates
  18.2 0.0 copy-done.3
  18.2 0.0 copy-start.9
  18.2 1.4 %inner_steps.1 = (f32[16,64,128]{2,1,0:T(8,128)S(1)}, f32[16,64,128]{2,1,0:T(8,128)S(1)}) custom-call(f32[16,128]{1,0:T(8,128)S(1)} %broadcast_in_dim.55.rates, f32[3,8,128]{2,1,0:T(8,128)S(1)} %pad_maximum_fusion.masks, f32[16,64,128]{2,1,0:T(8,128)S(1)} %copy-done.3, f32[2,16,64,128]{3,2,1,0:T(8,128)S(1)} %copy-done.1, ...), custom_call_target="tpu_custom_call" | custom-call | flops 2500000000 | bytes 9000000 | tf_op jit(solution)/shard_map/inner_steps/pallas_call | solution.py:421
  19.5 0.0 collective-permute-done.2.from_left
  19.5 0.0 collective-permute-done.3.from_right
  19.6 0.1 broadcast_in_dim.49.weights
  19.6 1.0 %columns.1 = (f32[16,64,128]{2,1,0:T(8,128)S(1)}, f32[8,64,128]{2,1,0:T(8,128)S(1)}, bf16[512,128]{1,0:T(8,128)(2,1)S(1)}) custom-call(f32[128,128]{1,0:T(8,128)S(1)} %broadcast_in_dim.49.weights, f32[3,8,128]{2,1,0:T(8,128)S(1)} %pad_maximum_fusion.masks, f32[16,64,128]{2,1,0:T(8,128)S(1)} %get-tuple-element.20.inner_last, ...), custom_call_target="tpu_custom_call" | custom-call | tf_op jit(solution)/shard_map/columns/pallas_call | solution.py:434
  20.7 9.8 %all_gather.3.gathered = bf16[2048,128]{1,0:T(8,128)(2,1)S(1)} all-gather(bf16[512,128]{1,0:T(8,128)(2,1)S(1)} %get-tuple-element.25), channel_id=1, replica_groups=mesh['grp'=4,'gx'=16,'gy'=4] {'grp'}, dimensions={0}, use_global_device_ids=true | all-gather | bytes 655360 | tf_op jit(solution)/shard_map/all_gather | solution.py:539
  30.4 0.0 copy-done.9
  30.4 0.1 broadcast_in_dim.47.heat
  30.5 3.9 %remap.1 = (f32[16,64,128]{2,1,0:T(8,128)}, f32[8,64,128]{2,1,0:T(8,128)}, f32[64,128]{1,0:T(8,128)}) custom-call(s32[833]{0:T(1024)S(1)} %pad_add_fusion.words, f32[8,128]{1,0:T(8,128)S(1)} %broadcast_in_dim.47.heat, bf16[2048,128]{1,0:T(8,128)(2,1)S(1)} %all_gather.3.gathered, bf16[64,128,128]{2,1,0:T(8,128)(2,1)S(1)} %turn_blocks.1.weights, ...), custom_call_target="tpu_custom_call" | custom-call | tf_op jit(solution)/shard_map/remap/pallas_call | solution.py:471
  (8 shorter events, 0.0 us)
Async XLA Ops:
  0.6 8.2 %copy-start.1 = (f32[2,16,64,128]{3,2,1,0:T(8,128)S(1)}, f32[2,16,64,128]{3,2,1,0:T(8,128)}, u32[]{:S(2)}) copy-start(f32[2,16,64,128]{3,2,1,0:T(8,128)} %winds.5) | copy-start | bytes 3145732
  0.6 8.2 %copy-start.2 = (f32[16,64,128]{2,1,0:T(8,128)S(1)}, f32[16,64,128]{2,1,0:T(8,128)}, u32[]{:S(2)}) copy-start(f32[16,64,128]{2,1,0:T(8,128)} %state.5) | copy-start | bytes 1572868
  1.9 7.4 %copy-start.7 = (f32[2,16]{1,0:T(2,128)S(1)}, f32[2,16]{1,0:T(2,128)}, u32[]{:S(2)}) copy-start(f32[2,16]{1,0:T(2,128)} %param.11) | copy-start | bytes 388
  1.9 7.5 %copy-start.4 = (f32[8,16]{1,0:T(8,128)S(1)}, f32[8,16]{1,0:T(8,128)}, u32[]{:S(2)}) copy-start(f32[8,16]{1,0:T(8,128)} %param.12) | copy-start | bytes 1540
  1.9 7.5 %copy-start.5 = (s32[1,1,64,6]{2,1,3,0:T(1,128)S(1)}, s32[1,1,64,6]{2,1,3,0:T(1,128)}, u32[]{:S(2)}) copy-start(s32[1,1,64,6]{2,1,3,0:T(1,128)} %param.15) | copy-start | bytes 4612
  1.9 7.5 %copy-start.6 = (s32[1,1,64,6]{2,1,3,0:T(1,128)S(1)}, s32[1,1,64,6]{2,1,3,0:T(1,128)}, u32[]{:S(2)}) copy-start(s32[1,1,64,6]{2,1,3,0:T(1,128)} %param.16) | copy-start | bytes 4612
  1.9 7.8 %copy-start.8 = (s32[1,1,64]{2,1,0:T(1,128)S(1)}, s32[1,1,64]{2,1,0:T(1,128)}, u32[]{:S(2)}) copy-start(s32[1,1,64]{2,1,0:T(1,128)} %param.17) | copy-start | bytes 772
  1.9 8.0 %copy-start = (bf16[64,128,128]{2,1,0:T(8,128)(2,1)S(1)}, bf16[64,128,128]{2,1,0:T(8,128)(2,1)}, u32[]{:S(2)}) copy-start(bf16[64,128,128]{2,1,0:T(8,128)(2,1)} %blocks.1) | copy-start | bytes 6291460
  1.9 8.6 %collective-permute-start = (bf16[256,128]{1,0:T(8,128)(2,1)S(1)}, bf16[256,128]{1,0:T(8,128)(2,1)S(1)}, u32[]{:S(2)}, u32[]{:S(2)}) collective-permute-start(bf16[256,128]{1,0:T(8,128)(2,1)S(1)} %get-tuple-element.17), channel_id=1, source_target_pairs={{0,252},{4,0},{8,4},{12,8},{16,12},{20,16},{24,20},{28,24},{32,28}... | collective-permute-start | bytes 196616 | tf_op jit(solution)/shard_map/ppermute | solution.py:525
  8.8 6.2 %collective-permute-start.1 = (bf16[256,128]{1,0:T(8,128)(2,1)S(1)}, bf16[256,128]{1,0:T(8,128)(2,1)S(1)}, u32[]{:S(2)}, u32[]{:S(2)}) collective-permute-start(bf16[256,128]{1,0:T(8,128)(2,1)S(1)} %get-tuple-element.18), channel_id=1, source_target_pairs={{0,4},{4,8},{8,12},{12,16},{16,20},{20,24},{24,28},{28,32},{32,36}... | collective-permute-start | bytes 196616 | tf_op jit(solution)/shard_map/ppermute | solution.py:525
  9.9 8.3 %copy-start.3 = (f32[16,64,128]{2,1,0:T(8,128)S(1)}, f32[16,64,128]{2,1,0:T(8,128)}, u32[]{:S(2)}) copy-start(f32[16,64,128]{2,1,0:T(8,128)} %state.5) | copy-start | bytes 1572868
  15.2 4.3 %collective-permute-start.2 = (bf16[144,128]{1,0:T(8,128)(2,1)S(1)}, bf16[144,128]{1,0:T(8,128)(2,1)S(1)}, u32[]{:S(2)}, u32[]{:S(2)}) collective-permute-start(bf16[144,128]{1,0:T(8,128)(2,1)S(1)} %get-tuple-element.23), channel_id=1, source_target_pairs={{0,1},{1,2},{2,3},{3,0},{4,5},{5,6},{6,7},{7,4},{8,9},{9,10},{10,1... | collective-permute-start | bytes 110600 | tf_op jit(solution)/shard_map/ppermute | solution.py:525
  16.6 3.0 %collective-permute-start.3 = (bf16[144,128]{1,0:T(8,128)(2,1)S(1)}, bf16[144,128]{1,0:T(8,128)(2,1)S(1)}, u32[]{:S(2)}, u32[]{:S(2)}) collective-permute-start(bf16[144,128]{1,0:T(8,128)(2,1)S(1)} %get-tuple-element.24), channel_id=1, source_target_pairs={{0,3},{1,0},{2,1},{3,2},{4,7},{5,4},{6,5},{7,6},{8,11},{9,8},{10,9... | collective-permute-start | bytes 110600 | tf_op jit(solution)/shard_map/ppermute | solution.py:525
  18.2 12.3 %copy-start.9 = (f32[8]{0:T(128)S(1)}, f32[8]{0:T(128)}, u32[]{:S(2)}) copy-start(f32[8]{0:T(128)} %param.13) | copy-start | bytes 100

commit v9 on v8

--- a/solution.py
+++ b/solution.py
@@ -14,7 +14,7 @@
 TILES = ROWS // 8
 BASE = 16
 DEEP = ROWS + 32
-UNROLL = 16
+UNROLL = 8
 FLUX_ROWS = 32
 PARTS = ((0, 48), (48, 64))
 F32 = jnp.float32

time: 34.7 us -> 34.7 us (level)
  blocking collectives: 9.78 us -> 9.28 us
  Pallas kernels: 8.83 us -> 9.32 us
    all_gather x1, blocking collectives: 9.78 us -> 9.28 us  [body(): gathered = lax.all_gather(rounded, 'grp', axis=0, tiled=True)]
    pallas_call x1, Pallas kernels: 1.37 us -> 1.86 us  [inner_steps(): pl.pallas_call(inner_steps_kernel, in_specs=[VMEM] * 5, out_specs=[VMEM]...]
  transfers between devices with their start and end apart: 4 -> 4, of which waited for: 1 -> 1; matrix products, arithmetic and copies ran while one was open for 2% -> 2% of each run, Pallas kernels for 7% -> 9%
where the time goes in v9:
time: 34.7 us; the launch traced here: 34.4 us
  starting transfers between devices  9.73 us (28%)
  Pallas kernels  9.32 us (27%)
  blocking collectives  9.28 us (27%)
  waiting for transfers between devices  4.47 us (13%)
  between operations  0.87 us (3%)
  local copies, waits for them, and re-layouts  0.58 us (2%)
    ppermute x4, starting transfers between devices, ring(): lax.ppermute(x, axis, [(i, (i + shift) % count) for i in range(count)])  9.73 us
    all_gather x1, blocking collectives, body(): gathered = lax.all_gather(rounded, 'grp', axis=0, tiled=True)  9.28 us
    ppermute x4, waiting for transfers between devices, ring(): lax.ppermute(x, axis, [(i, (i + shift) % count) for i in range(count)])  4.47 us
    pallas_call x1, Pallas kernels, remap(): pl.pallas_call(remap_kernel, in_specs=[ANY] + [VMEM] * 5, out_specs=[ANY]...  3.93 us
    pallas_call x1, Pallas kernels, inner_steps(): pl.pallas_call(inner_steps_kernel, in_specs=[VMEM] * 5, out_specs=[VMEM]...  1.86 us
    pallas_call x1, Pallas kernels, edge_rows(): pl.pallas_call(edge_rows_kernel, in_specs=[HBM, HBM], out_specs=[VMEM, VM...  1.21 us
    pallas_call x1, Pallas kernels, columns(): pl.pallas_call(columns_kernel, in_specs=[VMEM] * 7, out_specs=[VMEM] * 3,...  1.03 us
  transfers between devices with their start and end apart: 4, of which 1 were waited for; matrix products, arithmetic and copies ran while one was open for 2% of the time, Pallas kernels for 9%

profile of v9, /device:TPU:5, one launch (start us, length us, event | category | flops | bytes accessed | tf_op | source)
XLA Modules:
  0.0 34.4 jit_solution(12670042417652382799)
XLA Ops:
  0.6 0.0 copy-start.1
  0.6 0.0 copy-start.2
  0.7 1.2 %edge_rows.1 = (bf16[256,128]{1,0:T(8,128)(2,1)S(1)}, bf16[256,128]{1,0:T(8,128)(2,1)S(1)}) custom-call(f32[16,64,128]{2,1,0:T(8,128)} %state.5, f32[2,16,64,128]{3,2,1,0:T(8,128)} %winds.5), custom_call_target="tpu_custom_call" | custom-call | flops 1100000000 | bytes 3960000 | tf_op jit(solution)/shard_map/edge_rows/pallas_call | solution.py:372
  1.9 0.0 copy-start.7
  1.9 0.0 copy-start.4
  1.9 0.0 copy-start.5
  1.9 0.0 copy-start.6
  1.9 0.0 copy-start.8
  1.9 0.0 copy-start
  1.9 6.9 %collective-permute-start = (bf16[256,128]{1,0:T(8,128)(2,1)S(1)}, bf16[256,128]{1,0:T(8,128)(2,1)S(1)}, u32[]{:S(2)}, u32[]{:S(2)}) collective-permute-start(bf16[256,128]{1,0:T(8,128)(2,1)S(1)} %get-tuple-element.17), channel_id=1, source_target_pairs={{0,252},{4,0},{8,4},{12,8},{16,12},{20,16},{24,20},{28,24},{32,28}... | collective-permute-start | bytes 196616 | tf_op jit(solution)/shard_map/ppermute | solution.py:525
  8.8 0.0 collective-permute-start.1
  8.8 0.0 copy-done.1
  8.8 0.0 copy-done.2
  8.8 0.5 %own_strips.1.own = f32[3,64,128]{2,1,0:T(8,128)S(1)} custom-call(f32[16,64,128]{2,1,0:T(8,128)S(1)} %copy-done.2, f32[2,16,64,128]{3,2,1,0:T(8,128)S(1)} %copy-done.1), custom_call_target="tpu_custom_call" | custom-call | flops 1000000000 | bytes 3600000 | tf_op jit(solution)/shard_map/own_strips/pallas_call | solution.py:390
  9.3 0.0 copy-done.7
  9.3 0.0 copy-done.4
  9.3 0.1 broadcast_in_dim.48
  9.4 0.0 copy-done.5
  9.4 0.0 copy-done.6
  9.5 0.1 broadcast_in_dim.54
  9.5 0.1 mul.17
  9.7 0.1 add_bitcast_fusion
  9.7 0.0 copy-done.8
  9.7 0.1 pad_add_fusion.words
  9.8 0.1 iota.13
  9.9 0.0 copy-done
  9.9 0.0 copy-start.3
  9.9 0.6 %turn_blocks.1.weights = bf16[64,128,128]{2,1,0:T(8,128)(2,1)S(1)} custom-call(bf16[64,128,128]{2,1,0:T(8,128)(2,1)S(1)} %copy-done), custom_call_target="tpu_custom_call" | custom-call | flops 1000000000 | bytes 3600000 | tf_op jit(solution)/shard_map/turn_blocks/pallas_call | solution.py:458
  10.6 0.0 collective-permute-done.from_below
  10.6 4.5 %collective-permute-done.1.from_above = bf16[256,128]{1,0:T(8,128)(2,1)S(1)} collective-permute-done((bf16[256,128]{1,0:T(8,128)(2,1)S(1)}, bf16[256,128]{1,0:T(8,128)(2,1)S(1)}, u32[]{:S(2)}, u32[]{:S(2)}) %collective-permute-start.1) | collective-permute-done | bytes 65568 | tf_op jit(solution)/shard_map/ppermute | solution.py:525
  15.0 0.2 edge_columns.1
  15.2 1.3 %collective-permute-start.2 = (bf16[144,128]{1,0:T(8,128)(2,1)S(1)}, bf16[144,128]{1,0:T(8,128)(2,1)S(1)}, u32[]{:S(2)}, u32[]{:S(2)}) collective-permute-start(bf16[144,128]{1,0:T(8,128)(2,1)S(1)} %get-tuple-element.23), channel_id=1, source_target_pairs={{0,1},{1,2},{2,3},{3,0},{4,5},{5,6},{6,7},{7,4},{8,9},{9,10},{10,1... | collective-permute-start | bytes 110600 | tf_op jit(solution)/shard_map/ppermute | solution.py:525
  16.6 1.5 %collective-permute-start.3 = (bf16[144,128]{1,0:T(8,128)(2,1)S(1)}, bf16[144,128]{1,0:T(8,128)(2,1)S(1)}, u32[]{:S(2)}, u32[]{:S(2)}) collective-permute-start(bf16[144,128]{1,0:T(8,128)(2,1)S(1)} %get-tuple-element.24), channel_id=1, source_target_pairs={{0,3},{1,0},{2,1},{3,2},{4,7},{5,4},{6,5},{7,6},{8,11},{9,8},{10,9... | collective-permute-start | bytes 110600 | tf_op jit(solution)/shard_map/ppermute | solution.py:525
  18.1 0.1 broadcast_in_dim.55.rates
  18.2 0.0 copy-done.3
  18.2 0.0 copy-start.9
  18.2 1.9 %inner_steps.1 = (f32[16,64,128]{2,1,0:T(8,128)S(1)}, f32[16,64,128]{2,1,0:T(8,128)S(1)}) custom-call(f32[16,128]{1,0:T(8,128)S(1)} %broadcast_in_dim.55.rates, f32[3,8,128]{2,1,0:T(8,128)S(1)} %pad_maximum_fusion.masks, f32[16,64,128]{2,1,0:T(8,128)S(1)} %copy-done.3, f32[2,16,64,128]{3,2,1,0:T(8,128)S(1)} %copy-done.1, ...), custom_call_target="tpu_custom_call" | custom-call | flops 2500000000 | bytes 9000000 | tf_op jit(solution)/shard_map/inner_steps/pallas_call | solution.py:421
  20.0 0.0 collective-permute-done.2.from_left
  20.0 0.0 collective-permute-done.3.from_right
  20.0 0.1 broadcast_in_dim.49.weights
  20.1 1.0 %columns.1 = (f32[16,64,128]{2,1,0:T(8,128)S(1)}, f32[8,64,128]{2,1,0:T(8,128)S(1)}, bf16[512,128]{1,0:T(8,128)(2,1)S(1)}) custom-call(f32[128,128]{1,0:T(8,128)S(1)} %broadcast_in_dim.49.weights, f32[3,8,128]{2,1,0:T(8,128)S(1)} %pad_maximum_fusion.masks, f32[16,64,128]{2,1,0:T(8,128)S(1)} %get-tuple-element.20.inner_last, ...), custom_call_target="tpu_custom_call" | custom-call | tf_op jit(solution)/shard_map/columns/pallas_call | solution.py:434
  21.2 9.3 %all_gather.3.gathered = bf16[2048,128]{1,0:T(8,128)(2,1)S(1)} all-gather(bf16[512,128]{1,0:T(8,128)(2,1)S(1)} %get-tuple-element.25), channel_id=1, replica_groups=mesh['grp'=4,'gx'=16,'gy'=4] {'grp'}, dimensions={0}, use_global_device_ids=true | all-gather | bytes 655360 | tf_op jit(solution)/shard_map/all_gather | solution.py:539
  30.4 0.0 copy-done.9
  30.4 0.1 broadcast_in_dim.47.heat
  30.5 3.9 %remap.1 = (f32[16,64,128]{2,1,0:T(8,128)}, f32[8,64,128]{2,1,0:T(8,128)}, f32[64,128]{1,0:T(8,128)}) custom-call(s32[833]{0:T(1024)S(1)} %pad_add_fusion.words, f32[8,128]{1,0:T(8,128)S(1)} %broadcast_in_dim.47.heat, bf16[2048,128]{1,0:T(8,128)(2,1)S(1)} %all_gather.3.gathered, bf16[64,128,128]{2,1,0:T(8,128)(2,1)S(1)} %turn_blocks.1.weights, ...), custom_call_target="tpu_custom_call" | custom-call | tf_op jit(solution)/shard_map/remap/pallas_call | solution.py:471
  (8 shorter events, 0.0 us)
Async XLA Ops:
  0.6 8.2 %copy-start.1 = (f32[2,16,64,128]{3,2,1,0:T(8,128)S(1)}, f32[2,16,64,128]{3,2,1,0:T(8,128)}, u32[]{:S(2)}) copy-start(f32[2,16,64,128]{3,2,1,0:T(8,128)} %winds.5) | copy-start | bytes 3145732
  0.6 8.2 %copy-start.2 = (f32[16,64,128]{2,1,0:T(8,128)S(1)}, f32[16,64,128]{2,1,0:T(8,128)}, u32[]{:S(2)}) copy-start(f32[16,64,128]{2,1,0:T(8,128)} %state.5) | copy-start | bytes 1572868
  1.9 7.4 %copy-start.7 = (f32[2,16]{1,0:T(2,128)S(1)}, f32[2,16]{1,0:T(2,128)}, u32[]{:S(2)}) copy-start(f32[2,16]{1,0:T(2,128)} %param.11) | copy-start | bytes 388
  1.9 7.5 %copy-start.4 = (f32[8,16]{1,0:T(8,128)S(1)}, f32[8,16]{1,0:T(8,128)}, u32[]{:S(2)}) copy-start(f32[8,16]{1,0:T(8,128)} %param.12) | copy-start | bytes 1540
  1.9 7.5 %copy-start.5 = (s32[1,1,64,6]{2,1,3,0:T(1,128)S(1)}, s32[1,1,64,6]{2,1,3,0:T(1,128)}, u32[]{:S(2)}) copy-start(s32[1,1,64,6]{2,1,3,0:T(1,128)} %param.15) | copy-start | bytes 4612
  1.9 7.5 %copy-start.6 = (s32[1,1,64,6]{2,1,3,0:T(1,128)S(1)}, s32[1,1,64,6]{2,1,3,0:T(1,128)}, u32[]{:S(2)}) copy-start(s32[1,1,64,6]{2,1,3,0:T(1,128)} %param.16) | copy-start | bytes 4612
  1.9 7.8 %copy-start.8 = (s32[1,1,64]{2,1,0:T(1,128)S(1)}, s32[1,1,64]{2,1,0:T(1,128)}, u32[]{:S(2)}) copy-start(s32[1,1,64]{2,1,0:T(1,128)} %param.17) | copy-start | bytes 772
  1.9 8.0 %copy-start = (bf16[64,128,128]{2,1,0:T(8,128)(2,1)S(1)}, bf16[64,128,128]{2,1,0:T(8,128)(2,1)}, u32[]{:S(2)}) copy-start(bf16[64,128,128]{2,1,0:T(8,128)(2,1)} %blocks.1) | copy-start | bytes 6291460
  1.9 8.6 %collective-permute-start = (bf16[256,128]{1,0:T(8,128)(2,1)S(1)}, bf16[256,128]{1,0:T(8,128)(2,1)S(1)}, u32[]{:S(2)}, u32[]{:S(2)}) collective-permute-start(bf16[256,128]{1,0:T(8,128)(2,1)S(1)} %get-tuple-element.17), channel_id=1, source_target_pairs={{0,252},{4,0},{8,4},{12,8},{16,12},{20,16},{24,20},{28,24},{32,28}... | collective-permute-start | bytes 196616 | tf_op jit(solution)/shard_map/ppermute | solution.py:525
  8.8 6.2 %collective-permute-start.1 = (bf16[256,128]{1,0:T(8,128)(2,1)S(1)}, bf16[256,128]{1,0:T(8,128)(2,1)S(1)}, u32[]{:S(2)}, u32[]{:S(2)}) collective-permute-start(bf16[256,128]{1,0:T(8,128)(2,1)S(1)} %get-tuple-element.18), channel_id=1, source_target_pairs={{0,4},{4,8},{8,12},{12,16},{16,20},{20,24},{24,28},{28,32},{32,36}... | collective-permute-start | bytes 196616 | tf_op jit(solution)/shard_map/ppermute | solution.py:525
  9.9 8.3 %copy-start.3 = (f32[16,64,128]{2,1,0:T(8,128)S(1)}, f32[16,64,128]{2,1,0:T(8,128)}, u32[]{:S(2)}) copy-start(f32[16,64,128]{2,1,0:T(8,128)} %state.5) | copy-start | bytes 1572868
  15.2 4.8 %collective-permute-start.2 = (bf16[144,128]{1,0:T(8,128)(2,1)S(1)}, bf16[144,128]{1,0:T(8,128)(2,1)S(1)}, u32[]{:S(2)}, u32[]{:S(2)}) collective-permute-start(bf16[144,128]{1,0:T(8,128)(2,1)S(1)} %get-tuple-element.23), channel_id=1, source_target_pairs={{0,1},{1,2},{2,3},{3,0},{4,5},{5,6},{6,7},{7,4},{8,9},{9,10},{10,1... | collective-permute-start | bytes 110600 | tf_op jit(solution)/shard_map/ppermute | solution.py:525
  16.6 3.5 %collective-permute-start.3 = (bf16[144,128]{1,0:T(8,128)(2,1)S(1)}, bf16[144,128]{1,0:T(8,128)(2,1)S(1)}, u32[]{:S(2)}, u32[]{:S(2)}) collective-permute-start(bf16[144,128]{1,0:T(8,128)(2,1)S(1)} %get-tuple-element.24), channel_id=1, source_target_pairs={{0,3},{1,0},{2,1},{3,2},{4,7},{5,4},{6,5},{7,6},{8,11},{9,8},{10,9... | collective-permute-start | bytes 110600 | tf_op jit(solution)/shard_map/ppermute | solution.py:525
  18.2 12.3 %copy-start.9 = (f32[8]{0:T(128)S(1)}, f32[8]{0:T(128)}, u32[]{:S(2)}) copy-start(f32[8]{0:T(128)} %param.13) | copy-start | bytes 100
